TPU v7x, 32 devices: a whole 2x2x4 slice. The times are simulated.
32 devices in a mesh: dp: 8 (over y, x, core), tensor: 4 (over z).
Axes of the slice: x: 2, y: 2, z: 4, core: 2. Of those that a mesh axis runs over, the one named last changes fastest.
Arguments:
- block_input: bfloat16 [8192, 768], P(('dp', 'tensor')), may hold values from -6 to 6
- w_qkv: bfloat16 [2, 768, 3, 768], P(None, None, None, 'tensor'), may hold values from -0.3125 to 0.3125
- qv_bias: float32 [2, 2, 768], P(None, None, 'tensor'), may hold values from -4 to 4
- w_out: bfloat16 [2, 768, 768], P(None, 'tensor'), may hold values from -0.875 to 0.875
- out_bias: float32 [2, 2, 768], replicated, may hold values from -4 to 4
- w_up: bfloat16 [2, 768, 3072], P(None, None, 'tensor'), may hold values from -0.21875 to 0.21875
- up_bias: float32 [2, 3072], P(None, 'tensor'), may hold values from -4 to 4
- w_down: bfloat16 [2, 3072, 768], P(None, 'tensor'), may hold values from -0.109375 to 0.109375
- norm_gain: float32 [2, 2, 768], replicated, may hold values from 0.1 to 1.9
- norm_shift: float32 [2, 2, 768], replicated, may hold values from -4 to 4
- segment_ids: int32 [16, 512], P('dp'), may hold values from 0 to 3, never falling along the last dimension, each value on 1 to 256 neighbouring positions
- slot_counts: int32 [16], P('dp'), may hold values from 256 to 512
- cotangent: bfloat16 [8192, 768], P(('dp', 'tensor')), may hold values from -6 to 6
Outputs:
- mixed: bfloat16 [8192, 768], P(('dp', 'tensor'))
- input_grad: float32 [8192, 768], P(('dp', 'tensor'))
- grad_qkv: float32 [2, 768, 3, 768], P(None, None, None, 'tensor')
- grad_qv_bias: float32 [2, 2, 768], P(None, None, 'tensor')
- grad_out: float32 [2, 768, 768], P(None, 'tensor')
- grad_out_bias: float32 [2, 2, 768], replicated
- grad_up: float32 [2, 768, 3072], P(None, None, 'tensor')
- grad_up_bias: float32 [2, 3072], P(None, 'tensor')
- grad_down: float32 [2, 3072, 768], P(None, 'tensor')
- grad_gain: float32 [2, 2, 768], replicated
- grad_shift: float32 [2, 2, 768], replicated
All inputs are finite; a program needn't handle non-finite values.
Results may differ from a plain program's by a relative error of at most 0.04.
The roundings to bfloat16 on the way count: a program that leaves them out, or rounds other values in their place, can miss the bound.
Values may be sent and summed in bfloat16 or wider, within the bound.
No kernel may reach another device: no remote copies, remote signals or barrier semaphores. Data moves between devices by JAX's collectives and lax.ppermute only.
A program may use at most 128 MiB of HBM per device.

v0:
```python
from functools import partial
import math

import jax
import jax.numpy as jnp
from jax import lax
from jax.sharding import PartitionSpec as P

HEAD_DIM = 64


epsilon = 1e-06
masked_fill = -1e30


def contract_rows(left, right):
    return lax.dot_general(
        left, right, (((0,), (0,)), ((), ())), preferred_element_type=jnp.float32
    )


def times_transpose(left, right):
    return lax.dot_general(
        left, right, (((1,), (1,)), ((), ())), preferred_element_type=jnp.float32
    )


def norm_forward(summed, gain, shift):
    center = summed - jnp.mean(summed, -1, keepdims=True)
    recip = lax.rsqrt(jnp.mean(center * center, -1, keepdims=True) + epsilon)
    normed = center * recip
    return (normed * gain + shift, normed, recip)


def norm_backward(grad_rows, normed, recip, gain):
    scaled = grad_rows * gain
    first_mean = jnp.mean(scaled, -1, keepdims=True)
    second_mean = jnp.mean(scaled * normed, -1, keepdims=True)
    grad_in = recip * (scaled - first_mean - normed * second_mean)
    return (grad_in, jnp.sum(grad_rows * normed, 0), jnp.sum(grad_rows, 0))


def allowed(segments, slot_count):
    places = lax.broadcasted_iota(jnp.int32, (segments.shape[0],), 0)
    filled = places < slot_count
    same = segments[:, None] == segments[None, :]
    return same & (filled[None, :] | jnp.logical_not(filled)[:, None])


def masked_scores(queries, key_rows, visible, score_scale):
    raw_scores = (
        jnp.einsum("qhd,khd->hqk", queries, key_rows, preferred_element_type=jnp.float32)
        * score_scale
    )
    return jnp.where(visible[None], raw_scores, masked_fill)


def attend(packed, score_scale):
    queries, key_rows, value_rows, segments, slot_count = packed
    visible = allowed(segments, slot_count)
    scores = masked_scores(queries, key_rows, visible, score_scale)
    row_max = jnp.max(scores, -1, keepdims=True)
    exponent = jnp.exp(scores - row_max)
    denom_sum = jnp.sum(exponent, -1, keepdims=True)
    weights_low = (exponent / denom_sum).astype(jnp.bfloat16)
    result = jnp.einsum("hqk,khd->qhd", weights_low, value_rows, preferred_element_type=jnp.float32)
    return (result.astype(jnp.bfloat16), (row_max + jnp.log(denom_sum))[..., 0])


def attend_back(packed, score_scale):
    queries, key_rows, value_rows, segments, slot_count, log_total, grad_result = packed
    visible = allowed(segments, slot_count)
    scores = masked_scores(queries, key_rows, visible, score_scale)
    weights = jnp.exp(scores - log_total[..., None])
    weights_low = weights.astype(jnp.bfloat16)
    grad_values = jnp.einsum(
        "hqk,qhd->khd", weights_low, grad_result, preferred_element_type=jnp.float32
    )
    grad_weights = jnp.einsum(
        "qhd,khd->hqk", grad_result, value_rows, preferred_element_type=jnp.float32
    )
    grad_scores = weights * (grad_weights - jnp.sum(weights * grad_weights, -1, keepdims=True))
    scores_low = grad_scores.astype(jnp.bfloat16)
    grad_queries = (
        jnp.einsum("hqk,khd->qhd", scores_low, key_rows, preferred_element_type=jnp.float32)
        * score_scale
    )
    grad_keys = (
        jnp.einsum("hqk,qhd->khd", scores_low, queries, preferred_element_type=jnp.float32)
        * score_scale
    )
    return (grad_queries, grad_keys, grad_values)


def local(
    block_input,
    w_qkv,
    qv_bias,
    w_out,
    out_bias,
    w_up,
    up_bias,
    w_down,
    norm_gain,
    norm_shift,
    segment_ids,
    slot_counts,
    cotangent,
):
    layer_count = w_qkv.shape[0]
    model_width = w_qkv.shape[1]
    local_cols = w_qkv.shape[3]
    heads_here = local_cols // HEAD_DIM
    seq_count = segment_ids.shape[0]
    seq_len = segment_ids.shape[1]
    share_rows = block_input.shape[0]
    score_scale = 1.0 / math.sqrt(HEAD_DIM)
    key_zeros = jnp.zeros((local_cols,), jnp.float32)

    def project_qkv(share, depth):
        matrix = w_qkv[depth].reshape(model_width, 3 * local_cols)
        row_bias = jnp.concatenate([qv_bias[depth, 0], key_zeros, qv_bias[depth, 1]])

        def rows_fn(row_block, begin_row):
            return (
                jnp.dot(row_block, matrix, preferred_element_type=jnp.float32) + row_bias,
                row_block,
            )

        projected, gathered = rows_fn(
            lax.all_gather(share.astype(jnp.bfloat16), "tensor", axis=0, tiled=True), jnp.int32(0)
        )
        return (projected.astype(jnp.bfloat16), gathered)

    def project_up(share, depth):

        def rows_fn(row_block, begin_row):
            return (
                jnp.dot(row_block, w_up[depth], preferred_element_type=jnp.float32)
                + up_bias[depth],
                row_block,
            )

        return rows_fn(
            lax.all_gather(share.astype(jnp.bfloat16), "tensor", axis=0, tiled=True), jnp.int32(0)
        )

    def split_heads(qkv_low):
        qkv_parts = qkv_low.reshape(seq_count, seq_len, 3, heads_here, HEAD_DIM)
        return (qkv_parts[:, :, 0], qkv_parts[:, :, 1], qkv_parts[:, :, 2])

    state = block_input.astype(jnp.float32)
    saved = []
    for depth in range(layer_count):
        qkv_low, x_gathered = project_qkv(state, depth)
        run_queries, run_key_rows, run_value_rows = split_heads(qkv_low)
        result, run_log_total = lax.map(
            partial(attend, score_scale=score_scale),
            (run_queries, run_key_rows, run_value_rows, segment_ids, slot_counts),
        )
        attended = result.reshape(seq_count * seq_len, local_cols)
        log_total = run_log_total

        def out_rows(begin_row, row_count, attended=attended, depth=depth):
            return jnp.dot(attended, w_out[depth], preferred_element_type=jnp.float32)

        branch = lax.psum_scatter(
            out_rows(jnp.int32(0), lax.axis_size("tensor") * share_rows),
            "tensor",
            scatter_dimension=0,
            tiled=True,
        )
        middle, normed_one, recip_one = norm_forward(
            state + branch + out_bias[depth, 0], norm_gain[depth, 0], norm_shift[depth, 0]
        )
        upward, h_gathered = project_up(middle, depth)
        activated = jax.nn.gelu(upward, approximate=False).astype(jnp.bfloat16)

        def down_rows(begin_row, row_count, activated=activated, depth=depth):
            return jnp.dot(activated, w_down[depth], preferred_element_type=jnp.float32)

        feed = lax.psum_scatter(
            down_rows(jnp.int32(0), lax.axis_size("tensor") * share_rows),
            "tensor",
            scatter_dimension=0,
            tiled=True,
        )
        result, normed_two, recip_two = norm_forward(
            middle + feed + out_bias[depth, 1], norm_gain[depth, 1], norm_shift[depth, 1]
        )
        stored = ()
        saved.append(
            (
                state,
                middle,
                normed_one,
                recip_one,
                normed_two,
                recip_two,
                attended,
                log_total,
                stored,
            )
        )
        state = result
    grad_rows = cotangent.astype(jnp.float32)
    collected = []
    for depth in reversed(range(layer_count)):
        (
            layer_in,
            middle,
            normed_one,
            recip_one,
            normed_two,
            recip_two,
            attended,
            log_total,
            stored,
        ) = saved[depth]
        qkv_low, x_gathered = project_qkv(layer_in, depth)
        upward, h_gathered = project_up(middle, depth)
        grad_two, gain_two, shift_two = norm_backward(
            grad_rows, normed_two, recip_two, norm_gain[depth, 1]
        )

        def down_back(row_block, begin_row, depth=depth):
            return (times_transpose(row_block, w_down[depth]), row_block)

        grad_act, grad_two_all = down_back(
            lax.all_gather(grad_two.astype(jnp.bfloat16), "tensor", axis=0, tiled=True),
            jnp.int32(0),
        )
        activated_full, gelu_pull = jax.vjp(partial(jax.nn.gelu, approximate=False), upward)
        grad_down = contract_rows(activated_full.astype(jnp.bfloat16), grad_two_all)
        grad_upward = gelu_pull(grad_act)[0].astype(jnp.bfloat16)
        grad_up_bias = jnp.sum(grad_upward, 0, dtype=jnp.float32)
        grad_up = contract_rows(h_gathered, grad_upward)

        def up_back(begin_row, row_count, grad_upward=grad_upward, depth=depth):
            return times_transpose(grad_upward, w_up[depth])

        grad_middle = grad_two + lax.psum_scatter(
            up_back(jnp.int32(0), lax.axis_size("tensor") * share_rows),
            "tensor",
            scatter_dimension=0,
            tiled=True,
        )
        grad_one, gain_one, shift_one = norm_backward(
            grad_middle, normed_one, recip_one, norm_gain[depth, 0]
        )

        def out_back(row_block, begin_row, depth=depth):
            return (times_transpose(row_block, w_out[depth]), row_block)

        grad_attn, grad_one_all = out_back(
            lax.all_gather(grad_one.astype(jnp.bfloat16), "tensor", axis=0, tiled=True),
            jnp.int32(0),
        )
        grad_out = contract_rows(attended, grad_one_all)
        queries, key_rows, value_rows = split_heads(qkv_low)
        grad_low = grad_attn.astype(jnp.bfloat16).reshape(seq_count, seq_len, heads_here, HEAD_DIM)
        head_grads = lax.map(
            partial(attend_back, score_scale=score_scale),
            (queries, key_rows, value_rows, segment_ids, slot_counts, log_total, grad_low),
        )
        stacked = jnp.stack(head_grads, axis=2).astype(jnp.bfloat16)
        grad_qkv_low = stacked.reshape(seq_count * seq_len, 3 * local_cols)
        column_sums = jnp.sum(grad_qkv_low, 0, dtype=jnp.float32).reshape(3, local_cols)
        grad_qv_bias = jnp.stack([column_sums[0], column_sums[2]])
        grad_qkv = contract_rows(x_gathered, grad_qkv_low).reshape(model_width, 3, local_cols)
        matrix = w_qkv[depth].reshape(model_width, 3 * local_cols)

        def qkv_back(begin_row, row_count, grad_qkv_low=grad_qkv_low, matrix=matrix):
            return times_transpose(grad_qkv_low, matrix)

        grad_rows = grad_one + lax.psum_scatter(
            qkv_back(jnp.int32(0), lax.axis_size("tensor") * share_rows),
            "tensor",
            scatter_dimension=0,
            tiled=True,
        )
        weight_grads = (grad_qkv, grad_qv_bias, grad_out, grad_up, grad_up_bias, grad_down)
        norm_grads = (
            jnp.stack([gain_one, gain_two]),
            jnp.stack([shift_one, shift_two]),
            jnp.stack([jnp.sum(grad_one, 0), jnp.sum(grad_two, 0)]),
        )
        collected.append((weight_grads, norm_grads))
    ordered = collected[::-1]
    stacked_weights = tuple((jnp.stack([entry[0][slot] for entry in ordered]) for slot in range(6)))
    stacked_norms = tuple((jnp.stack([entry[1][slot] for entry in ordered]) for slot in range(3)))
    stacked_weights = lax.psum(stacked_weights, "dp")
    stacked_norms = lax.psum(stacked_norms, ("dp", "tensor"))
    return (
        state.astype(jnp.bfloat16),
        grad_rows,
        stacked_weights[0],
        stacked_weights[1],
        stacked_weights[2],
        stacked_norms[2],
        stacked_weights[3],
        stacked_weights[4],
        stacked_weights[5],
        stacked_norms[0],
        stacked_norms[1],
    )


def solution(mesh):
    placed = (
        P(("dp", "tensor"), None),
        P(None, None, None, "tensor"),
        P(None, None, "tensor"),
        P(None, "tensor", None),
        P(),
        P(None, None, "tensor"),
        P(None, "tensor"),
        P(None, "tensor", None),
        P(),
        P(),
        P("dp", None),
        P("dp"),
        P(("dp", "tensor"), None),
    )
    return jax.shard_map(
        local,
        mesh=mesh,
        in_specs=placed,
        out_specs=(
            P(("dp", "tensor"), None),
            P(("dp", "tensor"), None),
            P(None, None, None, "tensor"),
            P(None, None, "tensor"),
            P(None, "tensor", None),
            P(),
            P(None, None, "tensor"),
            P(None, "tensor"),
            P(None, "tensor", None),
            P(),
            P(),
        ),
        check_vma=False,
    )
```

profile of v0, /device:TPU:0, one launch (start us, length us, event | category | flops | bytes accessed | tf_op | source)
XLA Modules:
  0.0 1166.9 jit_solution(12073232613076066359)
XLA Ops:
  10.4 39.0 %all-gather.9.cloned.1.call-done = bf16[1024,768]{1,0:T(8,128)(2,1)} async-done(((bf16[256,768]{1,0:T(8,128)(2,1)}), bf16[1024,768]{1,0:T(8,128)(2,1)}) %all-gather.9.cloned.1.call-update) | async-done | bytes 1572880 | tf_op jit(solution)/shard_map/all_gather | solution.py:131
  49.4 2.5 add_convert_fusion.3
  54.0 8.3 while.52
  63.6 2.3 fusion.161
  67.3 57.9 %reduce-scatter.9.cloned.1.call-done = f32[256,768]{1,0:T(8,128)} async-done(((f32[1024,768]{1,0:T(8,128)}), f32[256,768]{1,0:T(8,128)}) %reduce-scatter.9.cloned.1.call-update) | async-done | bytes 786448 | tf_op jit(solution)/shard_map/reduce_scatter | solution.py:167
  128.6 36.4 %all-gather.11.cloned.1.call-done = bf16[1024,768]{1,0:T(8,128)(2,1)} async-done(((bf16[256,768]{1,0:T(8,128)(2,1)}), bf16[1024,768]{1,0:T(8,128)(2,1)}) %all-gather.11.cloned.1.call-update) | async-done | bytes 1572880 | tf_op jit(solution)/shard_map/all_gather | solution.py:145
  165.0 11.5 multiply_convert_fusion.3
  177.6 3.1 fusion.131
  180.8 59.2 %reduce-scatter.11.cloned.1.call-done = f32[256,768]{1,0:T(8,128)} async-done(((f32[1024,768]{1,0:T(8,128)}), f32[256,768]{1,0:T(8,128)}) %reduce-scatter.11.cloned.1.call-update) | async-done | bytes 786448 | tf_op jit(solution)/shard_map/reduce_scatter | solution.py:182
  243.1 37.0 %all-gather.13.cloned.1.call-done = bf16[1024,768]{1,0:T(8,128)(2,1)} async-done(((bf16[256,768]{1,0:T(8,128)(2,1)}), bf16[1024,768]{1,0:T(8,128)(2,1)}) %all-gather.13.cloned.1.call-update) | async-done | bytes 1572880 | tf_op jit(solution)/shard_map/all_gather | solution.py:131
  280.0 3.5 add_convert_fusion.2
  283.6 3.3 reshape.503
  288.0 8.3 while.53
  296.7 3.4 fusion.158
  300.2 59.2 %reduce-scatter.13.cloned.1.call-done = f32[256,768]{1,0:T(8,128)} async-done(((f32[1024,768]{1,0:T(8,128)}), f32[256,768]{1,0:T(8,128)}) %reduce-scatter.13.cloned.1.call-update) | async-done | bytes 786448 | tf_op jit(solution)/shard_map/reduce_scatter | solution.py:167
  363.9 36.8 %all-gather.15.cloned.1.call-done = bf16[1024,768]{1,0:T(8,128)(2,1)} async-done(((bf16[256,768]{1,0:T(8,128)(2,1)}), bf16[1024,768]{1,0:T(8,128)(2,1)}) %all-gather.15.cloned.1.call-update) | async-done | bytes 1572880 | tf_op jit(solution)/shard_map/all_gather | solution.py:145
  400.6 11.5 multiply_convert_fusion.2
  413.3 3.1 fusion.121
  416.5 59.2 %reduce-scatter.15.cloned.1.call-done = f32[256,768]{1,0:T(8,128)} async-done(((f32[1024,768]{1,0:T(8,128)}), f32[256,768]{1,0:T(8,128)}) %reduce-scatter.15.cloned.1.call-update) | async-done | bytes 786448 | tf_op jit(solution)/shard_map/reduce_scatter | solution.py:182
  481.9 37.2 %all-gather.17.cloned.1.call-done = bf16[1024,768]{1,0:T(8,128)(2,1)} async-done(((bf16[256,768]{1,0:T(8,128)(2,1)}), bf16[1024,768]{1,0:T(8,128)(2,1)}) %all-gather.17.cloned.1.call-update) | async-done | bytes 1572880 | tf_op jit(solution)/shard_map/all_gather | solution.py:230
  519.1 6.6 convert_reduce_fusion
  526.8 3.1 fusion.125
  530.0 59.2 %reduce-scatter.17.cloned.1.call-done = f32[256,768]{1,0:T(8,128)} async-done(((f32[1024,768]{1,0:T(8,128)}), f32[256,768]{1,0:T(8,128)}) %reduce-scatter.17.cloned.1.call-update) | async-done | bytes 786448 | tf_op jit(solution)/shard_map/reduce_scatter | solution.py:242
  589.2 2.4 multiply_reduce_fusion.2
  594.5 37.0 %all-gather.19.cloned.1.call-done = bf16[1024,768]{1,0:T(8,128)(2,1)} async-done(((bf16[256,768]{1,0:T(8,128)(2,1)}), bf16[1024,768]{1,0:T(8,128)(2,1)}) %all-gather.19.cloned.1.call-update) | async-done | bytes 1572880 | tf_op jit(solution)/shard_map/all_gather | solution.py:256
  631.5 2.1 convolution_convert_fusion.1
  635.6 16.0 %while.54 = (s32[]{:T(128)}, bf16[2,512,3,64]{1,3,2,0:T(8,128)(2,1)}, bf16[2,512,3,64]{1,3,2,0:T(8,128)(2,1)}, bf16[2,512,3,64]{1,3,2,0:T(8,128)(2,1)S(1)}, bf16...) while((s32[]{:T(128)}, ...), condition=%wide.region_27.28_spmd, body=%wide.region_25.27_spmd.sunk | while | flops 511376896 | bytes 33010948 | solution.py:262
  656.1 3.1 fusion.186
  659.3 59.2 %reduce-scatter.19.cloned.1.call-done = f32[256,768]{1,0:T(8,128)} async-done(((f32[1024,768]{1,0:T(8,128)}), f32[256,768]{1,0:T(8,128)}) %reduce-scatter.19.cloned.1.call-update) | async-done | bytes 786448 | tf_op jit(solution)/shard_map/reduce_scatter | solution.py:276
  718.5 2.2 multiply_reduce_fusion.3
  722.5 37.2 %all-gather.21.cloned.1.call-done = bf16[1024,768]{1,0:T(8,128)(2,1)} async-done(((bf16[256,768]{1,0:T(8,128)(2,1)}), bf16[1024,768]{1,0:T(8,128)(2,1)}) %all-gather.21.cloned.1.call-update) | async-done | bytes 1572880 | tf_op jit(solution)/shard_map/all_gather | solution.py:230
  759.7 6.6 convert_reduce_fusion.1
  767.4 3.1 fusion.135
  770.8 59.0 %reduce-scatter.21.cloned.1.call-done = f32[256,768]{1,0:T(8,128)} async-done(((f32[1024,768]{1,0:T(8,128)}), f32[256,768]{1,0:T(8,128)}) %reduce-scatter.21.cloned.1.call-update) | async-done | bytes 786448 | tf_op jit(solution)/shard_map/reduce_scatter | solution.py:242
  829.8 2.2 multiply_reduce_fusion.4
  833.7 37.2 %all-gather.23.cloned.1.call-done = bf16[1024,768]{1,0:T(8,128)(2,1)} async-done(((bf16[256,768]{1,0:T(8,128)(2,1)}), bf16[1024,768]{1,0:T(8,128)(2,1)}) %all-gather.23.cloned.1.call-update) | async-done | bytes 1572880 | tf_op jit(solution)/shard_map/all_gather | solution.py:256
  873.5 14.3 %while.55 = (s32[]{:T(128)}, bf16[2,512,3,64]{1,3,2,0:T(8,128)(2,1)S(1)}, bf16[2,512,3,64]{1,3,2,0:T(8,128)(2,1)S(1)}, bf16[2,512,3,64]{1,3,2,0:T(8,128)(2,1)S(1...) while((s32[]{:T(128)}, ...), condition=%wide.region_36.37_spmd, body=%wide.region_34.36_spmd.sunk | while | flops 511376896 | bytes 26719380 | solution.py:262
  889.5 3.1 fusion.187
  892.9 3.5 convolution_bitcast_fusion
  902.3 2.6 pad_maximum_fusion.1
  907.1 2.5 pad_maximum_fusion
  915.7 44.5 %all-reduce = (f32[2,2,768]{2,1,0:T(2,128)}, f32[2,2,768]{2,1,0:T(2,128)}, f32[2,2,768]{2,1,0:T(2,128)}) all-reduce(f32[2,2,768]{2,1,0:T(2,128)S(1)} %pad_maximum_fusion.4, f32[2,2,768]{2,1,0:T(2,128)S(1)} %pad_maximum_fusion.5, f32[2,2,768]{2,1,0:T(2,128)S(1)} %pad_maximum_fusion.6), channel_id=1, replica_groups=mesh['dp'=8,'tensor'=4] {'dp','tensor'}, use_global_device_ids=true, to_apply=%region_47.48 | all-reduce | flops 9216 | bytes 73728 | tf_op jit(solution)/shard_map/psum | solution.py:293
  960.4 24.4 %all-reduce.1 = (f32[2,2,192]{2,1,0:T(2,128)}, f32[2,768]{1,0:T(2,128)}) all-reduce(f32[2,2,192]{2,1,0:T(2,128)S(1)} %pad_maximum_fusion.10, f32[2,768]{1,0:T(2,128)S(1)} %pad_maximum_fusion.7), channel_id=1, replica_groups=mesh['dp'=8,'tensor'=4] {'dp'}, use_global_device_ids=true, to_apply=%region_41.42 | all-reduce | flops 2304 | bytes 18432 | tf_op jit(solution)/shard_map/psum | solution.py:292
  984.8 2.1 add.309
  986.9 161.9 %all-reduce.5.cloned.1.call-done = (f32[2,768,3,192]{1,3,2,0:T(8,128)}, f32[2,192,768]{2,1,0:T(8,128)}, f32[2,768,768]{2,1,0:T(8,128)}, f32[2,768,768]{2,1,0:T(8,128)}) async-done(((f32[2,768,3,192]{1,3,2,0:T(8,128)}, f32[2,192,768]{2,1,0:T(8,128)}, f32[2,768,768]{2,1,0:T(8,128)}, f32[2,768,768]{2,1,0:T(8,128)}), (f32[2,768,3,192]{1,3,2,0:T(8,128)}, f32[2,192,768]{2,1,0:T(8,128)}, f32[2,768,768]{2,1,0:T(8,128)}, ...) | async-done | bytes 14155792 | tf_op jit(solution)/shard_map/psum | solution.py:292
  1148.8 4.4 copy.146
  1154.2 2.4 copy.148
  1157.7 2.2 copy.149
  (420 shorter events, 110.9 us)
Async XLA Ops:
  7.2 42.2 %all-gather.9.cloned.1.call-start = ((), (), s32[]{:S(2)}) async-start(), calls=%async_computation.8 | async-start | bytes 1966080 | tf_op jit(solution)/shard_map/all_gather | solution.py:131
  7.9 117.2 %reduce-scatter.9.cloned.1.call-start = ((), (), s32[]{:S(2)}) async-start(), calls=%async_computation.9 | async-start | bytes 3932160 | tf_op jit(solution)/shard_map/reduce_scatter | solution.py:167
  10.4 39.1 %copy-start.24 = (bf16[1,768,3,192]{1,3,2,0:T(8,128)(2,1)}, bf16[1,768,3,192]{1,3,2,0:T(8,128)(2,1)S(1)}, u32[]{:S(2)}) copy-start(bf16[1,768,3,192]{1,3,2,0:T(8,128)(2,1)S(1)} %get-tuple-element.428) | copy-start | bytes 2654212
  10.4 269.6 %copy-start.26 = (bf16[1,768,3,192]{1,3,2,0:T(8,128)(2,1)}, bf16[1,768,3,192]{1,3,2,0:T(8,128)(2,1)S(1)}, u32[]{:S(2)}) copy-start(bf16[1,768,3,192]{1,3,2,0:T(8,128)(2,1)S(1)} %get-tuple-element.427) | copy-start | bytes 2654212
  54.0 9.6 copy-start.28
  63.5 61.6 %copy-start.15 = (bf16[256,768]{1,0:T(8,128)(2,1)S(1)}, bf16[256,768]{1,0:T(8,128)(2,1)}, u32[]{:S(2)}) copy-start(bf16[256,768]{1,0:T(8,128)(2,1)} %param.21) | copy-start | bytes 1179652
  65.8 62.1 %copy-start.62 = (f32[2,768]{1,0:T(2,128)S(1)}, f32[2,768]{1,0:T(2,128)}, u32[]{:S(2)}) copy-start(f32[2,768]{1,0:T(2,128)} %param.27) | copy-start | bytes 18436
  65.9 99.1 %all-gather.11.cloned.1.call-start = ((), (), s32[]{:S(2)}) async-start(), calls=%async_computation.10 | async-start | bytes 1966080 | tf_op jit(solution)/shard_map/all_gather | solution.py:145
  67.3 174.5 %copy-start.40 = (f32[768]{0:T(1024)}, f32[768]{0:T(1024)S(1)}, u32[]{:S(2)}) copy-start(f32[768]{0:T(1024)S(1)} %get-tuple-element.290) | copy-start | bytes 9220
  126.5 113.5 %copy-start.33 = (f32[256]{0:T(256)}, f32[256]{0:T(256)S(1)}, u32[]{:S(2)}) copy-start(f32[256]{0:T(256)S(1)} %broadcast_multiply_fusion.11) | copy-start | bytes 3076
  126.7 113.3 %copy-start.41 = (f32[256]{0:T(256)}, f32[256]{0:T(256)S(1)}, u32[]{:S(2)}) copy-start(f32[256]{0:T(256)S(1)} %add_rsqrt_fusion.3) | copy-start | bytes 3076
  127.7 112.3 %reduce-scatter.11.cloned.1.call-start = ((), (), s32[]{:S(2)}) async-start(), calls=%async_computation.11 | async-start | bytes 3932160 | tf_op jit(solution)/shard_map/reduce_scatter | solution.py:182
  128.6 47.9 %copy-start.63 = (f32[768]{0:T(1024)}, f32[768]{0:T(1024)S(1)}, u32[]{:S(2)}) copy-start(f32[768]{0:T(1024)S(1)} %get-tuple-element.298) | copy-start | bytes 9220
  165.0 12.7 %copy-start.67 = (bf16[2,768,768]{2,1,0:T(8,128)(2,1)S(1)}, bf16[2,768,768]{2,1,0:T(8,128)(2,1)}, u32[]{:S(2)}) copy-start(bf16[2,768,768]{2,1,0:T(8,128)(2,1)} %param.28) | copy-start | bytes 7077892
  180.7 99.3 %all-gather.13.cloned.1.call-start = ((), (), s32[]{:S(2)}) async-start(), calls=%async_computation.12 | async-start | bytes 1966080 | tf_op jit(solution)/shard_map/all_gather | solution.py:131
  241.5 42.0 %copy-start.35 = (f32[256]{0:T(256)}, f32[256]{0:T(256)S(1)}, u32[]{:S(2)}) copy-start(f32[256]{0:T(256)S(1)} %broadcast_multiply_fusion.10) | copy-start | bytes 3076
  241.8 41.8 %copy-start.43 = (f32[256]{0:T(256)}, f32[256]{0:T(256)S(1)}, u32[]{:S(2)}) copy-start(f32[256]{0:T(256)S(1)} %add_rsqrt_fusion.2) | copy-start | bytes 3076
  242.7 116.7 %reduce-scatter.13.cloned.1.call-start = ((), (), s32[]{:S(2)}) async-start(), calls=%async_computation.13 | async-start | bytes 3932160 | tf_op jit(solution)/shard_map/reduce_scatter | solution.py:167
  300.2 100.5 %all-gather.15.cloned.1.call-start = ((), (), s32[]{:S(2)}) async-start(), calls=%async_computation.14 | async-start | bytes 1966080 | tf_op jit(solution)/shard_map/all_gather | solution.py:145
  363.4 112.3 %reduce-scatter.15.cloned.1.call-start = ((), (), s32[]{:S(2)}) async-start(), calls=%async_computation.15 | async-start | bytes 3932160 | tf_op jit(solution)/shard_map/reduce_scatter | solution.py:182
  400.6 12.7 %copy-start.68 = (bf16[2,768,768]{2,1,0:T(8,128)(2,1)S(1)}, bf16[2,768,768]{2,1,0:T(8,128)(2,1)}, u32[]{:S(2)}) copy-start(bf16[2,768,768]{2,1,0:T(8,128)(2,1)} %param.28) | copy-start | bytes 7077892
  416.4 102.7 %all-gather.17.cloned.1.call-start = ((), (), s32[]{:S(2)}) async-start(), calls=%async_computation.16 | async-start | bytes 1966080 | tf_op jit(solution)/shard_map/all_gather | solution.py:230
  481.8 107.4 %reduce-scatter.17.cloned.1.call-start = ((), (), s32[]{:S(2)}) async-start(), calls=%async_computation.17 | async-start | bytes 3932160 | tf_op jit(solution)/shard_map/reduce_scatter | solution.py:242
  519.1 7.7 copy-start.69
  529.9 101.6 %all-gather.19.cloned.1.call-start = ((), (), s32[]{:S(2)}) async-start(), calls=%async_computation.18 | async-start | bytes 1966080 | tf_op jit(solution)/shard_map/all_gather | solution.py:256
  593.5 42.1 %copy-start.78 = (s32[2]{0:T(128)S(1)}, s32[2]{0:T(128)}, u32[]{:S(2)}) copy-start(s32[2]{0:T(128)} %copy-done.77) | copy-start | bytes 28
  594.3 124.3 %reduce-scatter.19.cloned.1.call-start = ((), (), s32[]{:S(2)}) async-start(), calls=%async_computation.19 | async-start | bytes 3932160 | tf_op jit(solution)/shard_map/reduce_scatter | solution.py:276
  651.6 4.5 copy-start.27
  659.2 59.3 %copy-start.5 = (f32[256,768]{1,0:T(8,128)S(1)}, f32[256,768]{1,0:T(8,128)}, u32[]{:S(2)}) copy-start(f32[256,768]{1,0:T(8,128)} %copy-done.4) | copy-start | bytes 2359300
  659.2 59.3 %copy-start.36 = (f32[256]{0:T(256)S(1)}, f32[256]{0:T(256)}, u32[]{:S(2)}) copy-start(f32[256]{0:T(256)} %copy-done.35) | copy-start | bytes 3076
  659.2 59.3 %copy-start.44 = (f32[256]{0:T(256)S(1)}, f32[256]{0:T(256)}, u32[]{:S(2)}) copy-start(f32[256]{0:T(256)} %copy-done.43) | copy-start | bytes 3076
  659.3 100.4 %copy-start.64 = (f32[768]{0:T(1024)S(1)}, f32[768]{0:T(1024)}, u32[]{:S(2)}) copy-start(f32[768]{0:T(1024)} %copy-done.63) | copy-start | bytes 9220
  659.3 100.4 %all-gather.21.cloned.1.call-start = ((), (), s32[]{:S(2)}) async-start(), calls=%async_computation.20 | async-start | bytes 1966080 | tf_op jit(solution)/shard_map/all_gather | solution.py:230
  722.4 107.3 %reduce-scatter.21.cloned.1.call-start = ((), (), s32[]{:S(2)}) async-start(), calls=%async_computation.21 | async-start | bytes 3932160 | tf_op jit(solution)/shard_map/reduce_scatter | solution.py:242
  759.7 7.7 copy-start.70
  770.5 59.3 %copy-start.34 = (f32[256]{0:T(256)S(1)}, f32[256]{0:T(256)}, u32[]{:S(2)}) copy-start(f32[256]{0:T(256)} %copy-done.33) | copy-start | bytes 3076
  770.5 59.3 %copy-start.42 = (f32[256]{0:T(256)S(1)}, f32[256]{0:T(256)}, u32[]{:S(2)}) copy-start(f32[256]{0:T(256)} %copy-done.41) | copy-start | bytes 3076
  770.5 100.4 %copy-start.29 = (bf16[2,192,768]{2,1,0:T(8,128)(2,1)S(1)}, bf16[2,192,768]{2,1,0:T(8,128)(2,1)}, u32[]{:S(2)}) copy-start(bf16[2,192,768]{2,1,0:T(8,128)(2,1)} %param.24) | copy-start | bytes 1769476
  770.5 100.4 %all-gather.23.cloned.1.call-start = ((), (), s32[]{:S(2)}) async-start(), calls=%async_computation.22 | async-start | bytes 1966080 | tf_op jit(solution)/shard_map/all_gather | solution.py:256
  832.8 40.6 %copy-start.1 = (bf16[2,512,3,64]{1,3,2,0:T(8,128)(2,1)S(1)}, bf16[2,512,3,64]{1,3,2,0:T(8,128)(2,1)}, u32[]{:S(2)}) copy-start(bf16[2,512,3,64]{1,3,2,0:T(8,128)(2,1)} %copy-done) | copy-start | bytes 1179652
  832.8 40.6 %copy-start.3 = (bf16[2,512,3,64]{1,3,2,0:T(8,128)(2,1)S(1)}, bf16[2,512,3,64]{1,3,2,0:T(8,128)(2,1)}, u32[]{:S(2)}) copy-start(bf16[2,512,3,64]{1,3,2,0:T(8,128)(2,1)} %copy-done.2) | copy-start | bytes 1179652
  832.8 40.6 %copy-start.8 = (bf16[2,512,3,64]{1,3,2,0:T(8,128)(2,1)S(1)}, bf16[2,512,3,64]{1,3,2,0:T(8,128)(2,1)}, u32[]{:S(2)}) copy-start(bf16[2,512,3,64]{1,3,2,0:T(8,128)(2,1)} %copy-done.7) | copy-start | bytes 1179652
  833.6 151.1 %reduce-scatter.23.cloned.1.call-start = ((), (), s32[]{:S(2)}) async-start(), calls=%async_computation.23 | async-start | bytes 3932160 | tf_op jit(solution)/shard_map/reduce_scatter | solution.py:276
  892.6 256.2 %all-reduce.5.cloned.1.call-start = ((), (), s32[]{:S(2)}) async-start(), calls=%async_computation.24 | async-start | bytes 28311552 | tf_op jit(solution)/shard_map/psum | solution.py:292
  1148.8 5.4 slice-start.2
  1148.8 4.4 copy-start.23
  1148.8 5.4 slice-start.3
  1153.2 4.2 slice-start
  (63 other events, 113.7 us)
Sparse Core Ops, SparseCore 0:
  9.6 39.7 all-gather.8
  66.0 59.1 reduce-scatter.8
  127.8 37.0 all-gather.10
  180.9 59.1 reduce-scatter.10
  242.9 37.0 all-gather.12
  300.3 59.0 reduce-scatter.12
  363.5 37.1 all-gather.14
  416.6 59.0 reduce-scatter.14
  482.0 37.1 all-gather.16
  530.1 59.1 reduce-scatter.16
  594.4 37.0 all-gather.18
  659.4 59.0 reduce-scatter.18
  722.5 37.1 all-gather.20
  770.6 59.0 reduce-scatter.20
  833.7 37.1 all-gather.22
  892.7 60.1 reduce-scatter.22
  957.9 190.8 all-reduce.4
where the time goes:
time: 1170 us
  waiting for transfers between devices  874 us (75%)
  matrix products  102 us (9%)
  blocking collectives  68.9 us (6%)
  other arithmetic  51.9 us (4%)
  local copies, waits for them, and re-layouts  51.7 us (4%)
  between operations  15.7 us (1%)
    psum x1, waiting for transfers between devices, local(): stacked_weights = lax.psum(stacked_weights, 'dp')  162 us
    reduce_scatter x2, waiting for transfers between devices, local(): lax.psum_scatter(down_rows(jnp.int32(0), lax.axis_size('tensor') * share_...  118 us
    reduce_scatter x2, waiting for transfers between devices, local(): lax.psum_scatter(up_back(jnp.int32(0), lax.axis_size('tensor') * share_ro...  118 us
    reduce_scatter x2, waiting for transfers between devices, local(): lax.psum_scatter(out_rows(jnp.int32(0), lax.axis_size('tensor') * share_r...  117 us
    all_gather x2, waiting for transfers between devices, project_qkv(): lax.all_gather(share.astype(jnp.bfloat16), 'tensor', axis=0, tiled=True)  76 us
    all_gather x2, waiting for transfers between devices, local(): lax.all_gather(grad_two.astype(jnp.bfloat16), 'tensor', axis=0, tiled=True)  74.5 us
    all_gather x2, waiting for transfers between devices, local(): lax.all_gather(grad_one.astype(jnp.bfloat16), 'tensor', axis=0, tiled=True)  74.3 us
    all_gather x2, waiting for transfers between devices, project_up(): lax.all_gather(share.astype(jnp.bfloat16), 'tensor', axis=0, tiled=True)  73.1 us
  transfers between devices with their start and end apart: 17, of which 16 were waited for; matrix products, arithmetic and copies ran while one was open for 2% of the time, Pallas kernels for 0%

commit v1 on v0

v1 whole, which is shorter than its diff:
```python
from functools import partial
import math

import jax
import jax.numpy as jnp
from jax import lax
from jax.sharding import PartitionSpec as P

HEAD_DIM = 64
epsilon = 1e-06
masked_fill = -1e30
bf16 = jnp.bfloat16
f32 = jnp.float32


def dot_nn(left, right):
    return lax.dot_general(left, right, (((1,), (0,)), ((), ())), preferred_element_type=f32)


def dot_nt(left, right):
    return lax.dot_general(left, right, (((1,), (1,)), ((), ())), preferred_element_type=f32)


def dot_tn(left, right):
    return lax.dot_general(left, right, (((0,), (0,)), ((), ())), preferred_element_type=f32)


def norm_forward(summed, gain, shift):
    center = summed - jnp.mean(summed, -1, keepdims=True)
    recip = lax.rsqrt(jnp.mean(center * center, -1, keepdims=True) + epsilon)
    normed = center * recip
    return normed * gain + shift, normed, recip


def norm_backward(grad_rows, normed, recip, gain):
    scaled = grad_rows * gain
    first_mean = jnp.mean(scaled, -1, keepdims=True)
    second_mean = jnp.mean(scaled * normed, -1, keepdims=True)
    grad_in = recip * (scaled - first_mean - normed * second_mean)
    return grad_in, jnp.sum(grad_rows * normed, 0), jnp.sum(grad_rows, 0)


def allowed(segments, slot_count):
    places = lax.broadcasted_iota(jnp.int32, (segments.shape[0],), 0)
    filled = places < slot_count
    same = segments[:, None] == segments[None, :]
    return same & (filled[None, :] | jnp.logical_not(filled)[:, None])


def attend(queries, key_rows, value_rows, visible, scale):
    scores = jnp.einsum("qhd,khd->hqk", queries, key_rows, preferred_element_type=f32) * scale
    scores = jnp.where(visible[None], scores, masked_fill)
    row_max = jnp.max(scores, -1, keepdims=True)
    exponent = jnp.exp(scores - row_max)
    denom = jnp.sum(exponent, -1, keepdims=True)
    weights = (exponent / denom).astype(bf16)
    result = jnp.einsum("hqk,khd->qhd", weights, value_rows, preferred_element_type=f32)
    return result.astype(bf16), row_max + jnp.log(denom)


def attend_back(queries, key_rows, value_rows, visible, log_total, grad_result, scale):
    scores = jnp.einsum("qhd,khd->hqk", queries, key_rows, preferred_element_type=f32) * scale
    scores = jnp.where(visible[None], scores, masked_fill)
    weights = jnp.exp(scores - log_total)
    weights_low = weights.astype(bf16)
    grad_values = jnp.einsum("hqk,qhd->khd", weights_low, grad_result, preferred_element_type=f32)
    grad_weights = jnp.einsum("qhd,khd->hqk", grad_result, value_rows, preferred_element_type=f32)
    grad_scores = weights * (grad_weights - jnp.sum(weights * grad_weights, -1, keepdims=True))
    low = grad_scores.astype(bf16)
    grad_queries = jnp.einsum("hqk,khd->qhd", low, key_rows, preferred_element_type=f32) * scale
    grad_keys = jnp.einsum("hqk,qhd->khd", low, queries, preferred_element_type=f32) * scale
    return grad_queries, grad_keys, grad_values


def local(
    block_input,
    w_qkv,
    qv_bias,
    w_out,
    out_bias,
    w_up,
    up_bias,
    w_down,
    norm_gain,
    norm_shift,
    segment_ids,
    slot_counts,
    cotangent,
):
    layers, width, _, cols = w_qkv.shape
    hidden = w_up.shape[2]
    seq_len = segment_ids.shape[1]
    n_dp, n_t = lax.axis_size("dp"), lax.axis_size("tensor")
    dp, z = lax.axis_index("dp"), lax.axis_index("tensor")
    core, place = dp & 1, (dp >> 1) & 3
    first = core == 0
    scale = 1.0 / math.sqrt(HEAD_DIM)
    half = cols // 2
    heads = n_t // 2 * cols // HEAD_DIM
    part = hidden // 8

    def flip(v, bit):
        return lax.ppermute(v, "dp", [(i, i ^ (1 << bit)) for i in range(n_dp)])

    def across(v):
        return flip(v, 0)

    def rotate(v, by):
        return lax.ppermute(v, "tensor", [(i, (i + by) % n_t) for i in range(n_t)])

    def swap(v):
        pairs = []
        for i in range(n_dp):
            for k in range(n_t):
                if (i & 1) != (k & 1):
                    pairs.append((i * n_t + k, (i ^ 1) * n_t + (k ^ 1)))
        moved = lax.ppermute(v, ("dp", "tensor"), pairs)
        return jnp.where(core == (z & 1), v, moved)

    def in_core_order(mine, theirs, axis):
        return jnp.where(
            first,
            jnp.concatenate([mine, theirs], axis),
            jnp.concatenate([theirs, mine], axis),
        )

    def add_low(a, b):
        return (a.astype(f32) + b.astype(f32)).astype(bf16)

    def whole_rows(v):
        own = swap(v)
        return in_core_order(own, across(own), 0)

    x_low = whole_rows(block_input)
    seg_theirs, count_theirs = across(segment_ids), across(slot_counts)
    seg_sel = jnp.where(core == (z & 1), segment_ids, seg_theirs)
    count_sel = jnp.where(core == (z & 1), slot_counts, count_theirs)
    segments = lax.dynamic_index_in_dim(seg_sel, z >> 1, 0, False)
    slot_count = lax.dynamic_index_in_dim(count_sel, z >> 1, 0, False)
    visible = allowed(segments, slot_count)

    def gather_pieces(piece, split):
        rel = jnp.stack([rotate(piece, k) for k in range(1, n_t)])
        a, b = rel[:, :split], rel[:, split:]
        xa = flip(a, 1)
        yb = flip(b, 2)
        ya = flip(jnp.stack([a, xa]), 2)
        xb = flip(jnp.stack([b, yb]), 1)
        return (
            jnp.stack([a, xa, ya[0], ya[1]], 1),
            jnp.stack([b, xb[0], yb, xb[1]], 1),
        )

    attn_w, up_w, down_w = [], [], []
    for l in range(layers):
        own_attn = jnp.concatenate(
            [jnp.transpose(w_qkv[l], (1, 2, 0)), w_out[l][None]], 0
        )
        piece = lax.dynamic_index_in_dim(own_attn, place, 0, False)
        piece = lax.dynamic_slice_in_dim(piece, core * half, half, 0)
        a, b = gather_pieces(piece, half // 2)
        got = jnp.concatenate([a, b], 2)
        got = in_core_order(got, across(got), 2)
        order = jnp.arange(4) ^ place
        got = jnp.take(got, order, axis=1)
        attn_w.append(jnp.concatenate([own_attn[None], got], 0))

        order_ff = (jnp.arange(4) ^ place) * 2 + core
        own_up = w_up[l].T.reshape(8, part, width)
        own_down = w_down[l].reshape(8, part, width)
        own_up = jnp.take(own_up, order_ff, axis=0)
        own_down = jnp.take(own_down, order_ff, axis=0)
        a, b = gather_pieces(jnp.concatenate([own_up[0], own_down[0]], 0), part)
        up_w.append(jnp.concatenate([own_up[None], a], 0).reshape(-1, width))
        down_w.append(jnp.concatenate([own_down[None], b], 0).reshape(-1, width))

    small = jnp.concatenate([up_bias.reshape(-1), qv_bias.reshape(-1)])
    small = lax.all_gather(small, "tensor", axis=0)
    rel_quarter = (z - jnp.arange(n_t)) % n_t
    small = jnp.take(small, rel_quarter, axis=0)
    up_bias_all = small[:, : layers * hidden].reshape(n_t, layers, 8, part)
    up_bias_all = jnp.take(up_bias_all, (jnp.arange(4) ^ place) * 2 + core, axis=2)
    up_bias_all = jnp.transpose(up_bias_all, (1, 0, 2, 3)).reshape(layers, -1)
    qv_all = small[:, layers * hidden :].reshape(n_t, layers, 2, cols)
    qv_mine = lax.dynamic_slice_in_dim(qv_all, core * (n_t // 2), n_t // 2, 0)
    qv_mine = jnp.transpose(qv_mine, (1, 2, 0, 3)).reshape(layers, 2, -1)

    def my_heads(w):
        return lax.dynamic_slice_in_dim(w, core * (n_t // 2), n_t // 2, 0)

    def their_heads(w):
        return lax.dynamic_slice_in_dim(w, (1 - core) * (n_t // 2), n_t // 2, 0)

    state = x_low.astype(f32)
    saved = []
    for l in range(layers):
        mine = my_heads(attn_w[l])
        w3 = jnp.transpose(mine[:, :3], (1, 0, 2, 3)).reshape(-1, width)
        w_o = mine[:, 3].reshape(-1, width)
        w_o_theirs = their_heads(attn_w[l])[:, 3].reshape(-1, width)
        xr = state.astype(bf16)
        bias = jnp.concatenate([qv_mine[l, 0], jnp.zeros_like(qv_mine[l, 0]), qv_mine[l, 1]])
        qkv = (dot_nt(xr, w3) + bias).astype(bf16).reshape(seq_len, 3, heads, HEAD_DIM)
        o, lse = attend(qkv[:, 0], qkv[:, 1], qkv[:, 2], visible, scale)
        o = o.reshape(seq_len, -1)
        o_theirs = across(o)
        branch = dot_nn(o, w_o) + dot_nn(o_theirs, w_o_theirs)
        h, n1, r1 = norm_forward(state + branch + out_bias[l, 0], norm_gain[l, 0], norm_shift[l, 0])
        hr = h.astype(bf16)
        u = dot_nt(hr, up_w[l]) + up_bias_all[l]
        g = jax.nn.gelu(u, approximate=False).astype(bf16)
        f_part = dot_nn(g, down_w[l])
        f = f_part + across(f_part.astype(bf16)).astype(f32)
        new, n2, r2 = norm_forward(h + f + out_bias[l, 1], norm_gain[l, 1], norm_shift[l, 1])
        saved.append((xr, w3, w_o, qkv, o, lse, n1, r1, hr, u, g, n2, r2))
        state = new
    out_rows = lax.dynamic_slice_in_dim(state.astype(bf16), core * (seq_len // 2), seq_len // 2, 0)
    mixed = swap(out_rows)

    def reduce_pieces(a, b):
        ra = flip(a[:, 2:], 2)
        rb = flip(b[:, 1::2], 1)
        a = add_low(a[:, :2], ra)
        b = add_low(b[:, 0::2], rb)
        a1 = flip(a[:, 1], 1)
        b1 = flip(b[:, 1], 2)
        both = jnp.concatenate([add_low(a[:, 0], a1), add_low(b[:, 0], b1)], 1)
        total = both[0].astype(f32)
        for k in range(1, n_t):
            total = total + rotate(both[k], n_t - k).astype(f32)
        total = total.astype(bf16)
        bit = 3
        while (1 << bit) < n_dp:
            total = add_low(total, flip(total, bit))
            bit += 1
        rows = a.shape[2]
        a, b = total[:rows], total[rows:]
        xa = flip(a, 1)
        yb = flip(b, 2)
        ya = flip(jnp.stack([a, xa]), 2)
        xb = flip(jnp.stack([b, yb]), 1)
        return jnp.stack([a, xa, ya[0], ya[1]]), jnp.stack([b, xb[0], yb, xb[1]])

    order = jnp.arange(4) ^ place
    grads = []
    dy = whole_rows(cotangent).astype(f32)
    for l in reversed(range(layers)):
        xr, w3, w_o, qkv, o, lse, n1, r1, hr, u, g, n2, r2 = saved[l]
        dz2, gain2, shift2 = norm_backward(dy, n2, r2, norm_gain[l, 1])
        dzr2 = dz2.astype(bf16)
        dg = dot_nt(dzr2, down_w[l])
        _, pull = jax.vjp(partial(jax.nn.gelu, approximate=False), u)
        du = pull(dg)[0].astype(bf16)
        dh_part = dot_nn(du, up_w[l])
        dh = dz2 + dh_part + across(dh_part.astype(bf16)).astype(f32)
        g_down = dot_tn(g, dzr2).astype(bf16).reshape(n_t, 4, part, width)
        g_up = dot_tn(du, hr).astype(bf16).reshape(n_t, 4, part, width)
        g_up_bias = jnp.sum(du, 0, dtype=f32).reshape(n_t, 4, part)
        g_up, g_down = reduce_pieces(g_up, g_down)
        ff = jnp.stack([g_up, g_down])
        ff = in_core_order(ff[:, :, None], across(ff)[:, :, None], 2)
        ff = jnp.take(ff, order, axis=1).reshape(2, hidden, width).astype(f32)

        dz1, gain1, shift1 = norm_backward(dh, n1, r1, norm_gain[l, 0])
        dzr1 = dz1.astype(bf16)
        do = dot_nt(dzr1, w_o).astype(bf16).reshape(seq_len, heads, HEAD_DIM)
        d3 = attend_back(qkv[:, 0], qkv[:, 1], qkv[:, 2], visible, lse, do, scale)
        d3 = jnp.stack(d3, 1).astype(bf16).reshape(seq_len, -1)
        dx_part = dot_nn(d3, w3)
        dy = dz1 + dx_part + across(dx_part.astype(bf16)).astype(f32)
        g3 = dot_tn(d3, xr).astype(bf16).reshape(3, n_t // 2, 2, half, width)
        g_o = dot_tn(o, dzr1).astype(bf16).reshape(1, n_t // 2, 2, half, width)
        g_attn = jnp.transpose(jnp.concatenate([g3, g_o], 0), (2, 1, 0, 3, 4))
        keep = lax.dynamic_index_in_dim(g_attn, core, 0, False)
        give = lax.dynamic_index_in_dim(g_attn, 1 - core, 0, False)
        both = in_core_order(keep, across(give), 0)
        both = jnp.take(both, order, axis=1)
        a, b = reduce_pieces(both[:, :, : half // 2], both[:, :, half // 2 :])
        at = jnp.concatenate([a, b], 1)
        at = in_core_order(at, across(at), 1)
        at = jnp.take(at, order, axis=0).astype(f32)

        col = jnp.sum(d3, 0, dtype=f32).reshape(3, n_t // 2, cols)
        g_qv = jnp.stack([col[0], col[2]])
        grads.append((ff, at, g_up_bias, g_qv, gain1, gain2, shift1, shift2, jnp.sum(dz1, 0), jnp.sum(dz2, 0)))

    grads = grads[::-1]
    out_half = lax.dynamic_slice_in_dim(dy, core * (seq_len // 2), seq_len // 2, 0)
    input_grad = swap(out_half)

    once = jnp.where(first, 1.0, 0.0).astype(f32)
    norm_rows = jnp.stack([jnp.stack(g[4:]) for g in grads]) * once
    abs_quarter = (z - jnp.arange(n_t)) % n_t
    ub = jnp.stack([g[2] for g in grads])
    ub = jnp.take(jnp.take(ub, abs_quarter, axis=1), order, axis=2)
    zero = jnp.zeros_like(ub)
    ub = in_core_order(jnp.where(first, ub, ub)[:, :, :, None], zero[:, :, :, None], 3)
    qv = jnp.stack([g[3] for g in grads])
    qv = in_core_order(qv, jnp.zeros_like(qv), 2)
    qv = jnp.take(qv, abs_quarter, axis=2)
    flat = jnp.concatenate([norm_rows.reshape(-1), ub.reshape(-1), qv.reshape(-1)])
    flat = flat.reshape(-1, 128)
    bit = 0
    while (1 << bit) < n_dp:
        flat = flat + flip(flat, bit)
        bit += 1
    bit = 0
    while (1 << bit) < n_t:
        flat = flat + lax.ppermute(flat, "tensor", [(i, i ^ (1 << bit)) for i in range(n_t)])
        bit += 1
    flat = flat.reshape(-1)
    n0 = norm_rows.size
    norm_rows = flat[:n0].reshape(layers, 6, width)
    ub = flat[n0 : n0 + ub.size].reshape(layers, n_t, hidden)
    qv = flat[n0 + ub.size :].reshape(layers, 2, n_t, cols)
    grad_up_bias = lax.dynamic_index_in_dim(ub, z, 1, False)
    grad_qv_bias = lax.dynamic_index_in_dim(qv, z, 2, False)
    return (
        mixed,
        input_grad,
        jnp.stack([jnp.transpose(g[1][:3], (2, 0, 1)) for g in grads]),
        grad_qv_bias,
        jnp.stack([g[1][3] for g in grads]),
        norm_rows[:, 4:6],
        jnp.stack([g[0][0].T for g in grads]),
        grad_up_bias,
        jnp.stack([g[0][1] for g in grads]),
        norm_rows[:, 0:2],
        norm_rows[:, 2:4],
    )


def solution(mesh):
    placed = (
        P(("dp", "tensor"), None),
        P(None, None, None, "tensor"),
        P(None, None, "tensor"),
        P(None, "tensor", None),
        P(),
        P(None, None, "tensor"),
        P(None, "tensor"),
        P(None, "tensor", None),
        P(),
        P(),
        P("dp", None),
        P("dp"),
        P(("dp", "tensor"), None),
    )
    return jax.shard_map(
        local,
        mesh=mesh,
        in_specs=placed,
        out_specs=(
            P(("dp", "tensor"), None),
            P(("dp", "tensor"), None),
            P(None, None, None, "tensor"),
            P(None, None, "tensor"),
            P(None, "tensor", None),
            P(),
            P(None, None, "tensor"),
            P(None, "tensor"),
            P(None, "tensor", None),
            P(),
            P(),
        ),
        check_vma=False,
    )
```

time: 1170 us -> 667 us (0.57)
  waiting for transfers between devices: 874 us -> 178 us
  starting transfers between devices: 2.27 us -> 144 us
  other arithmetic: 51.9 us -> 118 us
  local copies, waits for them, and re-layouts: 51.7 us -> 108 us
  blocking collectives: 68.9 us -> 21.7 us
  matrix products: 102 us -> 86 us
    reduce_scatter x8 -> x0, waiting for transfers between devices: 413 us -> none  [the longest x2 118 us: local(): lax.psum_scatter(down_rows(jnp.int32(0), lax.axis_size('tensor') * share_...]
    all_gather x8 -> x0, waiting for transfers between devices: 298 us -> none  [the longest x2 76 us: project_qkv(): lax.all_gather(share.astype(jnp.bfloat16), 'tensor', axis=0, tiled=True)]
    ppermute x0 -> x101, waiting for transfers between devices: none -> 178 us  [the longest x71 100 us: flip(): return lax.ppermute(v, 'dp', [(i, i ^ 1 << bit) for i in range(n_dp)])]
    psum x1 -> x0, waiting for transfers between devices: 162 us -> none  [local(): stacked_weights = lax.psum(stacked_weights, 'dp')]
    ppermute x0 -> x101, starting transfers between devices: none -> 144 us  [the longest x71 69.7 us: flip(): return lax.ppermute(v, 'dp', [(i, i ^ 1 << bit) for i in range(n_dp)])]
    psum x2 -> x0, blocking collectives: 68.9 us -> none  [the longest x1 44.5 us: local(): stacked_norms = lax.psum(stacked_norms, ('dp', 'tensor'))]
    select_n x0 -> x28, other arithmetic: none -> 31.4 us  [the longest x10 16.8 us: in_core_order(): jnp.where(first, jnp.concatenate([mine, theirs], axis), jnp.concatenate([...]
    gather x0 -> x17, local copies, waits for them, and re-layouts: none -> 25.8 us  [the longest x2 5.99 us: local(): both = jnp.take(both, order, axis=1)]
  transfers between devices with their start and end apart: 17 -> 101, of which waited for: 16 -> 40; matrix products, arithmetic and copies ran while one was open for 2% -> 42% of each run, Pallas kernels for 0% -> 0%
where the time goes in v1:
time: 667 us; the launch traced here: 659 us
  waiting for transfers between devices  178 us (27%)
  starting transfers between devices  144 us (22%)
  other arithmetic  118 us (18%)
  local copies, waits for them, and re-layouts  108 us (16%)
  matrix products  86 us (13%)
  blocking collectives  21.7 us (3%)
    ppermute x71, waiting for transfers between devices, flip(): return lax.ppermute(v, 'dp', [(i, i ^ 1 << bit) for i in range(n_dp)])  100 us
    ppermute x24, waiting for transfers between devices, rotate(): return lax.ppermute(v, 'tensor', [(i, (i + by) % n_t) for i in range(n_t)])  71.6 us
    ppermute x71, starting transfers between devices, flip(): return lax.ppermute(v, 'dp', [(i, i ^ 1 << bit) for i in range(n_dp)])  69.7 us
    ppermute x24, starting transfers between devices, rotate(): return lax.ppermute(v, 'tensor', [(i, (i + by) % n_t) for i in range(n_t)])  60.4 us
    dot_general x8, matrix products, dot_nt(): lax.dot_general(left, right, (((1,), (1,)), ((), ())), preferred_element_...  31.3 us
    unnamed x356, local copies, waits for them, and re-layouts  29.6 us
    dot_general x10, matrix products, dot_nn(): lax.dot_general(left, right, (((1,), (0,)), ((), ())), preferred_element_...  23.1 us
    all_gather x1, blocking collectives, local(): small = lax.all_gather(small, 'tensor', axis=0)  21.7 us
  transfers between devices with their start and end apart: 101, of which 40 were waited for; matrix products, arithmetic and copies ran while one was open for 42% of the time, Pallas kernels for 0%

profile of v1, /device:TPU:0, one launch (start us, length us, event | category | flops | bytes accessed | tf_op | source)
XLA Modules:
  0.0 659.2 jit_solution(12520016782786249365)
XLA Ops:
  4.1 5.0 collective-permute-start.23
  14.2 21.7 %all-gather.1 = f32[4,1,2304]{2,1,0:T(1,128)S(1)} all-gather(f32[1,1,2304]{2,1,0:T(1,128)S(1)} %reshape.724), channel_id=2, replica_groups=mesh['dp'=8,'tensor'=4] {'tensor'}, dimensions={0}, use_global_device_ids=true | all-gather | bytes 46080 | tf_op jit(solution)/shard_map/all_gather | solution.py:178
  63.4 4.0 collective-permute-done.2
  74.7 10.5 %collective-permute-done.15 = bf16[192,768]{1,0:T(8,128)(2,1)S(1)} collective-permute-done((bf16[192,768]{1,0:T(8,128)(2,1)S(1)}, bf16[192,768]{1,0:T(8,128)(2,1)S(1)}, u32[]{:S(2)}, u32[]{:S(2)}) %collective-permute-start.15) | collective-permute-done | bytes 294944 | tf_op jit(solution)/shard_map/ppermute | solution.py:109
  85.2 29.6 %collective-permute-start.30 = (bf16[192,768]{1,0:T(8,128)(2,1)S(1)}, bf16[192,768]{1,0:T(8,128)(2,1)S(1)}, u32[]{:S(2)}, u32[]{:S(2)}) collective-permute-start(bf16[192,768]{1,0:T(8,128)(2,1)S(1)} %pad_maximum_fusion.23), channel_id=1, source_target_pairs={{0,1},{1,2},{2,3},{3,0},{4,5},{5,6},{6,7},{7,4},{8,9},{9,10},{10,1... | collective-permute-start | bytes 884744 | tf_op jit(solution)/shard_map/ppermute | solution.py:109
  114.8 5.7 collective-permute-done.14
  138.9 4.9 collective-permute-done.18
  147.9 5.4 collective-permute-done.35
  157.4 5.4 collective-permute-done.6
  162.8 4.0 collective-permute-start.1
  168.3 4.0 collective-permute-done.25
  174.2 3.7 collective-permute-start.9
  179.4 11.8 %collective-permute-done.17 = bf16[2,3,96,768]{3,2,1,0:T(8,128)(2,1)S(1)} collective-permute-done((bf16[2,3,96,768]{3,2,1,0:T(8,128)(2,1)S(1)}, bf16[2,3,96,768]{3,2,1,0:T(8,128)(2,1)S(1)}, u32[]{:S(2)}, u32[]{:S(2)}) %collective-permute-start.17) | collective-permute-done | bytes 884768 | tf_op jit(solution)/shard_map/ppermute | solution.py:103
  197.5 15.3 %collective-permute-done.34 = bf16[2,3,96,768]{3,2,1,0:T(8,128)(2,1)S(1)} collective-permute-done((bf16[2,3,96,768]{3,2,1,0:T(8,128)(2,1)S(1)}, bf16[2,3,96,768]{3,2,1,0:T(8,128)(2,1)S(1)}, u32[]{:S(2)}, u32[]{:S(2)}) %collective-permute-start.34) | collective-permute-done | bytes 884768 | tf_op jit(solution)/shard_map/ppermute | solution.py:103
  218.7 4.7 maximum_select_fusion.1
  226.1 3.9 select_bitcast_fusion.1
  234.9 3.7 fusion.24
  252.9 10.9 %multiply_convert_fusion.3 = (bf16[512,1536]{1,0:T(8,128)(2,1)S(1)}, f32[512,1536]{1,0:T(8,128)}, f32[512,1536]{1,0:T(8,128)}) fusion(f32[1536]{0:T(1024)S(1)} %copy-done.145, bf16[1536,768]{1,0:T(8,128)(2,1)S(1)} %bitcast.554, f32[512,768]{1,0:T(8,128)S(1)} %get-tuple-element.237, f32[768]{0:T(1024)S(1)} %get-tuple-element.71, ...), kind=kOutput, calls=%fused_computation.83 | convolution fusion | flops 1261830144 | bytes 11812864 | tf_op jit(solution)/shard_map/dot_general | solution.py:21
  288.0 8.1 %multiply_convert_fusion.2 = (bf16[512,1536]{1,0:T(8,128)(2,1)S(1)}, f32[512,1536]{1,0:T(8,128)S(1)}, f32[512,1536]{1,0:T(8,128)S(1)}) fusion(f32[1536]{0:T(1024)S(1)} %copy-done.144, bf16[1536,768]{1,0:T(8,128)(2,1)S(1)} %bitcast.557, f32[512,768]{1,0:T(8,128)S(1)} %get-tuple-element.244, f32[768]{0:T(1024)S(1)} %copy-done.124, ...), kind=kOutput, calls=%fused_computation.70 | convolution fusion | flops 1261830144 | bytes 11812864 | tf_op jit(solution)/shard_map/dot_general | solution.py:21
  308.7 2.9 convolution_convert_fusion.1
  340.5 4.6 fusion.183
  350.6 3.5 collective-permute-done.89
  374.5 4.4 fusion.184
  395.1 10.2 %collective-permute-done.93 = bf16[192,768]{1,0:T(8,128)(2,1)S(1)} collective-permute-done((bf16[192,768]{1,0:T(8,128)(2,1)S(1)}, bf16[192,768]{1,0:T(8,128)(2,1)S(1)}, u32[]{:S(2)}, u32[]{:S(2)}) %collective-permute-start.93) | collective-permute-done | bytes 294944 | tf_op jit(solution)/shard_map/ppermute | solution.py:109
  407.2 12.0 %collective-permute-done.94 = bf16[192,768]{1,0:T(8,128)(2,1)S(1)} collective-permute-done((bf16[192,768]{1,0:T(8,128)(2,1)S(1)}, bf16[192,768]{1,0:T(8,128)(2,1)S(1)}, u32[]{:S(2)}, u32[]{:S(2)}) %collective-permute-start.94) | collective-permute-done | bytes 294944 | tf_op jit(solution)/shard_map/ppermute | solution.py:109
  421.9 3.3 maximum_select_fusion.3
  425.2 3.9 gather_fusion.13
  429.1 7.5 %collective-permute-done.98 = bf16[96,768]{1,0:T(8,128)(2,1)} collective-permute-done((bf16[96,768]{1,0:T(8,128)(2,1)}, bf16[96,768]{1,0:T(8,128)(2,1)}, u32[]{:S(2)}, u32[]{:S(2)}) %collective-permute-start.98) | collective-permute-done | bytes 147488 | tf_op jit(solution)/shard_map/ppermute | solution.py:103
  441.8 3.3 multiply_reduce_fusion.4
  459.4 4.1 fusion.185
  477.2 7.9 %collective-permute-start.75 = (f32[144,128]{1,0:T(8,128)S(1)}, f32[144,128]{1,0:T(8,128)S(1)}, u32[]{:S(2)}, u32[]{:S(2)}) collective-permute-start(f32[144,128]{1,0:T(8,128)S(1)} %add.567), channel_id=1, source_target_pairs={{0,1},{1,0},{2,3},{3,2},{4,5},{5,4},{6,7},{7,6},{8,9},{9,8},{10,11... | collective-permute-start | bytes 221192 | tf_op jit(solution)/shard_map/ppermute | solution.py:309
  490.5 4.3 collective-permute-done.76
  506.5 7.2 %collective-permute-done.78 = bf16[4,96,768]{2,1,0:T(8,128)(2,1)S(1)} collective-permute-done((bf16[4,96,768]{2,1,0:T(8,128)(2,1)S(1)}, bf16[4,96,768]{2,1,0:T(8,128)(2,1)S(1)}, u32[]{:S(2)}, u32[]{:S(2)}) %collective-permute-start.78) | collective-permute-done | bytes 589856 | tf_op jit(solution)/shard_map/ppermute | solution.py:103
  513.9 3.0 collective-permute-done.80
  535.6 9.9 %collective-permute-done.82 = bf16[192,768]{1,0:T(8,128)(2,1)} collective-permute-done((bf16[192,768]{1,0:T(8,128)(2,1)}, bf16[192,768]{1,0:T(8,128)(2,1)}, u32[]{:S(2)}, u32[]{:S(2)}) %collective-permute-start.82) | collective-permute-done | bytes 294944 | tf_op jit(solution)/shard_map/ppermute | solution.py:109
  549.5 3.3 maximum_select_fusion.5
  552.9 3.8 gather_fusion.16
  561.7 5.7 collective-permute-done.87
  568.9 7.6 %collective-permute-done.85 = bf16[2,96,768]{2,1,0:T(8,128)(2,1)S(1)} collective-permute-done((bf16[2,96,768]{2,1,0:T(8,128)(2,1)S(1)}, bf16[2,96,768]{2,1,0:T(8,128)(2,1)S(1)}, u32[]{:S(2)}, u32[]{:S(2)}) %collective-permute-start.85) | collective-permute-done | bytes 294944 | tf_op jit(solution)/shard_map/ppermute | solution.py:103
  584.3 3.9 collective-permute-done.61
  590.5 3.5 collective-permute-start.64
  596.1 3.5 collective-permute-start.51
  599.6 3.1 collective-permute-done.66
  603.3 9.8 %collective-permute-done.65 = bf16[96,768]{1,0:T(8,128)(2,1)S(1)} collective-permute-done((bf16[96,768]{1,0:T(8,128)(2,1)S(1)}, bf16[96,768]{1,0:T(8,128)(2,1)S(1)}, u32[]{:S(2)}, u32[]{:S(2)}) %collective-permute-start.65) | collective-permute-done | bytes 147488 | tf_op jit(solution)/shard_map/ppermute | solution.py:109
  615.1 4.0 collective-permute-done.52
  633.8 3.1 bitcast_convert_fusion.1
  641.4 6.0 copy.179
  647.4 4.2 pad_maximum_fusion.1
  (850 shorter events, 339.1 us)
Async XLA Ops:
  4.1 64.4 %collective-permute-start.23 = (bf16[96,768]{1,0:T(8,128)(2,1)}, bf16[96,768]{1,0:T(8,128)(2,1)}, u32[]{:S(2)}, u32[]{:S(2)}) collective-permute-start(bf16[96,768]{1,0:T(8,128)(2,1)} %fusion.132), channel_id=1, source_target_pairs={{0,3},{1,0},{2,1},{3,2},{4,7},{5,4},{6,5},{7,6},{8,11},{9,8},{10,9... | collective-permute-start | bytes 442376 | tf_op jit(solution)/shard_map/ppermute | solution.py:109
  9.2 59.9 %collective-permute-start.22 = (bf16[96,768]{1,0:T(8,128)(2,1)}, bf16[96,768]{1,0:T(8,128)(2,1)}, u32[]{:S(2)}, u32[]{:S(2)}) collective-permute-start(bf16[96,768]{1,0:T(8,128)(2,1)} %fusion.132), channel_id=1, source_target_pairs={{0,2},{1,3},{2,0},{3,1},{4,6},{5,7},{6,4},{7,5},{8,10},{9,11},{10,... | collective-permute-start | bytes 442376 | tf_op jit(solution)/shard_map/ppermute | solution.py:109
  9.9 49.6 %collective-permute-start.4 = (bf16[96,768]{1,0:T(8,128)(2,1)}, bf16[96,768]{1,0:T(8,128)(2,1)}, u32[]{:S(2)}, u32[]{:S(2)}) collective-permute-start(bf16[96,768]{1,0:T(8,128)(2,1)} %fusion.131), channel_id=1, source_target_pairs={{0,3},{1,0},{2,1},{3,2},{4,7},{5,4},{6,5},{7,6},{8,11},{9,8},{10,9... | collective-permute-start | bytes 442376 | tf_op jit(solution)/shard_map/ppermute | solution.py:109
  10.4 50.3 %collective-permute-start.3 = (bf16[96,768]{1,0:T(8,128)(2,1)}, bf16[96,768]{1,0:T(8,128)(2,1)}, u32[]{:S(2)}, u32[]{:S(2)}) collective-permute-start(bf16[96,768]{1,0:T(8,128)(2,1)} %fusion.131), channel_id=1, source_target_pairs={{0,2},{1,3},{2,0},{3,1},{4,6},{5,7},{6,4},{7,5},{8,10},{9,11},{10,... | collective-permute-start | bytes 442376 | tf_op jit(solution)/shard_map/ppermute | solution.py:109
  12.8 43.7 %collective-permute-start.11 = (s32[2]{0:T(128)}, s32[2]{0:T(128)}, u32[]{:S(2)}, u32[]{:S(2)}) collective-permute-start(s32[2]{0:T(128)} %param.34), channel_id=1, source_target_pairs={{0,4},{4,0},{8,12},{12,8},{16,20},{20,16},{24,28},{28,24},{1,5},{5... | collective-permute-start | bytes 32 | tf_op jit(solution)/shard_map/ppermute | solution.py:103
  60.6 62.4 %collective-permute-start.32 = (bf16[192,768]{1,0:T(8,128)(2,1)S(1)}, bf16[192,768]{1,0:T(8,128)(2,1)S(1)}, u32[]{:S(2)}, u32[]{:S(2)}) collective-permute-start(bf16[192,768]{1,0:T(8,128)(2,1)S(1)} %pad_maximum_fusion.23), channel_id=1, source_target_pairs={{0,3},{1,0},{2,1},{3,2},{4,7},{5,4},{6,5},{7,6},{8,11},{9,8},{10,9... | collective-permute-start | bytes 884744 | tf_op jit(solution)/shard_map/ppermute | solution.py:109
  67.3 57.2 %collective-permute-start.31 = (bf16[192,768]{1,0:T(8,128)(2,1)S(1)}, bf16[192,768]{1,0:T(8,128)(2,1)S(1)}, u32[]{:S(2)}, u32[]{:S(2)}) collective-permute-start(bf16[192,768]{1,0:T(8,128)(2,1)S(1)} %pad_maximum_fusion.23), channel_id=1, source_target_pairs={{0,2},{1,3},{2,0},{3,1},{4,6},{5,7},{6,4},{7,5},{8,10},{9,11},{10,... | collective-permute-start | bytes 884744 | tf_op jit(solution)/shard_map/ppermute | solution.py:109
  69.0 51.5 %collective-permute-start.14 = (bf16[192,768]{1,0:T(8,128)(2,1)S(1)}, bf16[192,768]{1,0:T(8,128)(2,1)S(1)}, u32[]{:S(2)}, u32[]{:S(2)}) collective-permute-start(bf16[192,768]{1,0:T(8,128)(2,1)S(1)} %pad_maximum_fusion.22), channel_id=1, source_target_pairs={{0,2},{1,3},{2,0},{3,1},{4,6},{5,7},{6,4},{7,5},{8,10},{9,11},{10,... | collective-permute-start | bytes 884744 | tf_op jit(solution)/shard_map/ppermute | solution.py:109
  71.6 49.6 %collective-permute-start.13 = (bf16[192,768]{1,0:T(8,128)(2,1)S(1)}, bf16[192,768]{1,0:T(8,128)(2,1)S(1)}, u32[]{:S(2)}, u32[]{:S(2)}) collective-permute-start(bf16[192,768]{1,0:T(8,128)(2,1)S(1)} %pad_maximum_fusion.22), channel_id=1, source_target_pairs={{0,1},{1,2},{2,3},{3,0},{4,5},{5,6},{6,7},{7,4},{8,9},{9,10},{10,1... | collective-permute-start | bytes 884744 | tf_op jit(solution)/shard_map/ppermute | solution.py:109
  85.2 40.9 %collective-permute-start.30 = (bf16[192,768]{1,0:T(8,128)(2,1)S(1)}, bf16[192,768]{1,0:T(8,128)(2,1)S(1)}, u32[]{:S(2)}, u32[]{:S(2)}) collective-permute-start(bf16[192,768]{1,0:T(8,128)(2,1)S(1)} %pad_maximum_fusion.23), channel_id=1, source_target_pairs={{0,1},{1,2},{2,3},{3,0},{4,5},{5,6},{6,7},{7,4},{8,9},{9,10},{10,1... | collective-permute-start | bytes 884744 | tf_op jit(solution)/shard_map/ppermute | solution.py:109
  121.2 177.1 %collective-permute-start.39 = (bf16[256,768]{1,0:T(8,128)(2,1)}, bf16[256,768]{1,0:T(8,128)(2,1)}, u32[]{:S(2)}, u32[]{:S(2)}) collective-permute-start(bf16[256,768]{1,0:T(8,128)(2,1)} %param.35), channel_id=1, source_target_pairs={{1,4},{3,6},{4,1},{6,3},{9,12},{11,14},{12,9},{14,11},{17,20},{19,... | collective-permute-start | bytes 1179656 | tf_op jit(solution)/shard_map/ppermute | solution.py:117
  136.7 18.9 %collective-permute-start.33 = (bf16[3,96,768]{2,1,0:T(8,128)(2,1)S(1)}, bf16[3,96,768]{2,1,0:T(8,128)(2,1)S(1)}, u32[]{:S(2)}, u32[]{:S(2)}) collective-permute-start(bf16[3,96,768]{2,1,0:T(8,128)(2,1)S(1)} %get-tuple-element.144), channel_id=1, source_target_pairs={{0,8},{4,12},{8,0},{12,4},{16,24},{20,28},{24,16},{28,20},{1,9},{5... | collective-permute-start | bytes 1327112 | tf_op jit(solution)/shard_map/ppermute | solution.py:103
  143.8 19.0 %collective-permute-start.6 = (bf16[2,3,48,768]{3,2,1,0:T(8,128)(2,1)S(1)}, bf16[2,3,48,768]{3,2,1,0:T(8,128)(2,1)S(1)}, u32[]{:S(2)}, u32[]{:S(2)}) collective-permute-start(bf16[2,3,48,768]{3,2,1,0:T(8,128)(2,1)S(1)} %pad_maximum_fusion.15), channel_id=1, source_target_pairs={{0,16},{4,20},{8,24},{12,28},{16,0},{20,4},{24,8},{28,12},{1,17},{... | collective-permute-start | bytes 1327112 | tf_op jit(solution)/shard_map/ppermute | solution.py:103
  145.6 21.1 %collective-permute-start.8 = (bf16[2,3,48,768]{3,2,1,0:T(8,128)(2,1)S(1)}, bf16[2,3,48,768]{3,2,1,0:T(8,128)(2,1)S(1)}, u32[]{:S(2)}, u32[]{:S(2)}) collective-permute-start(bf16[2,3,48,768]{3,2,1,0:T(8,128)(2,1)S(1)} %pad_maximum_fusion.16), channel_id=1, source_target_pairs={{0,8},{4,12},{8,0},{12,4},{16,24},{20,28},{24,16},{28,20},{1,9},{5... | collective-permute-start | bytes 1327112 | tf_op jit(solution)/shard_map/ppermute | solution.py:103
  153.3 19.0 %collective-permute-start.25 = (bf16[2,3,48,768]{3,2,1,0:T(8,128)(2,1)S(1)}, bf16[2,3,48,768]{3,2,1,0:T(8,128)(2,1)S(1)}, u32[]{:S(2)}, u32[]{:S(2)}) collective-permute-start(bf16[2,3,48,768]{3,2,1,0:T(8,128)(2,1)S(1)} %pad_maximum_fusion.18), channel_id=1, source_target_pairs={{0,16},{4,20},{8,24},{12,28},{16,0},{20,4},{24,8},{28,12},{1,17},{... | collective-permute-start | bytes 1327112 | tf_op jit(solution)/shard_map/ppermute | solution.py:103
  155.7 18.5 %collective-permute-start.27 = (bf16[2,3,48,768]{3,2,1,0:T(8,128)(2,1)S(1)}, bf16[2,3,48,768]{3,2,1,0:T(8,128)(2,1)S(1)}, u32[]{:S(2)}, u32[]{:S(2)}) collective-permute-start(bf16[2,3,48,768]{3,2,1,0:T(8,128)(2,1)S(1)} %pad_maximum_fusion.19), channel_id=1, source_target_pairs={{0,8},{4,12},{8,0},{12,4},{16,24},{20,28},{24,16},{28,20},{1,9},{5... | collective-permute-start | bytes 1327112 | tf_op jit(solution)/shard_map/ppermute | solution.py:103
  162.8 70.8 %collective-permute-start.1 = (bf16[256,768]{1,0:T(8,128)(2,1)}, bf16[256,768]{1,0:T(8,128)(2,1)}, u32[]{:S(2)}, u32[]{:S(2)}) collective-permute-start(bf16[256,768]{1,0:T(8,128)(2,1)} %broadcast_select_fusion.7), channel_id=1, source_target_pairs={{0,4},{4,0},{8,12},{12,8},{16,20},{20,16},{24,28},{28,24},{1,5},{5... | collective-permute-start | bytes 1179656 | tf_op jit(solution)/shard_map/ppermute | solution.py:103
  166.8 24.4 %collective-permute-start.17 = (bf16[2,3,96,768]{3,2,1,0:T(8,128)(2,1)S(1)}, bf16[2,3,96,768]{3,2,1,0:T(8,128)(2,1)S(1)}, u32[]{:S(2)}, u32[]{:S(2)}) collective-permute-start(bf16[2,3,96,768]{3,2,1,0:T(8,128)(2,1)S(1)} %pad_maximum_fusion.9), channel_id=1, source_target_pairs={{0,16},{4,20},{8,24},{12,28},{16,0},{20,4},{24,8},{28,12},{1,17},{... | collective-permute-start | bytes 2654216 | tf_op jit(solution)/shard_map/ppermute | solution.py:103
  172.2 22.4 %collective-permute-start.19 = (bf16[2,3,96,768]{3,2,1,0:T(8,128)(2,1)S(1)}, bf16[2,3,96,768]{3,2,1,0:T(8,128)(2,1)S(1)}, u32[]{:S(2)}, u32[]{:S(2)}) collective-permute-start(bf16[2,3,96,768]{3,2,1,0:T(8,128)(2,1)S(1)} %pad_maximum_fusion.10), channel_id=1, source_target_pairs={{0,8},{4,12},{8,0},{12,4},{16,24},{20,28},{24,16},{28,20},{1,9},{5... | collective-permute-start | bytes 2654216 | tf_op jit(solution)/shard_map/ppermute | solution.py:103
  174.2 40.7 %collective-permute-start.9 = (bf16[3,4,96,768]{3,2,0,1:T(8,128)(2,1)S(1)}, bf16[3,4,96,768]{3,2,0,1:T(8,128)(2,1)S(1)}, u32[]{:S(2)}, u32[]{:S(2)}) collective-permute-start(bf16[3,4,96,768]{3,2,0,1:T(8,128)(2,1)S(1)} %maximum_maximum_fusion.4), channel_id=1, source_target_pairs={{0,4},{4,0},{8,12},{12,8},{16,20},{20,16},{24,28},{28,24},{1,5},{5... | collective-permute-start | bytes 5308424 | tf_op jit(solution)/shard_map/ppermute | solution.py:103
  191.2 21.5 %collective-permute-start.34 = (bf16[2,3,96,768]{3,2,1,0:T(8,128)(2,1)S(1)}, bf16[2,3,96,768]{3,2,1,0:T(8,128)(2,1)S(1)}, u32[]{:S(2)}, u32[]{:S(2)}) collective-permute-start(bf16[2,3,96,768]{3,2,1,0:T(8,128)(2,1)S(1)} %pad_maximum_fusion.12), channel_id=1, source_target_pairs={{0,16},{4,20},{8,24},{12,28},{16,0},{20,4},{24,8},{28,12},{1,17},{... | collective-permute-start | bytes 2654216 | tf_op jit(solution)/shard_map/ppermute | solution.py:103
  194.6 73.4 %collective-permute-start.36 = (bf16[2,3,96,768]{3,2,1,0:T(8,128)(2,1)}, bf16[2,3,96,768]{3,2,1,0:T(8,128)(2,1)}, u32[]{:S(2)}, u32[]{:S(2)}) collective-permute-start(bf16[2,3,96,768]{3,2,1,0:T(8,128)(2,1)} %pad_maximum_fusion.13), channel_id=1, source_target_pairs={{0,8},{4,12},{8,0},{12,4},{16,24},{20,28},{24,16},{28,20},{1,9},{5... | collective-permute-start | bytes 2654216 | tf_op jit(solution)/shard_map/ppermute | solution.py:103
  325.9 28.2 %collective-permute-start.89 = (bf16[4,2,96,768]{3,2,0,1:T(8,128)(2,1)}, bf16[4,2,96,768]{3,2,0,1:T(8,128)(2,1)}, u32[]{:S(2)}, u32[]{:S(2)}) collective-permute-start(bf16[4,2,96,768]{3,2,0,1:T(8,128)(2,1)} %copy.202), channel_id=1, source_target_pairs={{0,16},{4,20},{8,24},{12,28},{16,0},{20,4},{24,8},{28,12},{1,17},{... | collective-permute-start | bytes 3538952 | tf_op jit(solution)/shard_map/ppermute | solution.py:103
  327.3 31.2 %collective-permute-start.91 = (bf16[4,2,96,768]{3,2,0,1:T(8,128)(2,1)}, bf16[4,2,96,768]{3,2,0,1:T(8,128)(2,1)}, u32[]{:S(2)}, u32[]{:S(2)}) collective-permute-start(bf16[4,2,96,768]{3,2,0,1:T(8,128)(2,1)} %copy.204), channel_id=1, source_target_pairs={{0,8},{4,12},{8,0},{12,4},{16,24},{20,28},{24,16},{28,20},{1,9},{5... | collective-permute-start | bytes 3538952 | tf_op jit(solution)/shard_map/ppermute | solution.py:103
  349.4 71.9 %collective-permute-start.59 = (bf16[2,4,96,768]{3,2,0,1:T(8,128)(2,1)}, bf16[2,4,96,768]{3,2,0,1:T(8,128)(2,1)}, u32[]{:S(2)}, u32[]{:S(2)}) collective-permute-start(bf16[2,4,96,768]{3,2,0,1:T(8,128)(2,1)} %get-tuple-element.122), channel_id=1, source_target_pairs={{0,4},{4,0},{8,12},{12,8},{16,20},{20,16},{24,28},{28,24},{1,5},{5... | collective-permute-start | bytes 3538952 | tf_op jit(solution)/shard_map/ppermute | solution.py:103
  357.0 29.6 %collective-permute-start.90 = (bf16[4,96,768]{2,1,0:T(8,128)(2,1)}, bf16[4,96,768]{2,1,0:T(8,128)(2,1)}, u32[]{:S(2)}, u32[]{:S(2)}) collective-permute-start(bf16[4,96,768]{2,1,0:T(8,128)(2,1)} %slice_bitcast_fusion.6), channel_id=1, source_target_pairs={{0,8},{4,12},{8,0},{12,4},{16,24},{20,28},{24,16},{28,20},{1,9},{5... | collective-permute-start | bytes 1769480 | tf_op jit(solution)/shard_map/ppermute | solution.py:103
  361.1 26.8 %collective-permute-start.92 = (bf16[4,96,768]{2,1,0:T(8,128)(2,1)}, bf16[4,96,768]{2,1,0:T(8,128)(2,1)}, u32[]{:S(2)}, u32[]{:S(2)}) collective-permute-start(bf16[4,96,768]{2,1,0:T(8,128)(2,1)} %slice_bitcast_fusion.4), channel_id=1, source_target_pairs={{0,16},{4,20},{8,24},{12,28},{16,0},{20,4},{24,8},{28,12},{1,17},{... | collective-permute-start | bytes 1769480 | tf_op jit(solution)/shard_map/ppermute | solution.py:103
  380.3 61.5 %collective-permute-start.43 = (bf16[512,768]{1,0:T(8,128)(2,1)}, bf16[512,768]{1,0:T(8,128)(2,1)}, u32[]{:S(2)}, u32[]{:S(2)}) collective-permute-start(bf16[512,768]{1,0:T(8,128)(2,1)} %get-tuple-element.254), channel_id=1, source_target_pairs={{0,4},{4,0},{8,12},{12,8},{16,20},{20,16},{24,28},{28,24},{1,5},{5... | collective-permute-start | bytes 2359304 | tf_op jit(solution)/shard_map/ppermute | solution.py:103
  391.5 27.7 %collective-permute-start.94 = (bf16[192,768]{1,0:T(8,128)(2,1)S(1)}, bf16[192,768]{1,0:T(8,128)(2,1)S(1)}, u32[]{:S(2)}, u32[]{:S(2)}) collective-permute-start(bf16[192,768]{1,0:T(8,128)(2,1)S(1)} %get-tuple-element.138), channel_id=1, source_target_pairs={{0,2},{1,3},{2,0},{3,1},{4,6},{5,7},{6,4},{7,5},{8,10},{9,11},{10,... | collective-permute-start | bytes 884744 | tf_op jit(solution)/shard_map/ppermute | solution.py:109
  405.4 90.9 %collective-permute-start.77 = (bf16[4,2,96,768]{3,2,0,1:T(8,128)(2,1)}, bf16[4,2,96,768]{3,2,0,1:T(8,128)(2,1)}, u32[]{:S(2)}, u32[]{:S(2)}) collective-permute-start(bf16[4,2,96,768]{3,2,0,1:T(8,128)(2,1)} %copy.198), channel_id=1, source_target_pairs={{0,16},{4,20},{8,24},{12,28},{16,0},{20,4},{24,8},{28,12},{1,17},{... | collective-permute-start | bytes 3538952 | tf_op jit(solution)/shard_map/ppermute | solution.py:103
  406.6 92.9 %collective-permute-start.79 = (bf16[4,2,96,768]{3,2,0,1:T(8,128)(2,1)}, bf16[4,2,96,768]{3,2,0,1:T(8,128)(2,1)}, u32[]{:S(2)}, u32[]{:S(2)}) collective-permute-start(bf16[4,2,96,768]{3,2,0,1:T(8,128)(2,1)} %copy.200), channel_id=1, source_target_pairs={{0,8},{4,12},{8,0},{12,4},{16,24},{20,28},{24,16},{28,20},{1,9},{5... | collective-permute-start | bytes 3538952 | tf_op jit(solution)/shard_map/ppermute | solution.py:103
  421.3 18.2 %collective-permute-start.96 = (bf16[96,768]{1,0:T(8,128)(2,1)}, bf16[96,768]{1,0:T(8,128)(2,1)}, u32[]{:S(2)}, u32[]{:S(2)}) collective-permute-start(bf16[96,768]{1,0:T(8,128)(2,1)} %get-tuple-element.196), channel_id=1, source_target_pairs={{0,8},{4,12},{8,0},{12,4},{16,24},{20,28},{24,16},{28,20},{1,9},{5... | collective-permute-start | bytes 442376 | tf_op jit(solution)/shard_map/ppermute | solution.py:103
  438.3 30.0 %collective-permute-start.99 = (bf16[2,96,768]{2,1,0:T(8,128)(2,1)}, bf16[2,96,768]{2,1,0:T(8,128)(2,1)}, u32[]{:S(2)}, u32[]{:S(2)}) collective-permute-start(bf16[2,96,768]{2,1,0:T(8,128)(2,1)} %pad_maximum_fusion.27), channel_id=1, source_target_pairs={{0,8},{4,12},{8,0},{12,4},{16,24},{20,28},{24,16},{28,20},{1,9},{5... | collective-permute-start | bytes 884744 | tf_op jit(solution)/shard_map/ppermute | solution.py:103
  441.1 36.0 %collective-permute-start.97 = (bf16[2,96,768]{2,1,0:T(8,128)(2,1)}, bf16[2,96,768]{2,1,0:T(8,128)(2,1)}, u32[]{:S(2)}, u32[]{:S(2)}) collective-permute-start(bf16[2,96,768]{2,1,0:T(8,128)(2,1)} %pad_maximum_fusion.26), channel_id=1, source_target_pairs={{0,16},{4,20},{8,24},{12,28},{16,0},{20,4},{24,8},{28,12},{1,17},{... | collective-permute-start | bytes 884744 | tf_op jit(solution)/shard_map/ppermute | solution.py:103
  467.7 35.2 %collective-permute-start.44 = (bf16[512,768]{1,0:T(8,128)(2,1)}, bf16[512,768]{1,0:T(8,128)(2,1)}, u32[]{:S(2)}, u32[]{:S(2)}) collective-permute-start(bf16[512,768]{1,0:T(8,128)(2,1)} %get-tuple-element.258), channel_id=1, source_target_pairs={{0,4},{4,0},{8,12},{12,8},{16,20},{20,16},{24,28},{28,24},{1,5},{5... | collective-permute-start | bytes 2359304 | tf_op jit(solution)/shard_map/ppermute | solution.py:103
  477.1 43.0 %collective-permute-start.46 = (bf16[2,4,96,768]{3,2,0,1:T(8,128)(2,1)}, bf16[2,4,96,768]{3,2,0,1:T(8,128)(2,1)}, u32[]{:S(2)}, u32[]{:S(2)}) collective-permute-start(bf16[2,4,96,768]{3,2,0,1:T(8,128)(2,1)} %get-tuple-element.120), channel_id=1, source_target_pairs={{0,4},{4,0},{8,12},{12,8},{16,20},{20,16},{24,28},{28,24},{1,5},{5... | collective-permute-start | bytes 3538952 | tf_op jit(solution)/shard_map/ppermute | solution.py:103
  494.9 53.5 %collective-permute-start.100 = (bf16[2,4,96,768]{3,2,1,0:T(8,128)(2,1)}, bf16[2,4,96,768]{3,2,1,0:T(8,128)(2,1)}, u32[]{:S(2)}, u32[]{:S(2)}) collective-permute-start(bf16[2,4,96,768]{3,2,1,0:T(8,128)(2,1)} %get-tuple-element.135), channel_id=1, source_target_pairs={{0,4},{4,0},{8,12},{12,8},{16,20},{20,16},{24,28},{28,24},{1,5},{5... | collective-permute-start | bytes 3538952 | tf_op jit(solution)/shard_map/ppermute | solution.py:103
  505.0 53.9 %collective-permute-start.45 = (f32[256,768]{1,0:T(8,128)}, f32[256,768]{1,0:T(8,128)}, u32[]{:S(2)}, u32[]{:S(2)}) collective-permute-start(f32[256,768]{1,0:T(8,128)} %fusion.64), channel_id=1, source_target_pairs={{1,4},{3,6},{4,1},{6,3},{9,12},{11,14},{12,9},{14,11},{17,20},{19,... | collective-permute-start | bytes 2359304 | tf_op jit(solution)/shard_map/ppermute | solution.py:117
  520.1 25.3 %collective-permute-start.82 = (bf16[192,768]{1,0:T(8,128)(2,1)}, bf16[192,768]{1,0:T(8,128)(2,1)}, u32[]{:S(2)}, u32[]{:S(2)}) collective-permute-start(bf16[192,768]{1,0:T(8,128)(2,1)} %get-tuple-element.133), channel_id=1, source_target_pairs={{0,2},{1,3},{2,0},{3,1},{4,6},{5,7},{6,4},{7,5},{8,10},{9,11},{10,... | collective-permute-start | bytes 884744 | tf_op jit(solution)/shard_map/ppermute | solution.py:109
  533.6 43.2 %collective-permute-start.60 = (bf16[4,2,48,768]{3,2,0,1:T(8,128)(2,1)}, bf16[4,2,48,768]{3,2,0,1:T(8,128)(2,1)}, u32[]{:S(2)}, u32[]{:S(2)}) collective-permute-start(bf16[4,2,48,768]{3,2,0,1:T(8,128)(2,1)} %slice.782), channel_id=1, source_target_pairs={{0,16},{4,20},{8,24},{12,28},{16,0},{20,4},{24,8},{28,12},{1,17},{... | collective-permute-start | bytes 1769480 | tf_op jit(solution)/shard_map/ppermute | solution.py:103
  534.4 44.9 %collective-permute-start.62 = (bf16[4,2,48,768]{3,2,0,1:T(8,128)(2,1)}, bf16[4,2,48,768]{3,2,0,1:T(8,128)(2,1)}, u32[]{:S(2)}, u32[]{:S(2)}) collective-permute-start(bf16[4,2,48,768]{3,2,0,1:T(8,128)(2,1)} %slice.613), channel_id=1, source_target_pairs={{0,8},{4,12},{8,0},{12,4},{16,24},{20,28},{24,16},{28,20},{1,9},{5... | collective-permute-start | bytes 1769480 | tf_op jit(solution)/shard_map/ppermute | solution.py:103
  556.7 25.1 %collective-permute-start.47 = (bf16[4,2,48,768]{3,2,0,1:T(8,128)(2,1)}, bf16[4,2,48,768]{3,2,0,1:T(8,128)(2,1)S(1)}, u32[]{:S(2)}, u32[]{:S(2)}) collective-permute-start(bf16[4,2,48,768]{3,2,0,1:T(8,128)(2,1)} %slice.764), channel_id=1, source_target_pairs={{0,16},{4,20},{8,24},{12,28},{16,0},{20,4},{24,8},{28,12},{1,17},{... | collective-permute-start | bytes 1769480 | tf_op jit(solution)/shard_map/ppermute | solution.py:103
  558.9 23.7 %collective-permute-start.49 = (bf16[4,2,48,768]{3,2,0,1:T(8,128)(2,1)S(1)}, bf16[4,2,48,768]{3,2,0,1:T(8,128)(2,1)S(1)}, u32[]{:S(2)}, u32[]{:S(2)}) collective-permute-start(bf16[4,2,48,768]{3,2,0,1:T(8,128)(2,1)S(1)} %copy-done.89), channel_id=1, source_target_pairs={{0,8},{4,12},{8,0},{12,4},{16,24},{20,28},{24,16},{28,20},{1,9},{5... | collective-permute-start | bytes 1769480 | tf_op jit(solution)/shard_map/ppermute | solution.py:103
  576.7 54.7 %collective-permute-start.88 = (bf16[2,4,96,768]{3,2,1,0:T(8,128)(2,1)S(1)}, bf16[2,4,96,768]{3,2,1,0:T(8,128)(2,1)S(1)}, u32[]{:S(2)}, u32[]{:S(2)}) collective-permute-start(bf16[2,4,96,768]{3,2,1,0:T(8,128)(2,1)S(1)} %get-tuple-element.130), channel_id=1, source_target_pairs={{0,4},{4,0},{8,12},{12,8},{16,20},{20,16},{24,28},{28,24},{1,5},{5... | collective-permute-start | bytes 3538952 | tf_op jit(solution)/shard_map/ppermute | solution.py:103
  594.1 19.0 %collective-permute-start.65 = (bf16[96,768]{1,0:T(8,128)(2,1)S(1)}, bf16[96,768]{1,0:T(8,128)(2,1)S(1)}, u32[]{:S(2)}, u32[]{:S(2)}) collective-permute-start(bf16[96,768]{1,0:T(8,128)(2,1)S(1)} %get-tuple-element.164), channel_id=1, source_target_pairs={{0,2},{1,3},{2,0},{3,1},{4,6},{5,7},{6,4},{7,5},{8,10},{9,11},{10,... | collective-permute-start | bytes 442376 | tf_op jit(solution)/shard_map/ppermute | solution.py:109
  596.1 18.4 %collective-permute-start.51 = (bf16[96,768]{1,0:T(8,128)(2,1)S(1)}, bf16[96,768]{1,0:T(8,128)(2,1)S(1)}, u32[]{:S(2)}, u32[]{:S(2)}) collective-permute-start(bf16[96,768]{1,0:T(8,128)(2,1)S(1)} %get-tuple-element.159), channel_id=1, source_target_pairs={{0,3},{1,0},{2,1},{3,2},{4,7},{5,4},{6,5},{7,6},{8,11},{9,8},{10,9... | collective-permute-start | bytes 442376 | tf_op jit(solution)/shard_map/ppermute | solution.py:109
  629.6 21.9 %collective-permute-start.71 = (bf16[4,96,768]{2,1,0:T(8,128)(2,1)}, bf16[4,96,768]{2,1,0:T(8,128)(2,1)S(1)}, u32[]{:S(2)}, u32[]{:S(2)}) collective-permute-start(bf16[4,96,768]{2,1,0:T(8,128)(2,1)} %maximum_maximum_fusion.7), channel_id=1, source_target_pairs={{0,4},{4,0},{8,12},{12,8},{16,20},{20,16},{24,28},{28,24},{1,5},{5... | collective-permute-start | bytes 1769480 | tf_op jit(solution)/shard_map/ppermute | solution.py:103
  631.4 21.1 %collective-permute-start.58 = (bf16[4,96,768]{2,1,0:T(8,128)(2,1)}, bf16[4,96,768]{2,1,0:T(8,128)(2,1)}, u32[]{:S(2)}, u32[]{:S(2)}) collective-permute-start(bf16[4,96,768]{2,1,0:T(8,128)(2,1)} %maximum_maximum_fusion.6), channel_id=1, source_target_pairs={{0,4},{4,0},{8,12},{12,8},{16,20},{20,16},{24,28},{28,24},{1,5},{5... | collective-permute-start | bytes 1769480 | tf_op jit(solution)/shard_map/ppermute | solution.py:103
  (225 other events, 2607.8 us)

commit v2 on v1

v2 whole, which is shorter than its diff:
```python
import functools
import math

import jax
import jax.numpy as jnp
from jax import lax
from jax.experimental import pallas as pl
from jax.experimental.pallas import tpu as pltpu
from jax.sharding import PartitionSpec as P

HEAD_DIM = 64
epsilon = 1e-06
masked_fill = -1e30
bf16 = jnp.bfloat16
f32 = jnp.float32
ANY = pl.BlockSpec(memory_space=pl.ANY)
SMEM = pl.BlockSpec(memory_space=pltpu.SMEM)
VMEM = pl.BlockSpec(memory_space=pltpu.VMEM)
ROOM = 56 * 1024 * 1024
SLOTS = 2


def dot_nn(left, right):
    return lax.dot_general(left, right, (((1,), (0,)), ((), ())), preferred_element_type=f32)


def dot_nt(left, right):
    return lax.dot_general(left, right, (((1,), (1,)), ((), ())), preferred_element_type=f32)


def dot_tn(left, right):
    return lax.dot_general(left, right, (((0,), (0,)), ((), ())), preferred_element_type=f32)


def norm_forward(summed, gain, shift):
    center = summed - jnp.mean(summed, -1, keepdims=True)
    recip = lax.rsqrt(jnp.mean(center * center, -1, keepdims=True) + epsilon)
    normed = center * recip
    return normed * gain + shift, normed, recip


def norm_backward(grad_rows, normed, recip, gain):
    scaled = grad_rows * gain
    first_mean = jnp.mean(scaled, -1, keepdims=True)
    second_mean = jnp.mean(scaled * normed, -1, keepdims=True)
    return recip * (scaled - first_mean - normed * second_mean)


def shape(dims, dtype):
    return jax.ShapeDtypeStruct(dims, dtype)


def params(**more):
    return pltpu.CompilerParams(vmem_limit_bytes=ROOM, **more)


def cost(us):
    return pl.CostEstimate(flops=int(us * 1.1e9), bytes_accessed=int(us * 3.6e6), transcendentals=0)


def lane_half(rows, which):
    lane = lax.broadcasted_iota(jnp.int32, (rows, 2 * HEAD_DIM), 1)
    return (lane < HEAD_DIM) if which == 0 else (lane >= HEAD_DIM)


def fetch_attn(scal, layer, own_qkv, own_out, a_refs, b_refs, w, sems):
    core, place = scal[0], scal[1]
    cols = own_out.shape[1]

    def b_copy(j):
        return pltpu.make_async_copy(b_refs[j].at[pl.ds(0, cols)], w.at[j ^ place, pl.ds(cols, cols)], sems.at[j])

    def a_copy(j):
        return pltpu.make_async_copy(a_refs[j].at[pl.ds(0, cols)], w.at[j ^ place, pl.ds(0, cols)], sems.at[4 + j])

    def own_copy(j):
        own = own_qkv.at[layer, j] if j < 3 else own_out.at[layer]
        return pltpu.make_async_copy(own, w.at[j, pl.ds(0, cols)], sems.at[4 + j])

    for j in range(4):
        b_copy(j).start()

    @pl.when(core == 0)
    def _():
        for j in range(4):
            own_copy(j).start()

    @pl.when(core != 0)
    def _():
        for j in range(4):
            a_copy(j).start()

    def wait():
        for j in range(4):
            b_copy(j).wait()
            own_copy(j).wait()

    return wait


def fetch_ff(scal, layer, own_up, own_down, moved, wu, wd, sems):
    core, place = scal[0], scal[1]
    n_t, width, half = wu.shape
    part, rows = width // 4, half // 4
    own, x, y, diag_up, diag_down = moved
    ups = [own.at[0], x.at[0], y.at[0], diag_up]
    downs = [own.at[1], x.at[1], y.at[1], diag_down]
    others = pl.ds(1, n_t - 1)
    copies = [
        pltpu.make_async_copy(own_up.at[layer, :, pl.ds(pl.multiple_of(core * half, half), half)], wu.at[0], sems.at[0]),
        pltpu.make_async_copy(own_down.at[layer, pl.ds(pl.multiple_of(core * half, half), half)], wd.at[0], sems.at[1]),
    ]
    for j in range(4):
        at = pl.ds(pl.multiple_of((j ^ place) * part, part), part)
        copies.append(pltpu.make_async_copy(ups[j], wu.at[others, at], sems.at[2 + 3 * j]))
        at = pl.ds(pl.multiple_of((j ^ place) * rows, rows), rows)
        for n in range(2):
            copies.append(
                pltpu.make_async_copy(
                    downs[j].at[:, pl.ds(n * rows, rows)],
                    wd.at[others, at, pl.ds(n * half, half)],
                    sems.at[3 + 3 * j + n],
                )
            )
    for c in copies:
        c.start()
    for c in copies:
        c.wait()


BIAS_ROWS = 16


def split_rows(v):
    parts = []
    for _ in range(3):
        low = v.astype(bf16)
        parts.append(low)
        v = v - low.astype(f32)
    n = sum(p.shape[0] for p in parts)
    return jnp.concatenate(parts + [jnp.zeros((BIAS_ROWS - n, v.shape[1]), bf16)], 0)


def pack_bias_kernel(scal, up_bias, qv_bias, out_up, out_qv):
    half = out_up.shape[2]
    for l in range(out_up.shape[0]):
        row = jnp.where(scal[0] == 0, up_bias[l : l + 1, :half], up_bias[l : l + 1, half:])
        out_up[l] = split_rows(row)
    out_qv[...] = split_rows(qv_bias[...])


def pack_bias(scal, up_bias, qv_bias):
    layers, hidden = up_bias.shape
    return pl.pallas_call(
        pack_bias_kernel,
        out_shape=[
            shape((layers, BIAS_ROWS, hidden // 2), bf16),
            shape((BIAS_ROWS, qv_bias.shape[1]), bf16),
        ],
        in_specs=[SMEM, VMEM, VMEM],
        out_specs=[VMEM, VMEM],
        compiler_params=params(),
        cost_estimate=cost(1),
        name="pack_bias",
    )(scal, up_bias, qv_bias)


def attn_fwd_kernel(layer, *refs):
    refs = list(refs)
    scal = refs.pop(0)
    first = layer == 0
    if first:
        x_mine, x_theirs = refs[:2]
        refs = refs[2:]
    else:
        h_in, f_mine, f_theirs, ob, gain, shift = refs[:6]
        refs = refs[6:]
    seg_row, seg_col = refs[:2]
    own_bias, a_bias, b_bias, own_qkv, own_out = refs[2:7]
    a_refs, b_refs = refs[7:11], refs[11:15]
    refs = refs[15:]
    state, xr = refs[:2]
    refs = refs[2:]
    if not first:
        normed, recip = refs[:2]
        refs = refs[2:]
    qkv, lse_t, o, a_low, w, mask, lse, packed, sems = refs
    cols = own_out.shape[1]
    bias_copies = [
        pltpu.make_async_copy(ref.at[pl.ds(cols, BIAS_ROWS)], packed.at[n], sems.at[8 + n])
        for n, ref in enumerate((a_bias, b_bias))
    ]
    for c in bias_copies:
        c.start()
    wait = fetch_attn(scal, layer, own_qkv, own_out, a_refs, b_refs, w, sems)
    core, slots = scal[0], scal[2]
    seq = xr.shape[0]
    half = seq // 2
    if first:
        mine = x_mine[...]
        theirs = x_theirs[...]
        at = pl.ds(pl.multiple_of(core * half, half), half)
        xr[at] = mine
        state[at] = mine.astype(f32)
        at = pl.ds(pl.multiple_of((1 - core) * half, half), half)
        xr[at] = theirs
        state[at] = theirs.astype(f32)
    else:
        @pl.loop(0, seq // 128)
        def _(i):
            at = pl.ds(pl.multiple_of(i * 128, 128), 128)
            z = h_in[at] + (f_mine[at].astype(f32) + f_theirs[at].astype(f32)) + ob[layer - 1, 1:2]
            new, n, r = norm_forward(z, gain[layer - 1, 1:2], shift[layer - 1, 1:2])
            state[at] = new
            xr[at] = new.astype(bf16)
            normed[at] = n
            recip[at] = r

    qi = lax.broadcasted_iota(jnp.int32, (seq, seq), 0)
    ki = lax.broadcasted_iota(jnp.int32, (seq, seq), 1)
    visible = (seg_col[...] == seg_row[...]) & ((ki < slots) | (qi >= slots))
    mask[...] = jnp.where(visible, 0.0, masked_fill)
    for c in bias_copies:
        c.wait()
    a_row, b_row = (jnp.sum(packed[n, 0:3].astype(f32), 0, keepdims=True) for n in range(2))
    a_row = jnp.where(core == 0, own_bias[...], a_row)
    qb = []
    for i in range(2):
        base = (2 * layer + i) * cols
        qb.append(jnp.concatenate([a_row[:, base : base + cols], b_row[:, base : base + cols]], 1))
    wait()
    rows = 256
    for t in range(3):
        for i in range(seq // rows):
            at = pl.ds(i * rows, rows)
            acc = dot_nt(xr[at], w[t])
            if t != 1:
                acc = acc + qb[t // 2]
            qkv[t, at] = acc.astype(bf16)
    pairs = qkv.shape[2] // 128
    tile = 128
    lane = lax.broadcasted_iota(jnp.int32, (tile, 128), 1)

    @pl.loop(0, seq // tile)
    def _(i):
        at = pl.ds(pl.multiple_of(i * tile, tile), tile)
        bias = mask[at]
        keep = jnp.zeros((tile, 128), f32)
        for g in range(pairs):
            cs = pl.ds(g * 128, 128)
            q2 = qkv[0, at, cs] * jnp.asarray(1.0 / math.sqrt(HEAD_DIM), bf16)
            k2 = qkv[1, :, cs]
            v2 = qkv[2, :, cs]
            acc = None
            for hh in range(2):
                qm = jnp.where(lane_half(tile, hh), q2, jnp.zeros_like(q2))
                s = dot_nt(qm, k2) + bias
                top = jnp.max(s, -1, keepdims=True)
                e = jnp.exp(s - top)
                d = jnp.sum(e, -1, keepdims=True)
                pr = (e * (1.0 / d)).astype(bf16)
                keep = jnp.where(lane == 2 * g + hh, top + jnp.log(d), keep)
                vm = jnp.where(lane_half(seq, hh), v2, jnp.zeros_like(v2))
                got = dot_nn(pr, vm)
                acc = got if acc is None else acc + got
            o[at, cs] = acc.astype(bf16)
        lse[at] = keep

    lse_t[...] = jnp.transpose(lse[...])[0:8]
    for i in range(seq // rows):
        at = pl.ds(i * rows, rows)
        a_low[at] = dot_nn(o[at], w[3]).astype(bf16)


def attn_fwd(layer, scal, rows_in, seg_row, seg_col, bias, own_qkv, own_out, a_refs, b_refs):
    first = layer == 0
    seq, width, cols = seg_row.shape[1], own_out.shape[2], own_out.shape[1]
    wide = SLOTS * cols
    outs = [shape((seq, width), f32), shape((seq, width), bf16)]
    if not first:
        outs += [shape((seq, width), f32), shape((seq, 1), f32)]
    outs += [
        shape((3, seq, wide), bf16),
        shape((8, seq), f32),
        shape((seq, wide), bf16),
        shape((seq, width), bf16),
    ]
    got = pl.pallas_call(
        functools.partial(attn_fwd_kernel, layer),
        out_shape=outs,
        in_specs=[SMEM] + [VMEM] * (len(rows_in) + 3) + [ANY] * 12,
        out_specs=[VMEM] * len(outs),
        scratch_shapes=[
            pltpu.VMEM((4, wide, width), bf16),
            pltpu.VMEM((seq, seq), f32),
            pltpu.VMEM((seq, 128), f32),
            pltpu.VMEM((2, BIAS_ROWS, width), bf16),
            pltpu.SemaphoreType.DMA((10,)),
        ],
        compiler_params=params(),
        cost_estimate=cost(12),
        name="attn_fwd",
    )(scal, *rows_in, seg_row, seg_col, *bias, own_qkv, own_out, *a_refs, *b_refs)
    if first:
        state, xr, qkv, lse_t, o, a_low = got
        return state, xr, None, None, qkv, lse_t, o, a_low
    return got


def ff_fwd_kernel(layer, scal, state, a_mine, a_theirs, ob, gain, shift, ub, own_up, own_down, *refs):
    moved = refs[:5]
    h, hr, normed, recip, g, gp, f_low, wu, wd, sems = refs[5:]
    step = pl.program_id(0)

    @pl.when(step == 0)
    def _():
        fetch_ff(scal, layer, own_up, own_down, moved, wu, wd, sems)

    z = state[...] + (a_mine[...].astype(f32) + a_theirs[...].astype(f32)) + ob[layer, 0:1]
    new, n, r = norm_forward(z, gain[layer, 0:1], shift[layer, 0:1])
    h[...] = new
    low = new.astype(bf16)
    hr[...] = low
    normed[...] = n
    recip[...] = r
    acc = None
    for k in range(wu.shape[0]):
        u = dot_nn(low, wu[k]) + ub[k : k + 1]
        phi = 0.5 * (1.0 + lax.erf(u * math.sqrt(0.5)))
        act = (u * phi).astype(bf16)
        g[k] = act
        gp[k] = (phi + u * (jnp.exp(-0.5 * u * u) * (1.0 / math.sqrt(2 * math.pi)))).astype(bf16)
        got = dot_nn(act, wd[k])
        acc = got if acc is None else acc + got
    f_low[...] = acc.astype(bf16)


def ff_scratch(n_t, width, half):
    return [
        pltpu.VMEM((n_t, width, half), bf16),
        pltpu.VMEM((n_t, half, width), bf16),
        pltpu.SemaphoreType.DMA((14,)),
    ]


def ff_fwd(layer, scal, state, a_mine, a_theirs, norms, ub, own_up, own_down, moved):
    seq, width = state.shape
    n_t, half = ub.shape
    rows = 256
    by_row = pl.BlockSpec((rows, width), lambda i: (i, 0))
    whole = lambda v: pl.BlockSpec(v.shape, lambda i: (0,) * v.ndim)
    by_quarter = pl.BlockSpec((n_t, rows, half), lambda i: (0, i, 0))
    return pl.pallas_call(
        functools.partial(ff_fwd_kernel, layer),
        grid=(seq // rows,),
        out_shape=[
            shape((seq, width), f32),
            shape((seq, width), bf16),
            shape((seq, width), f32),
            shape((seq, 1), f32),
            shape((n_t, seq, half), bf16),
            shape((n_t, seq, half), bf16),
            shape((seq, width), bf16),
        ],
        in_specs=[SMEM, by_row, by_row, by_row] + [whole(v) for v in norms] + [whole(ub)] + [ANY] * 7,
        out_specs=[
            by_row,
            by_row,
            by_row,
            pl.BlockSpec((rows, 1), lambda i: (i, 0)),
            by_quarter,
            by_quarter,
            by_row,
        ],
        scratch_shapes=ff_scratch(n_t, width, half),
        compiler_params=params(),
        cost_estimate=cost(11),
        name="ff_fwd",
    )(scal, state, a_mine, a_theirs, *norms, ub, own_up, own_down, *moved)


def ff_bwd_kernel(last, layer, scal, *refs):
    refs = list(refs)
    if last:
        h, f_mine, f_theirs, c_mine, c_theirs = refs[:5]
        refs = refs[5:]
    else:
        dz_in, x_mine, x_theirs, normed, recip = refs[:5]
        refs = refs[5:]
    ob, gain, shift, gp, own_up, own_down = refs[:6]
    moved = refs[6:11]
    refs = refs[11:]
    if last:
        out_low = refs.pop(0)
    dz2, dzr2, du, dh_low, small, ub_sum, wu, wd, sems = refs
    step = pl.program_id(0)

    @pl.when(step == 0)
    def _():
        small[...] = jnp.zeros_like(small)
        ub_sum[...] = jnp.zeros_like(ub_sum)
        fetch_ff(scal, layer, own_up, own_down, moved, wu, wd, sems)

    if last:
        z = h[...] + (f_mine[...].astype(f32) + f_theirs[...].astype(f32)) + ob[layer, 1:2]
        new, n, r = norm_forward(z, gain[layer, 1:2], shift[layer, 1:2])
        out_low[...] = new.astype(bf16)
        dy = jnp.where(step == scal[0], c_mine[...], c_theirs[...]).astype(f32)
    else:
        dy = dz_in[...] + (x_mine[...].astype(f32) + x_theirs[...].astype(f32))
        n, r = normed[...], recip[...]
    dz = norm_backward(dy, n, r, gain[layer, 1:2])
    dz2[...] = dz
    low = dz.astype(bf16)
    dzr2[...] = low
    small[0:1] += jnp.sum(dy * n, 0, keepdims=True)
    small[1:2] += jnp.sum(dy, 0, keepdims=True)
    small[2:3] += jnp.sum(dz, 0, keepdims=True)
    acc = None
    for k in range(wu.shape[0]):
        dg = dot_nt(low, wd[k])
        back = (dg * gp[k].astype(f32)).astype(bf16)
        du[k] = back
        ub_sum[k : k + 1] += jnp.sum(back.astype(f32), 0, keepdims=True)
        got = dot_nt(back, wu[k])
        acc = got if acc is None else acc + got
    dh_low[...] = acc.astype(bf16)


def ff_bwd(layer, scal, rows_in, norms, gp, own_up, own_down, moved, last):
    width = own_up.shape[1]
    n_t, seq, half = gp.shape
    rows = 256
    by_row = pl.BlockSpec((rows, width), lambda i: (i, 0))
    whole = lambda v: pl.BlockSpec(v.shape, lambda i: (0,) * v.ndim)
    by_quarter = pl.BlockSpec((n_t, rows, half), lambda i: (0, i, 0))
    if last:
        specs = [by_row] * 3 + [whole(rows_in[3]), whole(rows_in[4])]
    else:
        specs = [by_row] * 4 + [pl.BlockSpec((rows, 1), lambda i: (i, 0))]
    outs = [
        shape((seq, width), f32),
        shape((seq, width), bf16),
        shape((n_t, seq, half), bf16),
        shape((seq, width), bf16),
        shape((8, width), f32),
        shape((n_t, half), f32),
    ]
    out_specs = [by_row, by_row, by_quarter, by_row, pl.BlockSpec((8, width), lambda i: (0, 0)), pl.BlockSpec((n_t, half), lambda i: (0, 0))]
    if last:
        outs = [shape((seq, width), bf16)] + outs
        out_specs = [by_row] + out_specs
    return pl.pallas_call(
        functools.partial(ff_bwd_kernel, last, layer),
        grid=(seq // rows,),
        out_shape=outs,
        in_specs=[SMEM] + specs + [whole(v) for v in norms] + [by_quarter] + [ANY] * 7,
        out_specs=out_specs,
        scratch_shapes=ff_scratch(n_t, width, half),
        compiler_params=params(),
        cost_estimate=cost(11),
        name="ff_bwd",
    )(scal, *rows_in, *norms, gp, own_up, own_down, *moved)


SEND = ((2, 3), (1, 3))
NEXT = (1, 2)


def ff_dw_kernel(z_first, scal, g, du, hr, dzr2, *refs):
    outs, (su, sd, sems) = refs[:-3], refs[-3:]
    place = scal[1]
    n_t, width, half = su.shape
    part, rows = width // 4, half // 4

    def target(s, j):
        send, nxt, keep = outs[3 * s : 3 * s + 3]
        if j in SEND[s]:
            return send.at[SEND[s].index(j)]
        return nxt if j == NEXT[s] else keep

    def quarter(k):
        return lax.rem(scal[3] + n_t - k, n_t)

    copies = []

    def start(src, dst):
        copies.append(pltpu.make_async_copy(src, dst, sems.at[len(copies)]))
        copies[-1].start()

    chunk = 256
    for k in range(n_t):
        for c in range(width // chunk):
            at = pl.ds(c * chunk, chunk)
            su[k, at] = dot_tn(hr[:, at], du[k]).astype(bf16)
        if z_first:
            for p in range(4):
                start(su.at[k, pl.ds(p * part, part)], outs[0].at[quarter(k), p, 0])
    if not z_first:
        for j in range(4):
            at = pl.ds(pl.multiple_of((j ^ place) * part, part), part)
            start(su.at[:, at], target(0, j))
    for k in range(n_t):
        sd[k] = dot_tn(g[k], dzr2[...]).astype(bf16)
        if z_first:
            for p in range(4):
                for n in range(2):
                    start(
                        sd.at[k, pl.ds(p * rows, rows), pl.ds(n * half, half)],
                        outs[0].at[quarter(k), p, 1, pl.ds(n * rows, rows)],
                    )
    if not z_first:
        for j in range(4):
            at = pl.ds(pl.multiple_of((j ^ place) * rows, rows), rows)
            for n in range(2):
                start(sd.at[:, at, pl.ds(n * half, half)], target(1, j).at[:, pl.ds(n * rows, rows)])
    for c in copies:
        c.wait()


def ff_dw(scal, g, du, hr, dzr2, z_first):
    n_t, _, half = g.shape
    width = hr.shape[1]
    one = (n_t, width // 4, half)
    if z_first:
        outs = [shape((n_t, 4, 2, width // 4, half), bf16)]
    else:
        outs = [shape((2,) + one, bf16), shape(one, bf16), shape(one, bf16)] * 2
    return pl.pallas_call(
        functools.partial(ff_dw_kernel, z_first),
        out_shape=outs,
        in_specs=[SMEM] + [VMEM] * 4,
        out_specs=[ANY] * len(outs),
        scratch_shapes=[
            pltpu.VMEM((n_t, width, half), bf16),
            pltpu.VMEM((n_t, half, width), bf16),
            pltpu.SemaphoreType.DMA((12 * n_t,)),
        ],
        compiler_params=params(),
        cost_estimate=cost(6),
        name="ff_dw",
    )(scal, g, du, hr, dzr2)


def attn_bwd_kernel(layer, scal, dz2, h_mine, h_theirs, normed, recip, gain, qkv, lse_t, o, seg_row, seg_col, own_qkv, own_out, *refs):
    a_refs, b_refs = refs[:4], refs[4:8]
    dz1, dzr1, d4, dx_low, small, w, mask, do, sems = refs[8:]
    wait = fetch_attn(scal, layer, own_qkv, own_out, a_refs, b_refs, w, sems)
    slots = scal[2]
    seq, width = dz1.shape
    small[...] = jnp.zeros_like(small)

    @pl.loop(0, seq // 128)
    def _(i):
        at = pl.ds(pl.multiple_of(i * 128, 128), 128)
        dh = dz2[at] + (h_mine[at].astype(f32) + h_theirs[at].astype(f32))
        n = normed[at]
        dz = norm_backward(dh, n, recip[at], gain[layer, 0:1])
        dz1[at] = dz
        dzr1[at] = dz.astype(bf16)
        small[0:1] += jnp.sum(dh * n, 0, keepdims=True)
        small[1:2] += jnp.sum(dh, 0, keepdims=True)
        small[2:3] += jnp.sum(dz, 0, keepdims=True)

    ki = lax.broadcasted_iota(jnp.int32, (seq, seq), 0)
    qi = lax.broadcasted_iota(jnp.int32, (seq, seq), 1)
    visible = (seg_col[...] == seg_row[...]) & ((ki < slots) | (qi >= slots))
    mask[...] = jnp.where(visible, 0.0, masked_fill)
    wait()
    rows = 256
    for i in range(seq // rows):
        at = pl.ds(i * rows, rows)
        do[at] = dot_nt(dzr1[at], w[3]).astype(bf16)
    d4[3] = o[...]
    pairs = qkv.shape[2] // 128
    tile = 256
    scale = 1.0 / math.sqrt(HEAD_DIM)
    for g in range(pairs):
        cs = pl.ds(g * 128, 128)
        k2 = qkv[1, :, cs] * jnp.asarray(scale, bf16)
        v2 = qkv[2, :, cs]
        dv = dk = None
        for i in range(seq // tile):
            at = pl.ds(i * tile, tile)
            q2 = qkv[0, at, cs]
            do2 = do[at, cs]
            bias = mask[:, at]
            dq = None
            for hh in range(2):
                all_half = lane_half(seq, hh)
                tile_half = lane_half(tile, hh)
                km = jnp.where(all_half, k2, jnp.zeros_like(k2))
                vm = jnp.where(all_half, v2, jnp.zeros_like(v2))
                qm = jnp.where(tile_half, q2, jnp.zeros_like(q2))
                dom = jnp.where(tile_half, do2, jnp.zeros_like(do2))
                head = 2 * g + hh
                s = dot_nt(km, q2) + bias
                pr = jnp.exp(s - lse_t[head : head + 1, at])
                dp = dot_nt(vm, do2)
                delta = jnp.sum(pr * dp, 0, keepdims=True)
                ds = (pr * (dp - delta)).astype(bf16)
                got_v = dot_nn(pr.astype(bf16), dom)
                got_k = dot_nn(ds, qm)
                got_q = dot_nn(jnp.transpose(km), ds)
                dv = got_v if dv is None else dv + got_v
                dk = got_k if dk is None else dk + got_k
                dq = got_q if dq is None else dq + got_q
            dqr = jnp.transpose(dq)
            d4[0, at, cs] = dqr.astype(bf16)
        dkr = (dk * scale).astype(bf16)
        dvr = dv.astype(bf16)
        d4[1, :, cs] = dkr
        d4[2, :, cs] = dvr
    wide = d4.shape[2]
    small[3:4, 0:wide] = jnp.sum(d4[0].astype(f32), 0, keepdims=True)
    small[3:4, wide : 2 * wide] = jnp.sum(d4[2].astype(f32), 0, keepdims=True)
    for i in range(seq // rows):
        at = pl.ds(i * rows, rows)
        acc = dot_nn(d4[0, at], w[0]) + dot_nn(d4[1, at], w[1]) + dot_nn(d4[2, at], w[2])
        dx_low[at] = acc.astype(bf16)


def attn_bwd(layer, scal, dz2, h_mine, h_theirs, normed, recip, gain, qkv, lse_t, o, seg_row, seg_col, own_qkv, own_out, a_refs, b_refs):
    seq, width = dz2.shape
    wide = qkv.shape[2]
    return pl.pallas_call(
        functools.partial(attn_bwd_kernel, layer),
        out_shape=[
            shape((seq, width), f32),
            shape((seq, width), bf16),
            shape((4, seq, wide), bf16),
            shape((seq, width), bf16),
            shape((8, width), f32),
        ],
        in_specs=[SMEM] + [VMEM] * 11 + [ANY] * 10,
        out_specs=[VMEM] * 5,
        scratch_shapes=[
            pltpu.VMEM((4, wide, width), bf16),
            pltpu.VMEM((seq, seq), f32),
            pltpu.VMEM((seq, wide), bf16),
            pltpu.SemaphoreType.DMA((8,)),
        ],
        compiler_params=params(),
        cost_estimate=cost(14),
        name="attn_bwd",
    )(scal, dz2, h_mine, h_theirs, normed, recip, gain, qkv, lse_t, o, seg_row, seg_col, own_qkv, own_out, *a_refs, *b_refs)


def attn_dw_kernel(scal, d4, xr, dzr1, *outs):
    place = scal[1]
    cols = d4.shape[2] // 2
    for j in range(4):
        t = j ^ place
        right = jnp.where(t == 3, dzr1[...], xr[...])
        got = dot_tn(d4[t], right).astype(bf16)
        for s in range(SLOTS):
            send, nxt, keep = outs[3 * s : 3 * s + 3]
            val = got[s * cols : (s + 1) * cols]
            if j in SEND[s]:
                send[SEND[s].index(j), 0] = val
            elif j == NEXT[s]:
                nxt[0] = val
            else:
                keep[0] = val


def attn_dw(scal, d4, xr, dzr1):
    cols, width = d4.shape[2] // 2, xr.shape[1]
    outs = [shape((2, 1, cols, width), bf16), shape((1, cols, width), bf16), shape((1, cols, width), bf16)] * 2
    return pl.pallas_call(
        attn_dw_kernel,
        out_shape=outs,
        in_specs=[SMEM] + [VMEM] * 3,
        out_specs=[VMEM] * 6,
        compiler_params=params(),
        cost_estimate=cost(4.5),
        name="attn_dw",
    )(scal, d4, xr, dzr1)


def low_sum(*parts):
    total = parts[0].astype(f32)
    for v in parts[1:]:
        total = total + v.astype(f32)
    return total.astype(bf16)


def piece_call(kernel, outs, us, name, scal, *ins):
    specs, args = [], []
    for v in ins:
        if isinstance(v, tuple):
            v, at = v
            n = v.ndim
            specs.append(pl.BlockSpec((1,) + v.shape[1:], lambda i, at=at, n=n: (at,) + (0,) * (n - 1)))
        else:
            n = v.ndim
            specs.append(pl.BlockSpec(v.shape, lambda i, n=n: (0,) * n))
        args.append(v)
    return pl.pallas_call(
        kernel,
        grid=(1,),
        out_shape=outs,
        in_specs=[SMEM] + specs,
        out_specs=[pl.BlockSpec(v.shape, lambda i, n=len(v.shape): (0,) * n) for v in outs],
        compiler_params=params(),
        cost_estimate=cost(us),
        name=name,
    )(scal, *args)


def add2_kernel(scal, nxt_a, got_a, nxt_b, got_b, out_a, out_b):
    out_a[...] = low_sum(nxt_a[...], got_a[0])
    out_b[...] = low_sum(nxt_b[...], got_b[0])


def sum_kernel(scal, keep_a, got_a, more_a, keep_b, got_b, more_b, out_a, out_b):
    out_a[...] = low_sum(keep_a[...], got_a[0], more_a[...])
    out_b[...] = low_sum(keep_b[...], got_b[0], more_b[...])


def quarter_sum_kernel(scal, keep_a, got_a, more_a, keep_b, got_b, more_b, out):
    n_t = out.shape[0]
    for k in range(n_t):
        q = lax.rem(scal[3] + n_t - k, n_t)
        out[q, 0] = low_sum(keep_a[k], got_a[0, k], more_a[k])
        out[q, 1] = low_sum(keep_b[k], got_b[0, k], more_b[k])


def pick_kernel(scal, every, out, ub):
    n_t, rows = every.shape[0], out.shape[2]
    for k in range(n_t):
        q = lax.rem(scal[3] + n_t - k, n_t)
        ub[k : k + 1] = jnp.sum(every[q, 2 * rows : 2 * rows + 3].astype(f32), 0, keepdims=True)
        if k:
            for n in range(2):
                out[n, k - 1] = every[q, n * rows : (n + 1) * rows]


def pick(scal, every, rows):
    n_t, _, half = every.shape
    return pl.pallas_call(
        pick_kernel,
        out_shape=[shape((2, n_t - 1, rows, half), bf16), shape((n_t, half), f32)],
        in_specs=[SMEM, VMEM],
        out_specs=[VMEM, VMEM],
        compiler_params=params(),
        cost_estimate=cost(1.5),
        name="pick_quarters",
    )(scal, every)


def split_kernel(scal, every, *outs):
    place = scal[1]
    for s in range(SLOTS):
        send, nxt, keep = outs[3 * s : 3 * s + 3]
        for j in range(4):
            val = every[j ^ place, s]
            if j in SEND[s]:
                send[SEND[s].index(j), 0] = val
            elif j == NEXT[s]:
                nxt[0] = val
            else:
                keep[0] = val


def split_pieces(scal, every):
    _, _, rows, half = every.shape
    one = (1, rows, half)
    outs = [shape((2,) + one, bf16), shape(one, bf16), shape(one, bf16)] * 2
    return piece_call(split_kernel, outs, 1.5, "split_pieces", scal, every)


def tot_kernel(scal, a, moved_a, moved_b, out):
    @pl.when(scal[0] == 0)
    def _():
        out[...] = low_sum(a[...], moved_b[...])

    @pl.when(scal[0] != 0)
    def _():
        out[...] = low_sum(moved_a[...], moved_b[...])


def fin_kernel(scal, mine, theirs, out, half):
    rows = half.shape[1]
    out[...] = low_sum(mine[...], theirs[...])
    at = pl.ds(pl.multiple_of(scal[0] * rows, rows), rows)
    half[...] = out[:, at]


def halves(scal, mine, theirs):
    core = scal[0]
    rows = mine[0].shape[1]
    for j in range(1, 4):
        for ref, c in ((mine[j - 1], core), (theirs[j - 1], 1 - core)):
            yield j ^ scal[1], pl.multiple_of(c * rows, rows), rows, ref


def ff_out_kernel(n_alias, scal, mine, theirs, *refs):
    up, down = refs[n_alias:]
    _, _, part, half = mine.shape
    rows = half // 4
    for ref, c in ((mine, scal[0]), (theirs, 1 - scal[0])):
        off = pl.multiple_of(c * half, half)
        for p in range(4):
            up[0, pl.ds(p * part, part), pl.ds(off, half)] = ref[p, 0].astype(f32)
            at = pl.ds(pl.multiple_of(off + p * rows, rows), rows)
            for n in range(2):
                down[0, at, pl.ds(n * half, half)] = ref[p, 1, pl.ds(n * rows, rows)].astype(f32)


def attn_out_kernel(n_alias, scal, full, *refs):
    mine, theirs = refs[:3], refs[3:6]
    qkv, out = refs[6 + n_alias :]
    parts = [(scal[1], 0, full.shape[1], full)] + list(halves(scal, mine, theirs))
    for t, off, rows, ref in parts:
        val = ref[0].astype(f32)

        @pl.when(t < 3)
        def _(t=t, off=off, rows=rows, val=val):
            qkv[0, jnp.minimum(t, 2), pl.ds(off, rows)] = val

        @pl.when(t == 3)
        def _(off=off, rows=rows, val=val):
            out[0, pl.ds(off, rows)] = val


def out_call(kernel, name, layer, dims, scal, ins, before):
    whole = lambda v: pl.BlockSpec(v.shape, lambda i: (0,) * v.ndim)
    before = list(before or [])
    return pl.pallas_call(
        functools.partial(kernel, len(before)),
        grid=(1,),
        out_shape=[shape(d, f32) for d in dims],
        in_specs=[SMEM] + [whole(v) for v in ins] + [ANY] * len(before),
        out_specs=[pl.BlockSpec((1,) + d[1:], lambda i, n=len(d): (layer,) + (0,) * (n - 1)) for d in dims],
        input_output_aliases={1 + len(ins) + i: i for i in range(len(before))},
        compiler_params=params(),
        cost_estimate=cost(3),
        name=name,
    )(scal, *ins, *before)


def after(v, *others):
    return lax.optimization_barrier((v, *others))[0]


def local(
    block_input,
    w_qkv,
    qv_bias,
    w_out,
    out_bias,
    w_up,
    up_bias,
    w_down,
    norm_gain,
    norm_shift,
    segment_ids,
    slot_counts,
    cotangent,
):
    layers, width, _, cols = w_qkv.shape
    hidden = w_up.shape[2]
    seq = segment_ids.shape[1]
    n_dp, n_t = lax.axis_size("dp"), lax.axis_size("tensor")
    dp, z = lax.axis_index("dp"), lax.axis_index("tensor")
    core, place = dp & 1, (dp >> 1) & 3
    first = core == 0
    part = hidden // 4
    norms_in = (out_bias, norm_gain, norm_shift)

    def flip(v, bits, odd=False):
        pairs = [(i, i ^ bits) for i in range(n_dp) if not odd or i & 1]
        return lax.ppermute(v, "dp", pairs)

    def across(v):
        return flip(v, 1)

    def shift(v, by):
        pairs = []
        for i in range(n_dp):
            move = by[i & 1]
            if move:
                pairs += [(i * n_t + k, i * n_t + (k + move) % n_t) for k in range(n_t)]
        return lax.ppermute(v, ("dp", "tensor"), pairs)

    def rotate(v, by):
        return lax.ppermute(v, "tensor", [(i, (i + by) % n_t) for i in range(n_t)])

    def swap(v):
        pairs = []
        for i in range(n_dp):
            for k in range(n_t):
                if (i & 1) != (k & 1):
                    pairs.append((i * n_t + k, (i ^ 1) * n_t + (k ^ 1)))
        moved = lax.ppermute(v, ("dp", "tensor"), pairs)
        return jnp.where(core == (z & 1), v, moved)

    own_qkv = jnp.transpose(w_qkv, (0, 2, 3, 1))

    def attn_piece(l):
        qkv_piece = lax.dynamic_index_in_dim(own_qkv[l], jnp.minimum(place, 2), 0, False)
        return jnp.where(place == 3, w_out[l], qkv_piece)

    half = hidden // 2

    def ff_piece(l):
        up_piece = lax.dynamic_slice(w_up[l], (place * part, core * half), (part, half))
        down_piece = lax.dynamic_slice_in_dim(w_down[l], core * half + place * (half // 4), half // 4, 0)
        return jnp.concatenate([up_piece, down_piece[:, :half], down_piece[:, half:], up_packed[l]], 0)

    def ff_over_xy(every):
        own, ub = pick(scal, every, part)
        x, y = flip(own, 2), flip(own, 4)
        return (own, x, y, flip(x[0], 4), flip(y[1], 2)), ub

    def over_z(piece):
        return shift(piece, (1, 2)), shift(piece, (0, 3))

    def over_xy(b, a):
        bx = flip(b, 2)
        by = flip(b, 4)
        ay = flip(a, 4, True)
        ax = flip(a, 2, True)
        bd = flip(bx, 4)
        ad = flip(ay, 2, True)
        return (a, ax, ay, ad), (b, bx, by, bd)

    packed = jnp.concatenate([segment_ids, jnp.broadcast_to(slot_counts[:, None], (segment_ids.shape[0], 128))], 1)
    packed = jnp.where(core == (z & 1), packed, across(packed))
    packed = lax.dynamic_index_in_dim(packed, z >> 1, 0, False)
    segments, slot_count = packed[:seq], packed[seq]
    seg_row, seg_col = segments[None, :], segments[:, None]
    scal = jnp.stack([core, place, slot_count, z]).astype(jnp.int32)
    own_bias = qv_bias.reshape(1, -1)
    up_packed, qv_packed = pack_bias(jnp.stack([core, place]).astype(jnp.int32), up_bias, own_bias)
    piece = jnp.concatenate([attn_piece(0), qv_packed], 0)
    z_moved = [over_z(piece)]
    x_mine = swap(block_input)
    x_theirs = across(x_mine)
    ff_every = []
    for l in range(layers):
        if l:
            z_moved.append(over_z(after(attn_piece(l), ff_every[-1])))
        piece = ff_piece(l) if l == 0 else after(ff_piece(l), ff_every[-1])
        ff_every.append(lax.all_gather(piece, "tensor", axis=0))
    attn_w = [over_xy(*m) for m in z_moved]
    bias = (own_bias,) + z_moved[0][::-1]
    ff_w, ub = zip(*[ff_over_xy(e) for e in ff_every])

    rows_in = (x_mine, x_theirs)
    saved = []
    for l in range(layers):
        rows_in = (after(rows_in[0], ff_w[l][0]),) + rows_in[1:]
        state, xr, n2, r2, qkv, lse_t, o, a_low = attn_fwd(
            l, scal, rows_in, seg_row, seg_col, bias, own_qkv, w_out, *attn_w[l]
        )
        if l:
            saved[l - 1] += (n2, r2)
        if l + 1 < layers:
            state = after(state, *z_moved[l + 1])
        h, hr, n1, r1, g, gp, f_low = ff_fwd(
            l, scal, state, a_low, across(a_low), norms_in, ub[l], w_up, w_down, ff_w[l]
        )
        saved.append((xr, qkv, lse_t, o, hr, n1, r1, g, gp))
        rows_in = (h, f_low, across(f_low)) + norms_in

    class Chunk:
        def __init__(self, pieces):
            self.pieces = pieces
            self.got = (flip(pieces[0], 4), flip(pieces[3], 2))

        def second(self, *late):
            p, got = self.pieces, self.got
            nxt = after(p[1], *late)
            outs = [shape(nxt.shape, bf16)] * 2
            self.sec = piece_call(add2_kernel, outs, 1.2, "add_second", scal, nxt, (got[0], 1), p[4], (got[1], 1))
            self.more = (flip(self.sec[0], 2), flip(self.sec[1], 4))
            return self

        def plain_third(self, *late):
            p, got, more = self.pieces, self.got, self.more
            keep = after(p[2], *late)
            outs = [shape(keep.shape, bf16)] * 2
            self.sums = piece_call(
                sum_kernel, outs, 1.5, "add_third", scal, keep, (got[0], 0), more[0], p[5], (got[1], 0), more[1]
            )
            return self.sums

        def third(self, *late):
            a, b = self.plain_third(*late)
            self.moved = (shift(a, (0, n_t - 3)), shift(b, (n_t - 1, n_t - 2)))
            return self

        def fourth(self, *late):
            a = after(self.sums[0], *late)
            (total,) = piece_call(tot_kernel, [shape(a.shape, bf16)], 1.2, "add_fourth", scal, a, *self.moved)
            bits = 8
            while bits < n_dp:
                total = low_sum(total, flip(total, bits))
                bits *= 2
            self.total = total
            self.other = across(total)
            return self

        def fifth(self, *late):
            total = after(self.total, *late)
            n, rows, wide = total.shape
            outs = [shape(total.shape, bf16), shape((n, rows // 2, wide), bf16)]
            self.full, half = piece_call(fin_kernel, outs, 1.2, "add_fifth", scal, total, self.other)
            self.half = half
            self.mine = [flip(half, bits) for bits in (2, 4, 6)]
            self.theirs = [across(v) for v in self.mine]
            return self

    class FFChunk(Chunk):
        def __init__(self, pieces):
            self.z_first = len(pieces) == 1
            if self.z_first:
                self.total = lax.psum_scatter(pieces[0], "tensor", scatter_dimension=0, tiled=False)
            else:
                super().__init__(pieces)

        def split(self, *late):
            super().__init__(split_pieces(scal, after(self.total, *late)))
            return self

        def third(self, *late):
            if self.z_first:
                super_sums = self.plain_third(*late)
                self.total = jnp.concatenate(super_sums, 0)
                return self
            p, got, more = self.pieces, self.got, self.more
            keep = after(p[2], *late)
            n, rows, wide = keep.shape
            (self.sums,) = piece_call(
                quarter_sum_kernel,
                [shape((n, 2, rows, wide), bf16)],
                1.5,
                "add_quarters",
                scal,
                keep,
                (got[0], 0),
                more[0],
                p[5],
                (got[1], 0),
                more[1],
            )
            self.total = lax.psum_scatter(self.sums, "tensor", scatter_dimension=0, tiled=False)
            self.sums = (self.sums,)
            return self

        def fourth(self, *late):
            total = after(self.total, *late)
            bits = 8
            while bits < n_dp:
                total = low_sum(total, flip(total, bits))
                bits *= 2
            groups = [[i | j for j in (0, 2, 4, 6)] for i in range(n_dp) if not i & 6]
            self.mine = lax.all_gather(total, "dp", axis=0, axis_index_groups=groups)
            self.theirs = across(self.mine)
            return self

    chunks, smalls = [], []
    for l in reversed(range(layers)):
        last = l == layers - 1
        xr, qkv, lse_t, o, hr, n1, r1, g, gp = saved[l][:9]
        if last:
            c_mine = swap(cotangent)
            ff_rows = rows_in[:3] + (c_mine, across(c_mine))
        else:
            ff_rows = (dz1, dx_low, across(dx_low)) + saved[l][9:]
        got = ff_bwd(l, scal, ff_rows, norms_in, gp, w_up, w_down, ff_w[l], last)
        if last:
            out_low = got[0]
            got = got[1:]
        dz2, dzr2, du, dh_low, small2, ub_sum = got
        ff_pieces = ff_dw(scal, g, du, hr, dzr2, last)
        ff = FFChunk(ff_pieces)
        dh_theirs = across(dh_low)
        if chunks:
            chunks[1].second(ff_pieces[0])
            dz2 = after(dz2, *chunks[1].sec)
        dz2 = after(dz2, ff_pieces[0])
        dz1, dzr1, d4, dx_low, small1 = attn_bwd(
            l, scal, dz2, dh_low, dh_theirs, n1, r1, norm_gain, qkv, lse_t, o, seg_row, seg_col, own_qkv, w_out, *attn_w[l]
        )
        if chunks:
            chunks[1].third(dx_low)
            xr = after(xr, *chunks[1].sums)
        at_pieces = attn_dw(scal, d4, xr, dzr1)
        at = Chunk(at_pieces)
        dz1 = after(dz1, at_pieces[0])
        chunks += [ff, at]
        smalls.append((small1, small2, ub_sum))
    smalls = smalls[::-1]

    f1, a1, f0, a0 = chunks
    f0.second(at_pieces[2])
    a1.fourth(*f0.sec)
    a1.fifth()
    a0.second(a1.full)
    f0.third(*a0.sec)
    f1.split(*f0.sums)
    a0.third(f1.pieces[0])
    f1.second(*a0.sums)
    f1.third(*f1.sec)
    a0.fourth(*f1.sums)
    a0.fifth()
    f1.fourth(a0.full)
    f0.fourth(f1.mine)
    ff_dims = [(layers, width, hidden), (layers, hidden, width)]
    at_dims = [(layers, 3, cols, width), (layers, cols, width)]

    def ff_finish(l, c, before):
        return out_call(ff_out_kernel, "ff_out", l, ff_dims, scal, [c.mine, c.theirs], before)

    def at_finish(l, c, before):
        return out_call(attn_out_kernel, "attn_out", l, at_dims, scal, [c.full, *c.mine, *c.theirs], before)

    ff_out = ff_finish(0, f0, ff_finish(1, f1, None))
    at_out = at_finish(0, a0, at_finish(1, a1, None))

    out_half = lax.dynamic_slice_in_dim(out_low, core * (seq // 2), seq // 2, 0)
    mixed = swap(out_half)
    dx = dz1 + (dx_low.astype(f32) + across(dx_low).astype(f32))
    input_grad = swap(lax.dynamic_slice_in_dim(dx, core * (seq // 2), seq // 2, 0))

    once = jnp.where(first, 1.0, 0.0).astype(f32)
    norms = jnp.stack([jnp.concatenate([g[0][:3], g[1][:3]]) for g in smalls]) * once
    quarters = jnp.where(first, jnp.stack([z, z + n_t - 1]), jnp.stack([z + 1, z + 2])) % n_t
    spread = (quarters[:, None] == jnp.arange(n_t)[None]).astype(f32)
    qv_slots = jnp.stack([g[0][3].reshape(2, SLOTS, cols).transpose(1, 0, 2).reshape(SLOTS, -1) for g in smalls])
    qv_placed = jnp.sum(qv_slots[:, :, None] * spread[None, :, :, None], 1)
    ub_quarters = (z + n_t - jnp.arange(n_t)) % n_t
    ub_placed = jnp.take(jnp.stack([g[2] for g in smalls]), ub_quarters, axis=1)
    ub_placed = jnp.where(
        first,
        jnp.concatenate([ub_placed, jnp.zeros_like(ub_placed)], 2),
        jnp.concatenate([jnp.zeros_like(ub_placed), ub_placed], 2),
    )
    placed = jnp.concatenate([ub_placed, qv_placed], 2)
    flat = jnp.concatenate([norms.reshape(-1), placed.reshape(-1)]).reshape(-1, 128)
    bits = 1
    while bits < n_dp:
        flat = flat + flip(flat, bits)
        bits *= 2
    bits = 1
    while bits < n_t:
        flat = flat + lax.ppermute(flat, "tensor", [(i, i ^ bits) for i in range(n_t)])
        bits *= 2
    flat = flat.reshape(-1)
    norms = flat[: norms.size].reshape(layers, 2, 3, width)
    placed = lax.dynamic_index_in_dim(flat[norms.size :].reshape(placed.shape), z, 1, False)
    return (
        mixed,
        input_grad,
        jnp.transpose(at_out[0], (0, 3, 1, 2)),
        placed[:, hidden:].reshape(layers, 2, cols),
        at_out[1],
        norms[:, :, 2],
        ff_out[0],
        placed[:, :hidden],
        ff_out[1],
        norms[:, :, 0],
        norms[:, :, 1],
    )


def solution(mesh):
    placed = (
        P(("dp", "tensor"), None),
        P(None, None, None, "tensor"),
        P(None, None, "tensor"),
        P(None, "tensor", None),
        P(),
        P(None, None, "tensor"),
        P(None, "tensor"),
        P(None, "tensor", None),
        P(),
        P(),
        P("dp", None),
        P("dp"),
        P(("dp", "tensor"), None),
    )
    return jax.shard_map(
        local,
        mesh=mesh,
        in_specs=placed,
        out_specs=(
            P(("dp", "tensor"), None),
            P(("dp", "tensor"), None),
            P(None, None, None, "tensor"),
            P(None, None, "tensor"),
            P(None, "tensor", None),
            P(),
            P(None, None, "tensor"),
            P(None, "tensor"),
            P(None, "tensor", None),
            P(),
            P(),
        ),
        check_vma=False,
    )
```

time: 667 us -> 484 us (0.73)
  Pallas kernels: 0 us -> 169 us
  other arithmetic: 118 us -> 7.98 us
  matrix products: 86 us -> 0 us
  local copies, waits for them, and re-layouts: 108 us -> 36.1 us
  waiting for transfers between devices: 178 us -> 125 us
  blocking collectives: 21.7 us -> 0 us
  starting transfers between devices: 144 us -> 123 us
  between operations: 4.1 us -> 15.6 us
    pallas_call x0 -> x32, Pallas kernels: none -> 169 us  [the longest x13 29.6 us: piece_call(): pl.pallas_call(kernel, grid=(1,), out_shape=outs, in_specs=[SMEM] + specs...]
    dot_general x38 -> x0, matrix products: 86 us -> none  [the longest x8 31.3 us: dot_nt(): lax.dot_general(left, right, (((1,), (1,)), ((), ())), preferred_element_...]
    ppermute x97 -> x76, waiting for transfers between devices: 178 us -> 99.6 us  [the longest x66 74 us: flip(): return lax.ppermute(v, 'dp', pairs)]
    select_n x24 -> x6, other arithmetic: 26.6 us -> 0.26 us  [the longest x2 0.09 us: local(): ub_placed = jnp.take(jnp.stack([g[2] for g in smalls]), ub_quarters, axis=1)]
    gather x17 -> x1, local copies, waits for them, and re-layouts: 25.8 us -> 0.58 us  [local(): ub_placed = jnp.take(jnp.stack([g[2] for g in smalls]), ub_quarters, axis=1)]
    all_gather x0 -> x4, waiting for transfers between devices: none -> 24.9 us  [the longest x2 24.9 us: fourth(): self.mine = lax.all_gather(total, 'dp', axis=0, axis_index_groups=groups)]
    convert_element_type x25 -> x1, other arithmetic: 22.9 us -> 0.07 us  [local(): spread = (quarters[:, None] == jnp.arange(n_t)[None]).astype(f32)]
    all_gather x1 -> x0, blocking collectives: 21.7 us -> none  [local(): small = lax.all_gather(small, 'tensor', axis=0)]
  transfers between devices with their start and end apart: 101 -> 86, of which waited for: 40 -> 31; matrix products, arithmetic and copies ran while one was open for 42% -> 3% of each run, Pallas kernels for 0% -> 31%
where the time goes in v2:
time: 484 us; the launch traced here: 477 us
  Pallas kernels  169 us (35%)
  waiting for transfers between devices  125 us (26%)
  starting transfers between devices  123 us (25%)
  local copies, waits for them, and re-layouts  36.1 us (7%)
  between operations  15.6 us (3%)
  other arithmetic  7.98 us (2%)
    ppermute x66, starting transfers between devices, flip(): return lax.ppermute(v, 'dp', pairs)  93.1 us
    ppermute x66, waiting for transfers between devices, flip(): return lax.ppermute(v, 'dp', pairs)  74 us
    pallas_call x13, Pallas kernels, piece_call(): pl.pallas_call(kernel, grid=(1,), out_shape=outs, in_specs=[SMEM] + specs...  29.6 us
    pallas_call x2, Pallas kernels, attn_bwd(): pl.pallas_call(functools.partial(attn_bwd_kernel, layer), out_shape=[shap...  28 us
    pallas_call x2, Pallas kernels, attn_fwd(): pl.pallas_call(functools.partial(attn_fwd_kernel, layer), out_shape=outs,...  25.5 us
    all_gather x2, waiting for transfers between devices, fourth(): self.mine = lax.all_gather(total, 'dp', axis=0, axis_index_groups=groups)  24.9 us
    ppermute x8, waiting for transfers between devices, shift(): return lax.ppermute(v, ('dp', 'tensor'), pairs)  23.3 us
    pallas_call x2, Pallas kernels, ff_bwd(): pl.pallas_call(functools.partial(ff_bwd_kernel, last, layer), grid=(seq /...  22.5 us
  transfers between devices with their start and end apart: 86, of which 31 were waited for; matrix products, arithmetic and copies ran while one was open for 3% of the time, Pallas kernels for 31%

profile of v2, /device:TPU:0, one launch (start us, length us, event | category | flops | bytes accessed | tf_op | source)
XLA Modules:
  0.0 476.6 jit_solution(15944465150822316640)
XLA Ops:
  7.2 2.9 fusion.6
  20.1 3.1 collective-permute-start.4
  25.3 3.4 collective-permute-start
  28.7 4.9 %collective-permute-done.4.refs_7_.refs_14_.refs_11_.refs_4_ = bf16[208,768]{1,0:T(8,128)(2,1)S(1)} collective-permute-done((bf16[208,768]{1,0:T(8,128)(2,1)S(1)}, bf16[208,768]{1,0:T(8,128)(2,1)S(1)}, u32[]{:S(2)}, u32[]{:S(2)}) %collective-permute-start.4) | collective-permute-done | bytes 319520 | tf_op jit(solution)/shard_map/ppermute | solution.py:885
  39.7 19.7 %collective-permute-start.2 = (bf16[256,768]{1,0:T(8,128)(2,1)S(1)}, bf16[256,768]{1,0:T(8,128)(2,1)S(1)}, u32[]{:S(2)}, u32[]{:S(2)}) collective-permute-start(bf16[256,768]{1,0:T(8,128)(2,1)S(1)} %broadcast_select_fusion.3.refs_1_), channel_id=1, source_target_pairs={{0,4},{4,0},{8,12},{12,8},{16,20},{20,16},{24,28},{28,24},{1,5},{5... | collective-permute-start | bytes 1179656 | tf_op jit(solution)/shard_map/ppermute | solution.py:874
  70.9 12.2 %attn_fwd.2 = (f32[512,768]{1,0:T(8,128)}, bf16[512,768]{1,0:T(8,128)(2,1)}, bf16[3,512,384]{2,1,0:T(8,128)(2,1)}, f32[8,512]{1,0:T(8,128)}, bf16[512,384]{1,0:T(8,128)(2,1)}, /*index=5*/bf16[512,768]{1,0:T(8,128)(2,1)}) custom-call(s32[4]{0:T(128)} %pad_add_fusion.1.scal.refs_0_, bf16[256,768]{1,0:T(8,128)(2,1)} %copy-done.8, bf16[256,768]{1,0:T(8,128)(2,1)} %copy-done.48, ...), custom_call_target="tpu_custom_call" | custom-call | flops 13200000000 | bytes 43200000 | tf_op jit(solution)/shard_map/attn_fwd/pallas_call | solution.py:288
  83.2 7.2 %collective-permute-done.14.refs_1_.refs_12_ = bf16[2,3,192,384]{3,2,1,0:T(8,128)(2,1)S(1)} collective-permute-done((bf16[2,3,192,384]{3,2,1,0:T(8,128)(2,1)}, bf16[2,3,192,384]{3,2,1,0:T(8,128)(2,1)S(1)}, u32[]{:S(2)}, u32[]{:S(2)}) %collective-permute-start.14) | collective-permute-done | bytes 884768 | tf_op jit(solution)/shard_map/ppermute | solution.py:874
  95.1 9.6 %collective-permute-done.11.refs_18_.refs_4_ = bf16[192,768]{1,0:T(8,128)(2,1)S(1)} collective-permute-done((bf16[192,768]{1,0:T(8,128)(2,1)S(1)}, bf16[192,768]{1,0:T(8,128)(2,1)S(1)}, u32[]{:S(2)}, u32[]{:S(2)}) %collective-permute-start.11) | collective-permute-done | bytes 294944 | tf_op jit(solution)/shard_map/ppermute | solution.py:885
  104.6 10.3 %ff_fwd.2 = (f32[512,768]{1,0:T(8,128)}, bf16[512,768]{1,0:T(8,128)(2,1)}, f32[512,768]{1,0:T(8,128)}, f32[512,1]{1,0:T(8,128)}, bf16[4,512,384]{2,1,0:T(8,128)(...) custom-call(s32[4]{0:T(128)} %pad_add_fusion.1.scal.refs_0_, f32[512,768]{1,0:T(8,128)} %get-tuple-element.148.state, ...), custom_call_target="tpu_custom_call" | custom-call | flops 12099999744 | bytes 39600000 | tf_op jit(solution)/shard_map/ff_fwd/pallas_call | solution.py:353
  114.9 3.2 collective-permute-start.18
  120.8 7.6 %collective-permute-done.22.refs_19_.refs_5_ = bf16[192,768]{1,0:T(8,128)(2,1)S(1)} collective-permute-done((bf16[192,768]{1,0:T(8,128)(2,1)S(1)}, bf16[192,768]{1,0:T(8,128)(2,1)S(1)}, u32[]{:S(2)}, u32[]{:S(2)}) %collective-permute-start.22) | collective-permute-done | bytes 294944 | tf_op jit(solution)/shard_map/ppermute | solution.py:874
  128.5 2.4 pick_quarters.3
  133.4 3.4 collective-permute-done.24.refs_21_.refs_7_
  138.4 13.3 %attn_fwd.3 = (f32[512,768]{1,0:T(8,128)}, bf16[512,768]{1,0:T(8,128)(2,1)}, f32[512,768]{1,0:T(8,128)}, f32[512,1]{1,0:T(8,128)}, bf16[3,512,384]{2,1,0:T(8,128...) custom-call(s32[4]{0:T(128)} %pad_add_fusion.1.scal.refs_0_, ...), custom_call_target="tpu_custom_call" | custom-call | flops 13200000000 | bytes 43200000 | tf_op jit(solution)/shard_map/attn_fwd/pallas_call | solution.py:288
  151.7 3.8 collective-permute-start.25
  157.6 10.2 %collective-permute-done.28.refs_3_.refs_14_ = bf16[3,192,384]{2,1,0:T(8,128)(2,1)S(1)} collective-permute-done((bf16[3,192,384]{2,1,0:T(8,128)(2,1)S(1)}, bf16[3,192,384]{2,1,0:T(8,128)(2,1)S(1)}, u32[]{:S(2)}, u32[]{:S(2)}) %collective-permute-start.28) | collective-permute-done | bytes 442400 | tf_op jit(solution)/shard_map/ppermute | solution.py:874
  169.1 10.2 %ff_fwd.3 = (f32[512,768]{1,0:T(8,128)}, bf16[512,768]{1,0:T(8,128)(2,1)}, f32[512,768]{1,0:T(8,128)}, f32[512,1]{1,0:T(8,128)}, bf16[4,512,384]{2,1,0:T(8,128)(...) custom-call(s32[4]{0:T(128)} %pad_add_fusion.1.scal.refs_0_, f32[512,768]{1,0:T(8,128)} %get-tuple-element.156.state, ...), custom_call_target="tpu_custom_call" | custom-call | flops 12099999744 | bytes 39600000 | tf_op jit(solution)/shard_map/ff_fwd/pallas_call | solution.py:353
  183.3 11.1 %ff_bwd.2 = (bf16[512,768]{1,0:T(8,128)(2,1)}, f32[512,768]{1,0:T(8,128)}, bf16[512,768]{1,0:T(8,128)(2,1)}, bf16[4,512,384]{2,1,0:T(8,128)(2,1)}, bf16[512,768]...) custom-call(s32[4]{0:T(128)} %pad_add_fusion.1.scal.refs_0_, f32[512,768]{1,0:T(8,128)} %get-tuple-element.159.refs_0_, ...), custom_call_target="tpu_custom_call" | custom-call | flops 12099999744 | bytes 39600000 | tf_op jit(solution)/shard_map/ff_bwd/pallas_call | solution.py:453
  194.4 6.6 %ff_dw.2 = bf16[4,4,2,192,384]{4,3,2,1,0:T(8,128)(2,1)} custom-call(s32[4]{0:T(128)} %pad_add_fusion.1.scal.refs_0_, bf16[4,512,384]{2,1,0:T(8,128)(2,1)} %get-tuple-element.164.g, bf16[4,512,384]{2,1,0:T(8,128)(2,1)} %get-tuple-element.165.du, bf16[512,768]{1,0:T(8,128)(2,1)} %get-tuple-element.166.hr, bf16[512,768]{1,0:T(8,128)(2,1)} %get-tuple-element.167.dzr2), custom_call_target="tpu_custom_call" | custom-call | flops 6600000000 | bytes 21600000 | tf_op jit(solution)/shard_map/ff_dw/pallas_call | solution.py:529
  205.4 13.9 %attn_bwd.2 = (f32[512,768]{1,0:T(8,128)}, bf16[512,768]{1,0:T(8,128)(2,1)}, bf16[4,512,384]{2,1,0:T(8,128)(2,1)}, bf16[512,768]{1,0:T(8,128)(2,1)}, f32[8,768]{1,0:T(8,128)}) custom-call(s32[4]{0:T(128)} %pad_add_fusion.1.scal.refs_0_, f32[512,768]{1,0:T(8,128)} %get-tuple-element.168.dz2, bf16[512,768]{1,0:T(8,128)(2,1)} %get-tuple-element.169.h_mine, ...), custom_call_target="tpu_custom_call" | custom-call | flops 15399999488 | bytes 50400000 | tf_op jit(solution)/shard_map/attn_bwd/pallas_call | solution.py:626
  219.7 4.4 attn_dw.2
  225.0 11.4 %ff_bwd.3 = (f32[512,768]{1,0:T(8,128)}, bf16[512,768]{1,0:T(8,128)(2,1)}, bf16[4,512,384]{2,1,0:T(8,128)(2,1)}, bf16[512,768]{1,0:T(8,128)(2,1)}, f32[8,768]{1,0:T(8,128)}, /*index=5*/f32[4,384]{1,0:T(4,128)}) custom-call(s32[4]{0:T(128)} %pad_add_fusion.1.scal.refs_0_, f32[512,768]{1,0:T(8,128)} %get-tuple-element.180.refs_0_, ...), custom_call_target="tpu_custom_call" | custom-call | flops 12099999744 | bytes 39600000 | tf_op jit(solution)/shard_map/ff_bwd/pallas_call | solution.py:453
  238.7 7.2 %ff_dw.3 = (bf16[2,4,192,384]{3,2,1,0:T(8,128)(2,1)}, bf16[4,192,384]{2,1,0:T(8,128)(2,1)}, bf16[4,192,384]{2,1,0:T(8,128)(2,1)}, bf16[2,4,192,384]{3,2,1,0:T(8,...) custom-call(s32[4]{0:T(128)} %pad_add_fusion.1.scal.refs_0_, ...), custom_call_target="tpu_custom_call" | custom-call | flops 6600000000 | bytes 21600000 | tf_op jit(solution)/shard_map/ff_dw/pallas_call | solution.py:529
  246.8 6.1 %collective-permute-done.36.got_a = bf16[2,1,192,768]{3,2,1,0:T(8,128)(2,1)S(1)} collective-permute-done((bf16[2,1,192,768]{3,2,1,0:T(8,128)(2,1)S(1)}, bf16[2,1,192,768]{3,2,1,0:T(8,128)(2,1)S(1)}, u32[]{:S(2)}, u32[]{:S(2)}) %collective-permute-start.36) | collective-permute-done | bytes 589856 | tf_op jit(solution)/shard_map/ppermute | solution.py:874
  260.6 14.1 %attn_bwd.3 = (f32[512,768]{1,0:T(8,128)}, bf16[512,768]{1,0:T(8,128)(2,1)}, bf16[4,512,384]{2,1,0:T(8,128)(2,1)}, bf16[512,768]{1,0:T(8,128)(2,1)}, f32[8,768]{1,0:T(8,128)}) custom-call(s32[4]{0:T(128)} %pad_add_fusion.1.scal.refs_0_, f32[512,768]{1,0:T(8,128)} %get-tuple-element.198.dz2, bf16[512,768]{1,0:T(8,128)(2,1)} %get-tuple-element.199.h_mine, ...), custom_call_target="tpu_custom_call" | custom-call | flops 15399999488 | bytes 50400000 | tf_op jit(solution)/shard_map/attn_bwd/pallas_call | solution.py:626
  274.7 9.1 %collective-permute-done.40.more_b = bf16[1,192,768]{2,1,0:T(8,128)(2,1)S(1)} collective-permute-done((bf16[1,192,768]{2,1,0:T(8,128)(2,1)}, bf16[1,192,768]{2,1,0:T(8,128)(2,1)S(1)}, u32[]{:S(2)}, u32[]{:S(2)}) %collective-permute-start.40) | collective-permute-done | bytes 294944 | tf_op jit(solution)/shard_map/ppermute | solution.py:874
  284.6 2.4 add_third.3
  287.6 3.3 collective-permute-start.46
  290.9 4.3 attn_dw.3
  298.0 2.8 add_second.5
  305.8 4.9 %collective-permute-start.47 = (bf16[1,192,768]{2,1,0:T(8,128)(2,1)}, bf16[1,192,768]{2,1,0:T(8,128)(2,1)S(1)}, u32[]{:S(2)}, u32[]{:S(2)}) collective-permute-start(bf16[1,192,768]{2,1,0:T(8,128)(2,1)} %add_fourth.2.mine), channel_id=1, source_target_pairs={{0,4},{4,0},{8,12},{12,8},{16,20},{20,16},{24,28},{28,24},{1,5},{5... | collective-permute-start | bytes 884744 | tf_op jit(solution)/shard_map/ppermute | solution.py:874
  317.9 3.5 collective-permute-done.50.more_a
  322.5 3.5 add_quarters.1
  327.4 2.4 split_pieces.1
  336.6 3.3 collective-permute-done.54.got_a
  346.6 9.1 %collective-permute-start.59 = (bf16[1,192,768]{2,1,0:T(8,128)(2,1)S(1)}, bf16[1,192,768]{2,1,0:T(8,128)(2,1)S(1)}, u32[]{:S(2)}, u32[]{:S(2)}) collective-permute-start(bf16[1,192,768]{2,1,0:T(8,128)(2,1)S(1)} %copy-done.61), channel_id=1, source_target_pairs={{0,3},{1,0},{2,1},{3,2},{4,6},{5,7},{6,4},{7,5},{8,11},{9,8},{10,9... | collective-permute-start | bytes 884744 | tf_op jit(solution)/shard_map/ppermute | solution.py:885
  358.5 8.9 %collective-permute-done.59.moved_b = bf16[1,192,768]{2,1,0:T(8,128)(2,1)S(1)} collective-permute-done((bf16[1,192,768]{2,1,0:T(8,128)(2,1)S(1)}, bf16[1,192,768]{2,1,0:T(8,128)(2,1)S(1)}, u32[]{:S(2)}, u32[]{:S(2)}) %collective-permute-start.59) | collective-permute-done | bytes 294944 | tf_op jit(solution)/shard_map/ppermute | solution.py:885
  370.0 5.3 %collective-permute-start.60 = (bf16[1,192,768]{2,1,0:T(8,128)(2,1)}, bf16[1,192,768]{2,1,0:T(8,128)(2,1)S(1)}, u32[]{:S(2)}, u32[]{:S(2)}) collective-permute-start(bf16[1,192,768]{2,1,0:T(8,128)(2,1)} %add_fourth.3.mine), channel_id=1, source_target_pairs={{0,4},{4,0},{8,12},{12,8},{16,20},{20,16},{24,28},{28,24},{1,5},{5... | collective-permute-start | bytes 884744 | tf_op jit(solution)/shard_map/ppermute | solution.py:874
  381.4 24.9 %all-gather.13.cloned.1.call-done = bf16[8,192,384]{2,1,0:T(8,128)(2,1)} async-done(((bf16[2,192,384]{2,1,0:T(8,128)(2,1)}), bf16[8,192,384]{2,1,0:T(8,128)(2,1)}) %all-gather.13.cloned.1.call-update) | async-done | bytes 1179664 | tf_op jit(solution)/shard_map/all_gather | solution.py:1060
  409.5 2.9 collective-permute-done.74
  413.9 3.0 collective-permute-done.75
  417.0 4.1 collective-permute-start.76
  423.5 3.2 collective-permute-start.77
  433.2 2.5 collective-permute-start.79
  449.0 3.0 attn_out.2
  457.1 3.0 attn_out.3
  460.0 4.1 ff_out.2
  465.2 4.1 ff_out.3
  (424 shorter events, 141.3 us)
Async XLA Ops:
  7.2 58.5 %all-gather.9.cloned.1.call-start = ((), (), s32[]{:S(2)}) async-start(), calls=%async_computation.4 | async-start | bytes 1536000 | tf_op jit(solution)/shard_map/all_gather | solution.py:946
  18.8 109.6 %all-gather.11.cloned.1.call-start = ((), (), s32[]{:S(2)}) async-start(), calls=%async_computation.5 | async-start | bytes 1536000 | tf_op jit(solution)/shard_map/all_gather | solution.py:946
  20.1 13.6 %collective-permute-start.4 = (bf16[208,768]{1,0:T(8,128)(2,1)S(1)}, bf16[208,768]{1,0:T(8,128)(2,1)S(1)}, u32[]{:S(2)}, u32[]{:S(2)}) collective-permute-start(bf16[208,768]{1,0:T(8,128)(2,1)S(1)} %pad_maximum_fusion), channel_id=1, source_target_pairs={{0,1},{1,2},{2,3},{3,0},{4,6},{5,7},{6,4},{7,5},{8,9},{9,10},{10,1... | collective-permute-start | bytes 958472 | tf_op jit(solution)/shard_map/ppermute | solution.py:885
  23.2 12.2 %collective-permute-start.3 = (bf16[208,768]{1,0:T(8,128)(2,1)S(1)}, bf16[208,768]{1,0:T(8,128)(2,1)}, u32[]{:S(2)}, u32[]{:S(2)}) collective-permute-start(bf16[208,768]{1,0:T(8,128)(2,1)S(1)} %pad_maximum_fusion), channel_id=1, source_target_pairs={{4,7},{5,4},{6,5},{7,6},{12,15},{13,12},{14,13},{15,14},{20,23},{2... | collective-permute-start | bytes 958472 | tf_op jit(solution)/shard_map/ppermute | solution.py:885
  24.5 15.1 %collective-permute-start.1 = (bf16[256,768]{1,0:T(8,128)(2,1)S(1)}, bf16[256,768]{1,0:T(8,128)(2,1)S(1)}, u32[]{:S(2)}, u32[]{:S(2)}) collective-permute-start(bf16[256,768]{1,0:T(8,128)(2,1)S(1)} %copy-done.6), channel_id=1, source_target_pairs={{1,4},{3,6},{4,1},{6,3},{9,12},{11,14},{12,9},{14,11},{17,20},{19,... | collective-permute-start | bytes 1179656 | tf_op jit(solution)/shard_map/ppermute | solution.py:896
  33.6 25.8 %collective-permute-start.8 = (bf16[208,768]{1,0:T(8,128)(2,1)S(1)}, bf16[208,768]{1,0:T(8,128)(2,1)}, u32[]{:S(2)}, u32[]{:S(2)}) collective-permute-start(bf16[208,768]{1,0:T(8,128)(2,1)S(1)} %collective-permute-done.4.refs_7_.refs_14_.refs_11_.refs_4_), channel_id=1, source_target_pairs={{0,8},{4,12},{8,0},{12,4},{16,24},{20,28},{24,16},{28,20},{1,9},{5... | collective-permute-start | bytes 958472 | tf_op jit(solution)/shard_map/ppermute | solution.py:874
  35.3 25.8 %collective-permute-start.6 = (bf16[208,768]{1,0:T(8,128)(2,1)}, bf16[208,768]{1,0:T(8,128)(2,1)}, u32[]{:S(2)}, u32[]{:S(2)}) collective-permute-start(bf16[208,768]{1,0:T(8,128)(2,1)} %collective-permute-done.3.refs_6_.refs_10_.refs_0_), channel_id=1, source_target_pairs={{4,20},{12,28},{20,4},{28,12},{5,21},{13,29},{21,5},{29,13},{6,22}... | collective-permute-start | bytes 958472 | tf_op jit(solution)/shard_map/ppermute | solution.py:874
  36.7 31.3 %collective-permute-start.5 = (bf16[208,768]{1,0:T(8,128)(2,1)}, bf16[208,768]{1,0:T(8,128)(2,1)}, u32[]{:S(2)}, u32[]{:S(2)}) collective-permute-start(bf16[208,768]{1,0:T(8,128)(2,1)} %collective-permute-done.3.refs_6_.refs_10_.refs_0_), channel_id=1, source_target_pairs={{4,12},{12,4},{20,28},{28,20},{5,13},{13,5},{21,29},{29,21},{6,14}... | collective-permute-start | bytes 958472 | tf_op jit(solution)/shard_map/ppermute | solution.py:874
  38.1 31.5 %collective-permute-start.9 = (bf16[208,768]{1,0:T(8,128)(2,1)S(1)}, bf16[208,768]{1,0:T(8,128)(2,1)}, u32[]{:S(2)}, u32[]{:S(2)}) collective-permute-start(bf16[208,768]{1,0:T(8,128)(2,1)S(1)} %collective-permute-done.4.refs_7_.refs_14_.refs_11_.refs_4_), channel_id=1, source_target_pairs={{0,16},{4,20},{8,24},{12,28},{16,0},{20,4},{24,8},{28,12},{1,17},{... | collective-permute-start | bytes 958472 | tf_op jit(solution)/shard_map/ppermute | solution.py:874
  39.7 30.4 %collective-permute-start.2 = (bf16[256,768]{1,0:T(8,128)(2,1)S(1)}, bf16[256,768]{1,0:T(8,128)(2,1)S(1)}, u32[]{:S(2)}, u32[]{:S(2)}) collective-permute-start(bf16[256,768]{1,0:T(8,128)(2,1)S(1)} %broadcast_select_fusion.3.refs_1_), channel_id=1, source_target_pairs={{0,4},{4,0},{8,12},{12,8},{16,20},{20,16},{24,28},{28,24},{1,5},{5... | collective-permute-start | bytes 1179656 | tf_op jit(solution)/shard_map/ppermute | solution.py:874
  68.1 22.3 %collective-permute-start.14 = (bf16[2,3,192,384]{3,2,1,0:T(8,128)(2,1)}, bf16[2,3,192,384]{3,2,1,0:T(8,128)(2,1)S(1)}, u32[]{:S(2)}, u32[]{:S(2)}) collective-permute-start(bf16[2,3,192,384]{3,2,1,0:T(8,128)(2,1)} %get-tuple-element.143.refs_0_.refs_11_), channel_id=1, source_target_pairs={{0,8},{4,12},{8,0},{12,4},{16,24},{20,28},{24,16},{28,20},{1,9},{5... | collective-permute-start | bytes 2654216 | tf_op jit(solution)/shard_map/ppermute | solution.py:874
  69.6 22.0 %collective-permute-start.15 = (bf16[2,3,192,384]{3,2,1,0:T(8,128)(2,1)}, bf16[2,3,192,384]{3,2,1,0:T(8,128)(2,1)S(1)}, u32[]{:S(2)}, u32[]{:S(2)}) collective-permute-start(bf16[2,3,192,384]{3,2,1,0:T(8,128)(2,1)} %get-tuple-element.143.refs_0_.refs_11_), channel_id=1, source_target_pairs={{0,16},{4,20},{8,24},{12,28},{16,0},{20,4},{24,8},{28,12},{1,17},{... | collective-permute-start | bytes 2654216 | tf_op jit(solution)/shard_map/ppermute | solution.py:874
  83.1 21.5 %collective-permute-start.13 = (bf16[512,768]{1,0:T(8,128)(2,1)}, bf16[512,768]{1,0:T(8,128)(2,1)}, u32[]{:S(2)}, u32[]{:S(2)}) collective-permute-start(bf16[512,768]{1,0:T(8,128)(2,1)} %get-tuple-element.149.a_mine), channel_id=1, source_target_pairs={{0,4},{4,0},{8,12},{12,8},{16,20},{20,16},{24,28},{28,24},{1,5},{5... | collective-permute-start | bytes 2359304 | tf_op jit(solution)/shard_map/ppermute | solution.py:874
  90.4 14.2 %collective-permute-start.16 = (bf16[3,192,384]{2,1,0:T(8,128)(2,1)S(1)}, bf16[3,192,384]{2,1,0:T(8,128)(2,1)}, u32[]{:S(2)}, u32[]{:S(2)}) collective-permute-start(bf16[3,192,384]{2,1,0:T(8,128)(2,1)S(1)} %slice_bitcast_fusion.3), channel_id=1, source_target_pairs={{0,16},{4,20},{8,24},{12,28},{16,0},{20,4},{24,8},{28,12},{1,17},{... | collective-permute-start | bytes 1327112 | tf_op jit(solution)/shard_map/ppermute | solution.py:874
  91.7 12.9 %collective-permute-start.17 = (bf16[3,192,384]{2,1,0:T(8,128)(2,1)S(1)}, bf16[3,192,384]{2,1,0:T(8,128)(2,1)}, u32[]{:S(2)}, u32[]{:S(2)}) collective-permute-start(bf16[3,192,384]{2,1,0:T(8,128)(2,1)S(1)} %slice_bitcast_fusion.2), channel_id=1, source_target_pairs={{0,8},{4,12},{8,0},{12,4},{16,24},{20,28},{24,16},{28,20},{1,9},{5... | collective-permute-start | bytes 1327112 | tf_op jit(solution)/shard_map/ppermute | solution.py:874
  95.0 232.4 %reduce-scatter.3.cloned.1.call-start = ((), (), s32[]{:S(2)}) async-start(), calls=%async_computation.2 | async-start | bytes 5898240 | tf_op jit(solution)/shard_map/reduce_scatter | solution.py:1020
  114.9 21.9 %collective-permute-start.18 = (bf16[512,768]{1,0:T(8,128)(2,1)}, bf16[512,768]{1,0:T(8,128)(2,1)S(1)}, u32[]{:S(2)}, u32[]{:S(2)}) collective-permute-start(bf16[512,768]{1,0:T(8,128)(2,1)} %get-tuple-element.155.refs_2_), channel_id=1, source_target_pairs={{0,4},{4,0},{8,12},{12,8},{16,20},{20,16},{24,28},{28,24},{1,5},{5... | collective-permute-start | bytes 2359304 | tf_op jit(solution)/shard_map/ppermute | solution.py:874
  118.8 12.0 %collective-permute-start.19 = (bf16[192,768]{1,0:T(8,128)(2,1)}, bf16[192,768]{1,0:T(8,128)(2,1)S(1)}, u32[]{:S(2)}, u32[]{:S(2)}) collective-permute-start(bf16[192,768]{1,0:T(8,128)(2,1)} %collective-permute-done.12.refs_14_.refs_0_), channel_id=1, source_target_pairs={{4,12},{12,4},{20,28},{28,20},{5,13},{13,5},{21,29},{29,21},{6,14}... | collective-permute-start | bytes 884744 | tf_op jit(solution)/shard_map/ppermute | solution.py:874
  119.5 12.3 %collective-permute-start.23 = (bf16[192,768]{1,0:T(8,128)(2,1)S(1)}, bf16[192,768]{1,0:T(8,128)(2,1)S(1)}, u32[]{:S(2)}, u32[]{:S(2)}) collective-permute-start(bf16[192,768]{1,0:T(8,128)(2,1)S(1)} %collective-permute-done.11.refs_18_.refs_4_), channel_id=1, source_target_pairs={{0,16},{4,20},{8,24},{12,28},{16,0},{20,4},{24,8},{28,12},{1,17},{... | collective-permute-start | bytes 884744 | tf_op jit(solution)/shard_map/ppermute | solution.py:874
  119.6 13.8 %collective-permute-start.21 = (bf16[192,768]{1,0:T(8,128)(2,1)S(1)}, bf16[192,768]{1,0:T(8,128)(2,1)S(1)}, u32[]{:S(2)}, u32[]{:S(2)}) collective-permute-start(bf16[192,768]{1,0:T(8,128)(2,1)S(1)} %collective-permute-done.20.refs_16_.refs_2_), channel_id=1, source_target_pairs={{4,12},{12,4},{20,28},{28,20},{5,13},{13,5},{21,29},{29,21},{6,14}... | collective-permute-start | bytes 884744 | tf_op jit(solution)/shard_map/ppermute | solution.py:874
  130.9 24.6 %collective-permute-start.26 = (bf16[2,3,192,384]{3,2,1,0:T(8,128)(2,1)}, bf16[2,3,192,384]{3,2,1,0:T(8,128)(2,1)S(1)}, u32[]{:S(2)}, u32[]{:S(2)}) collective-permute-start(bf16[2,3,192,384]{3,2,1,0:T(8,128)(2,1)} %get-tuple-element.153.refs_0_.refs_11_), channel_id=1, source_target_pairs={{0,8},{4,12},{8,0},{12,4},{16,24},{20,28},{24,16},{28,20},{1,9},{5... | collective-permute-start | bytes 2654216 | tf_op jit(solution)/shard_map/ppermute | solution.py:874
  131.8 24.0 %collective-permute-start.27 = (bf16[2,3,192,384]{3,2,1,0:T(8,128)(2,1)}, bf16[2,3,192,384]{3,2,1,0:T(8,128)(2,1)S(1)}, u32[]{:S(2)}, u32[]{:S(2)}) collective-permute-start(bf16[2,3,192,384]{3,2,1,0:T(8,128)(2,1)} %get-tuple-element.153.refs_0_.refs_11_), channel_id=1, source_target_pairs={{0,16},{4,20},{8,24},{12,28},{16,0},{20,4},{24,8},{28,12},{1,17},{... | collective-permute-start | bytes 2654216 | tf_op jit(solution)/shard_map/ppermute | solution.py:874
  155.6 12.3 %collective-permute-start.28 = (bf16[3,192,384]{2,1,0:T(8,128)(2,1)S(1)}, bf16[3,192,384]{2,1,0:T(8,128)(2,1)S(1)}, u32[]{:S(2)}, u32[]{:S(2)}) collective-permute-start(bf16[3,192,384]{2,1,0:T(8,128)(2,1)S(1)} %slice_bitcast_fusion.1), channel_id=1, source_target_pairs={{0,16},{4,20},{8,24},{12,28},{16,0},{20,4},{24,8},{28,12},{1,17},{... | collective-permute-start | bytes 1327112 | tf_op jit(solution)/shard_map/ppermute | solution.py:874
  155.8 12.5 %collective-permute-start.29 = (bf16[3,192,384]{2,1,0:T(8,128)(2,1)S(1)}, bf16[3,192,384]{2,1,0:T(8,128)(2,1)S(1)}, u32[]{:S(2)}, u32[]{:S(2)}) collective-permute-start(bf16[3,192,384]{2,1,0:T(8,128)(2,1)S(1)} %slice_bitcast_fusion), channel_id=1, source_target_pairs={{0,8},{4,12},{8,0},{12,4},{16,24},{20,28},{24,16},{28,20},{1,9},{5... | collective-permute-start | bytes 1327112 | tf_op jit(solution)/shard_map/ppermute | solution.py:874
  156.4 23.3 %collective-permute-start.31 = (bf16[256,768]{1,0:T(8,128)(2,1)S(1)}, bf16[256,768]{1,0:T(8,128)(2,1)S(1)}, u32[]{:S(2)}, u32[]{:S(2)}) collective-permute-start(bf16[256,768]{1,0:T(8,128)(2,1)S(1)} %copy-done.7), channel_id=1, source_target_pairs={{1,4},{3,6},{4,1},{6,3},{9,12},{11,14},{12,9},{14,11},{17,20},{19,... | collective-permute-start | bytes 1179656 | tf_op jit(solution)/shard_map/ppermute | solution.py:896
  201.1 180.3 %reduce-scatter.5.cloned.1.call-start = ((), (), s32[]{:S(2)}) async-start(), calls=%async_computation.3 | async-start | bytes 1474560 | tf_op jit(solution)/shard_map/reduce_scatter | solution.py:1049
  236.4 23.3 %collective-permute-start.38 = (bf16[512,768]{1,0:T(8,128)(2,1)}, bf16[512,768]{1,0:T(8,128)(2,1)S(1)}, u32[]{:S(2)}, u32[]{:S(2)}) collective-permute-start(bf16[512,768]{1,0:T(8,128)(2,1)} %get-tuple-element.199.h_mine), channel_id=1, source_target_pairs={{0,4},{4,0},{8,12},{12,8},{16,20},{20,16},{24,28},{28,24},{1,5},{5... | collective-permute-start | bytes 2359304 | tf_op jit(solution)/shard_map/ppermute | solution.py:874
  236.7 16.1 %collective-permute-start.36 = (bf16[2,1,192,768]{3,2,1,0:T(8,128)(2,1)S(1)}, bf16[2,1,192,768]{3,2,1,0:T(8,128)(2,1)S(1)}, u32[]{:S(2)}, u32[]{:S(2)}) collective-permute-start(bf16[2,1,192,768]{3,2,1,0:T(8,128)(2,1)S(1)} %copy-done.43), channel_id=1, source_target_pairs={{0,16},{4,20},{8,24},{12,28},{16,0},{20,4},{24,8},{28,12},{1,17},{... | collective-permute-start | bytes 1769480 | tf_op jit(solution)/shard_map/ppermute | solution.py:874
  238.2 15.0 %collective-permute-start.37 = (bf16[2,1,192,768]{3,2,1,0:T(8,128)(2,1)S(1)}, bf16[2,1,192,768]{3,2,1,0:T(8,128)(2,1)S(1)}, u32[]{:S(2)}, u32[]{:S(2)}) collective-permute-start(bf16[2,1,192,768]{3,2,1,0:T(8,128)(2,1)S(1)} %copy-done.42), channel_id=1, source_target_pairs={{0,8},{4,12},{8,0},{12,4},{16,24},{20,28},{24,16},{28,20},{1,9},{5... | collective-permute-start | bytes 1769480 | tf_op jit(solution)/shard_map/ppermute | solution.py:874
  246.0 50.4 %collective-permute-start.43 = (bf16[2,4,192,384]{3,2,1,0:T(8,128)(2,1)}, bf16[2,4,192,384]{3,2,1,0:T(8,128)(2,1)S(1)}, u32[]{:S(2)}, u32[]{:S(2)}) collective-permute-start(bf16[2,4,192,384]{3,2,1,0:T(8,128)(2,1)} %get-tuple-element.191), channel_id=1, source_target_pairs={{0,16},{4,20},{8,24},{12,28},{16,0},{20,4},{24,8},{28,12},{1,17},{... | collective-permute-start | bytes 3538952 | tf_op jit(solution)/shard_map/ppermute | solution.py:874
  256.3 18.4 %collective-permute-start.39 = (bf16[1,192,768]{2,1,0:T(8,128)(2,1)}, bf16[1,192,768]{2,1,0:T(8,128)(2,1)S(1)}, u32[]{:S(2)}, u32[]{:S(2)}) collective-permute-start(bf16[1,192,768]{2,1,0:T(8,128)(2,1)} %get-tuple-element.195), channel_id=1, source_target_pairs={{0,8},{4,12},{8,0},{12,4},{16,24},{20,28},{24,16},{28,20},{1,9},{5... | collective-permute-start | bytes 884744 | tf_op jit(solution)/shard_map/ppermute | solution.py:874
  256.9 26.9 %collective-permute-start.40 = (bf16[1,192,768]{2,1,0:T(8,128)(2,1)}, bf16[1,192,768]{2,1,0:T(8,128)(2,1)S(1)}, u32[]{:S(2)}, u32[]{:S(2)}) collective-permute-start(bf16[1,192,768]{2,1,0:T(8,128)(2,1)} %get-tuple-element.196), channel_id=1, source_target_pairs={{0,16},{4,20},{8,24},{12,28},{16,0},{20,4},{24,8},{28,12},{1,17},{... | collective-permute-start | bytes 884744 | tf_op jit(solution)/shard_map/ppermute | solution.py:874
  258.2 38.8 %collective-permute-start.44 = (bf16[2,4,192,384]{3,2,1,0:T(8,128)(2,1)S(1)}, bf16[2,4,192,384]{3,2,1,0:T(8,128)(2,1)S(1)}, u32[]{:S(2)}, u32[]{:S(2)}) collective-permute-start(bf16[2,4,192,384]{3,2,1,0:T(8,128)(2,1)S(1)} %copy-done.29), channel_id=1, source_target_pairs={{0,8},{4,12},{8,0},{12,4},{16,24},{20,28},{24,16},{28,20},{1,9},{5... | collective-permute-start | bytes 3538952 | tf_op jit(solution)/shard_map/ppermute | solution.py:874
  286.9 15.3 %collective-permute-start.45 = (bf16[1,192,768]{2,1,0:T(8,128)(2,1)}, bf16[1,192,768]{2,1,0:T(8,128)(2,1)S(1)}, u32[]{:S(2)}, u32[]{:S(2)}) collective-permute-start(bf16[1,192,768]{2,1,0:T(8,128)(2,1)} %get-tuple-element.227.a), channel_id=1, source_target_pairs={{4,5},{5,6},{6,7},{7,4},{12,13},{13,14},{14,15},{15,12},{20,21},{2... | collective-permute-start | bytes 884744 | tf_op jit(solution)/shard_map/ppermute | solution.py:885
  287.6 15.5 %collective-permute-start.46 = (bf16[1,192,768]{2,1,0:T(8,128)(2,1)}, bf16[1,192,768]{2,1,0:T(8,128)(2,1)S(1)}, u32[]{:S(2)}, u32[]{:S(2)}) collective-permute-start(bf16[1,192,768]{2,1,0:T(8,128)(2,1)} %get-tuple-element.213), channel_id=1, source_target_pairs={{0,3},{1,0},{2,1},{3,2},{4,6},{5,7},{6,4},{7,5},{8,11},{9,8},{10,9... | collective-permute-start | bytes 884744 | tf_op jit(solution)/shard_map/ppermute | solution.py:885
  295.2 19.5 %collective-permute-start.48 = (bf16[2,1,192,768]{3,2,1,0:T(8,128)(2,1)}, bf16[2,1,192,768]{3,2,1,0:T(8,128)(2,1)S(1)}, u32[]{:S(2)}, u32[]{:S(2)}) collective-permute-start(bf16[2,1,192,768]{3,2,1,0:T(8,128)(2,1)} %get-tuple-element.216), channel_id=1, source_target_pairs={{0,16},{4,20},{8,24},{12,28},{16,0},{20,4},{24,8},{28,12},{1,17},{... | collective-permute-start | bytes 1769480 | tf_op jit(solution)/shard_map/ppermute | solution.py:874
  296.4 18.4 %collective-permute-start.49 = (bf16[2,1,192,768]{3,2,1,0:T(8,128)(2,1)}, bf16[2,1,192,768]{3,2,1,0:T(8,128)(2,1)S(1)}, u32[]{:S(2)}, u32[]{:S(2)}) collective-permute-start(bf16[2,1,192,768]{3,2,1,0:T(8,128)(2,1)} %get-tuple-element.231), channel_id=1, source_target_pairs={{0,8},{4,12},{8,0},{12,4},{16,24},{20,28},{24,16},{28,20},{1,9},{5... | collective-permute-start | bytes 1769480 | tf_op jit(solution)/shard_map/ppermute | solution.py:874
  300.8 20.7 %collective-permute-start.50 = (bf16[4,192,384]{2,1,0:T(8,128)(2,1)}, bf16[4,192,384]{2,1,0:T(8,128)(2,1)S(1)}, u32[]{:S(2)}, u32[]{:S(2)}) collective-permute-start(bf16[4,192,384]{2,1,0:T(8,128)(2,1)} %get-tuple-element.225), channel_id=1, source_target_pairs={{0,8},{4,12},{8,0},{12,4},{16,24},{20,28},{24,16},{28,20},{1,9},{5... | collective-permute-start | bytes 1769480 | tf_op jit(solution)/shard_map/ppermute | solution.py:874
  302.2 19.2 %collective-permute-start.51 = (bf16[4,192,384]{2,1,0:T(8,128)(2,1)}, bf16[4,192,384]{2,1,0:T(8,128)(2,1)S(1)}, u32[]{:S(2)}, u32[]{:S(2)}) collective-permute-start(bf16[4,192,384]{2,1,0:T(8,128)(2,1)} %get-tuple-element.226), channel_id=1, source_target_pairs={{0,16},{4,20},{8,24},{12,28},{16,0},{20,4},{24,8},{28,12},{1,17},{... | collective-permute-start | bytes 1769480 | tf_op jit(solution)/shard_map/ppermute | solution.py:874
  326.0 80.3 %all-gather.13.cloned.1.call-start = ((), (), s32[]{:S(2)}) async-start(), calls=%async_computation.6 | async-start | bytes 1474560 | tf_op jit(solution)/shard_map/all_gather | solution.py:1060
  345.9 12.5 %collective-permute-start.58 = (bf16[1,192,768]{2,1,0:T(8,128)(2,1)S(1)}, bf16[1,192,768]{2,1,0:T(8,128)(2,1)S(1)}, u32[]{:S(2)}, u32[]{:S(2)}) collective-permute-start(bf16[1,192,768]{2,1,0:T(8,128)(2,1)S(1)} %copy-done.60), channel_id=1, source_target_pairs={{4,5},{5,6},{6,7},{7,4},{12,13},{13,14},{14,15},{15,12},{20,21},{2... | collective-permute-start | bytes 884744 | tf_op jit(solution)/shard_map/ppermute | solution.py:885
  346.6 20.7 %collective-permute-start.59 = (bf16[1,192,768]{2,1,0:T(8,128)(2,1)S(1)}, bf16[1,192,768]{2,1,0:T(8,128)(2,1)S(1)}, u32[]{:S(2)}, u32[]{:S(2)}) collective-permute-start(bf16[1,192,768]{2,1,0:T(8,128)(2,1)S(1)} %copy-done.61), channel_id=1, source_target_pairs={{0,3},{1,0},{2,1},{3,2},{4,6},{5,7},{6,4},{7,5},{8,11},{9,8},{10,9... | collective-permute-start | bytes 884744 | tf_op jit(solution)/shard_map/ppermute | solution.py:885
  379.4 69.5 %all-gather.15.cloned.1.call-start = ((), (), s32[]{:S(2)}) async-start(), calls=%async_computation.7 | async-start | bytes 1474560 | tf_op jit(solution)/shard_map/all_gather | solution.py:1060
  380.6 46.0 %collective-permute-start.41 = (bf16[512,768]{1,0:T(8,128)(2,1)}, bf16[512,768]{1,0:T(8,128)(2,1)}, u32[]{:S(2)}, u32[]{:S(2)}) collective-permute-start(bf16[512,768]{1,0:T(8,128)(2,1)} %get-tuple-element.209), channel_id=1, source_target_pairs={{0,4},{4,0},{8,12},{12,8},{16,20},{20,16},{24,28},{28,24},{1,5},{5... | collective-permute-start | bytes 2359304 | tf_op jit(solution)/shard_map/ppermute | solution.py:874
  407.3 21.5 %collective-permute-start.33 = (bf16[256,768]{1,0:T(8,128)(2,1)}, bf16[256,768]{1,0:T(8,128)(2,1)S(1)}, u32[]{:S(2)}, u32[]{:S(2)}) collective-permute-start(bf16[256,768]{1,0:T(8,128)(2,1)} %constant_dynamic-slice_fusion.1), channel_id=1, source_target_pairs={{1,4},{3,6},{4,1},{6,3},{9,12},{11,14},{12,9},{14,11},{17,20},{19,... | collective-permute-start | bytes 1179656 | tf_op jit(solution)/shard_map/ppermute | solution.py:896
  428.0 20.9 %collective-permute-start.42 = (f32[256,768]{1,0:T(8,128)S(1)}, f32[256,768]{1,0:T(8,128)S(1)}, u32[]{:S(2)}, u32[]{:S(2)}) collective-permute-start(f32[256,768]{1,0:T(8,128)S(1)} %dynamic-slice_add_fusion), channel_id=1, source_target_pairs={{1,4},{3,6},{4,1},{6,3},{9,12},{11,14},{12,9},{14,11},{17,20},{19,... | collective-permute-start | bytes 2359304 | tf_op jit(solution)/shard_map/ppermute | solution.py:896
  433.2 26.8 %collective-permute-start.79 = (bf16[4,2,192,384]{3,2,1,0:T(8,128)(2,1)}, bf16[4,2,192,384]{3,2,1,0:T(8,128)(2,1)}, u32[]{:S(2)}, u32[]{:S(2)}) collective-permute-start(bf16[4,2,192,384]{3,2,1,0:T(8,128)(2,1)} %bitcast.90), channel_id=1, source_target_pairs={{0,4},{4,0},{8,12},{12,8},{16,20},{20,16},{24,28},{28,24},{1,5},{5... | collective-permute-start | bytes 3538952 | tf_op jit(solution)/shard_map/ppermute | solution.py:874
  448.9 15.3 %collective-permute-start.78 = (bf16[4,2,192,384]{3,2,1,0:T(8,128)(2,1)}, bf16[4,2,192,384]{3,2,1,0:T(8,128)(2,1)S(1)}, u32[]{:S(2)}, u32[]{:S(2)}) collective-permute-start(bf16[4,2,192,384]{3,2,1,0:T(8,128)(2,1)} %bitcast.93), channel_id=1, source_target_pairs={{0,4},{4,0},{8,12},{12,8},{16,20},{20,16},{24,28},{28,24},{1,5},{5... | collective-permute-start | bytes 3538952 | tf_op jit(solution)/shard_map/ppermute | solution.py:874
  (127 other events, 732.2 us)
Sparse Core Ops, SparseCore 0:
  18.9 41.9 all-gather.8
  95.1 33.3 all-gather.10
  201.2 89.0 reduce-scatter.2
  326.2 37.2 reduce-scatter.4
  379.5 26.7 all-gather.12
  408.0 29.8 all-gather.14

commit v3 on v1

v3 whole, which is shorter than its diff:
```python
import functools
import math

import jax
import jax.numpy as jnp
from jax import lax
from jax.experimental import pallas as pl
from jax.experimental.pallas import tpu as pltpu
from jax.sharding import PartitionSpec as P

HEAD_DIM = 64
epsilon = 1e-06
masked_fill = -1e30
bf16 = jnp.bfloat16
f32 = jnp.float32
ANY = pl.BlockSpec(memory_space=pl.ANY)
SMEM = pl.BlockSpec(memory_space=pltpu.SMEM)
VMEM = pl.BlockSpec(memory_space=pltpu.VMEM)
HBM = pl.BlockSpec(memory_space=pltpu.HBM)
SLOTS = 2
PACE = 1.0


def dot_nn(left, right):
    return lax.dot_general(left, right, (((1,), (0,)), ((), ())), preferred_element_type=f32)


def dot_nt(left, right):
    return lax.dot_general(left, right, (((1,), (1,)), ((), ())), preferred_element_type=f32)


def dot_tn(left, right):
    return lax.dot_general(left, right, (((0,), (0,)), ((), ())), preferred_element_type=f32)


def norm_forward(summed, gain, shift):
    center = summed - jnp.mean(summed, -1, keepdims=True)
    recip = lax.rsqrt(jnp.mean(center * center, -1, keepdims=True) + epsilon)
    normed = center * recip
    return normed * gain + shift, normed, recip


def norm_backward(grad_rows, normed, recip, gain):
    scaled = grad_rows * gain
    first_mean = jnp.mean(scaled, -1, keepdims=True)
    second_mean = jnp.mean(scaled * normed, -1, keepdims=True)
    return recip * (scaled - first_mean - normed * second_mean)


def shape(dims, dtype):
    return jax.ShapeDtypeStruct(dims, dtype)


def params(mib):
    return pltpu.CompilerParams(vmem_limit_bytes=mib * 1024 * 1024)


def here():
    dp = lax.axis_index("dp")
    return dp & 1, (dp >> 1) & 3, lax.axis_index("tensor")


def cost(us):
    return pl.CostEstimate(flops=int(us * 1.1e9 * PACE), bytes_accessed=int(us * 3.6e6 * PACE), transcendentals=0)


def lane_half(rows, which):
    lane = lax.broadcasted_iota(jnp.int32, (rows, 2 * HEAD_DIM), 1)
    return (lane < HEAD_DIM) if which == 0 else (lane >= HEAD_DIM)


class Moves:
    def __init__(self, sems):
        self.sems, self.count, self.out = sems, 0, []

    def make(self, src, dst):
        self.count += 1
        return pltpu.make_async_copy(src, dst, self.sems.at[self.count - 1])

    def start(self, src, dst):
        copy = self.make(src, dst)
        copy.start()
        return copy

    def send(self, src, dst):
        self.out.append(self.start(src, dst))

    def finish(self):
        for copy in self.out:
            copy.wait()


def wait_all(copies):
    for c in copies:
        c.wait()


MOVES = 80
CHUNK = 256


def fetch_attn(moves, layer, own_qkv, own_out, a_refs, b_refs, w):
    core, place, _ = here()
    cols = own_out.shape[1]
    waits = []
    for j in range(4):
        t = j ^ place
        b = moves.start(b_refs[j].at[pl.ds(0, cols)], w.at[t, pl.ds(cols, cols)])
        dst = w.at[t, pl.ds(0, cols)]
        a = moves.make(a_refs[j].at[pl.ds(0, cols)], dst)
        sem = moves.sems.at[moves.count - 1]
        qkv_copy = pltpu.make_async_copy(own_qkv.at[layer, jnp.minimum(t, 2)], dst, sem)
        out_copy = pltpu.make_async_copy(own_out.at[layer], dst, sem)

        @pl.when(core != 0)
        def _(a=a):
            a.start()

        @pl.when((core == 0) & (t < 3))
        def _(qkv_copy=qkv_copy):
            qkv_copy.start()

        @pl.when((core == 0) & (t == 3))
        def _(out_copy=out_copy):
            out_copy.start()

        waits += [b, a]
    return waits


def fetch_ff(moves, layer, own_up, own_down, moved, wu, wd):
    core, place, _ = here()
    width, half = wu.shape[0], own_up.shape[2] // 2
    n_t = wu.shape[1] // half
    part, rows = width // 4, half // 4
    own, x, y, diag_up, diag_down = moved
    ups = [own.at[0], x.at[0], y.at[0], diag_up]
    downs = [own.at[1], x.at[1], y.at[1], diag_down]
    mine = pl.ds(pl.multiple_of(core * half, half), half)

    def up(k):
        if k == 0:
            return [moves.start(own_up.at[layer, :, mine], wu.at[:, pl.ds(0, half)])]
        got = []
        for j in range(4):
            at = pl.ds(pl.multiple_of((j ^ place) * part, part), part)
            got.append(moves.start(ups[j].at[k - 1], wu.at[at, pl.ds(k * half, half)]))
        return got

    def down(k):
        if k == 0:
            return [moves.start(own_down.at[layer, mine], wd.at[pl.ds(0, half)])]
        got = []
        for j in range(4):
            at = pl.ds(pl.multiple_of(k * half + (j ^ place) * rows, rows), rows)
            for n in range(2):
                src = downs[j].at[k - 1, pl.ds(n * rows, rows)]
                got.append(moves.start(src, wd.at[at, pl.ds(n * half, half)]))
        return got

    return up, down, n_t


def chunk_waits(waits, chunk, half):
    start, end = chunk * CHUNK, (chunk + 1) * CHUNK
    for k, copies in enumerate(waits):
        if start <= k * half < end:
            wait_all(copies)


BIAS_ROWS = 16


def split_rows(v):
    parts = []
    for _ in range(3):
        low = v.astype(bf16)
        parts.append(low)
        v = v - low.astype(f32)
    n = sum(p.shape[0] for p in parts)
    return jnp.concatenate(parts + [jnp.zeros((BIAS_ROWS - n, v.shape[1]), bf16)], 0)


def prepare_kernel(own_qkv, own_out, own_up, own_down, up_bias, qv_bias, segments, counts, *refs):
    layers = own_out.shape[0]
    attn, ff, packed, sems = refs[:layers], refs[layers : 2 * layers], refs[2 * layers], refs[2 * layers + 1]
    core, place, _ = here()
    cols, half = own_out.shape[1], up_bias.shape[1] // 2
    part, rows = own_up.shape[1] // 4, half // 4
    copies = []
    for l in range(layers):
        weights = attn[l].at[pl.ds(0, cols)]

        @pl.when(place < 3)
        def _(l=l, weights=weights):
            pltpu.make_async_copy(own_qkv.at[l, jnp.minimum(place, 2)], weights, sems.at[4 * l]).start()

        @pl.when(place == 3)
        def _(l=l, weights=weights):
            pltpu.make_async_copy(own_out.at[l], weights, sems.at[4 * l]).start()

        copies.append(pltpu.make_async_copy(own_out.at[l], weights, sems.at[4 * l]))
        up = own_up.at[l, pl.ds(pl.multiple_of(place * part, part), part), pl.ds(pl.multiple_of(core * half, half), half)]
        copies.append(pltpu.make_async_copy(up, ff[l].at[pl.ds(0, part)], sems.at[4 * l + 1]))
        copies[-1].start()
        at = pl.ds(pl.multiple_of(core * half + place * rows, rows), rows)
        for n in range(2):
            down = own_down.at[l, at, pl.ds(n * half, half)]
            copies.append(pltpu.make_async_copy(down, ff[l].at[pl.ds(part + n * rows, rows)], sems.at[4 * l + 2 + n]))
            copies[-1].start()
    for l in range(layers):
        row = jnp.where(core == 0, up_bias[l : l + 1, :half], up_bias[l : l + 1, half:])
        ff[l][2 * part :] = split_rows(row)
    attn[0][cols:] = split_rows(qv_bias[...])
    n, seq = segments.shape
    packed[:, :seq] = segments[...]
    for i in range(n):
        packed[i : i + 1, seq:] = jnp.full((1, packed.shape[1] - seq), counts[i], jnp.int32)
    for c in copies:
        c.wait()


def prepare(own_qkv, own_out, own_up, own_down, up_bias, qv_bias, segments, counts):
    layers, cols, width = own_out.shape
    half = up_bias.shape[1] // 2
    outs = [shape((cols + (0 if l else BIAS_ROWS), width), bf16) for l in range(layers)]
    outs += [shape((width // 2 + BIAS_ROWS, half), bf16)] * layers
    outs += [shape((segments.shape[0], segments.shape[1] + 128), jnp.int32)]
    got = pl.pallas_call(
        prepare_kernel,
        out_shape=outs,
        in_specs=[HBM] * 4 + [VMEM] * 3 + [SMEM],
        out_specs=[VMEM] * len(outs),
        scratch_shapes=[pltpu.SemaphoreType.DMA((4 * layers,))],
        compiler_params=params(56),
        cost_estimate=cost(2),
        name="prepare",
    )(own_qkv, own_out, own_up, own_down, up_bias, qv_bias, segments, counts)
    return got[:layers], got[layers : 2 * layers], got[2 * layers]


def mask_kernel(mine, theirs, out, out_t):
    core, _, z = here()
    row = pl.ds(z >> 1, 1)
    packed = jnp.where(core == (z & 1), mine[row], theirs[row])
    seq = out.shape[0]
    segments, slots = packed[:, :seq].astype(f32), packed[:, seq : seq + 1]
    column = jnp.transpose(jnp.broadcast_to(segments, (128, seq)))[:, 0:1]
    same = column == segments
    down = lax.broadcasted_iota(jnp.int32, (seq, seq), 0)
    along = lax.broadcasted_iota(jnp.int32, (seq, seq), 1)
    out[...] = jnp.where(same & ((along < slots) | (down >= slots)), 0.0, masked_fill)
    out_t[...] = jnp.where(same & ((down < slots) | (along >= slots)), 0.0, masked_fill)


def masks(mine, theirs):
    seq = mine.shape[1] - 128
    return pl.pallas_call(
        mask_kernel,
        out_shape=[shape((seq, seq), f32)] * 2,
        in_specs=[VMEM, VMEM],
        out_specs=[VMEM] * 2,
        compiler_params=params(12),
        cost_estimate=cost(2),
        name="masks",
    )(mine, theirs)


def attn_fwd_kernel(layer, *refs):
    refs = list(refs)
    first = layer == 0
    rows_in = refs[: 2 if first else 3]
    refs = refs[len(rows_in) :]
    if not first:
        ob, gain, shift = refs[:3]
        refs = refs[3:]
    own_bias, mask_in, a_bias, b_bias, own_qkv, own_out = refs[:6]
    a_refs, b_refs = refs[6:10], refs[10:14]
    refs = refs[14:]
    n_out = 5 if first else 7
    outs, refs = refs[:n_out], refs[n_out:]
    bufs, refs = refs[: len(rows_in)], refs[len(rows_in) :]
    vals, refs = refs[:n_out], refs[n_out:]
    mask, w, lse, packed, sems = refs
    xr = vals[0]
    qkv, lse_t, o, a_low = vals[-4:]
    core, _, _ = here()
    seq, width = xr.shape
    half, cols = seq // 2, own_out.shape[1]
    moves = Moves(sems)
    if first:
        at = [pl.ds(pl.multiple_of(c * half, half), half) for c in (core, 1 - core)]
        row_waits = [moves.start(src, xr.at[a]) for src, a in zip(rows_in, at)]
    else:
        row_waits = [
            [moves.start(src.at[pl.ds(i * half, half)], buf.at[pl.ds(i * half, half)]) for src, buf in zip(rows_in, bufs)]
            for i in range(2)
        ]
    bias_waits = [moves.start(ref.at[pl.ds(cols, BIAS_ROWS)], packed.at[n]) for n, ref in enumerate((a_bias, b_bias))]
    weight_waits = fetch_attn(moves, layer, own_qkv, own_out, a_refs, b_refs, w)
    mask_wait = moves.start(mask_in, mask)

    if first:
        wait_all(row_waits)
        moves.send(xr, outs[0])
    else:
        normed, recip = vals[1:3]
        h_in, f_mine, f_theirs = bufs
        for i in range(seq // 128):
            if i * 128 % half == 0:
                wait_all(row_waits[i * 128 // half])
            at = pl.ds(i * 128, 128)
            h = h_in[at] * gain[layer - 1, 0:1] + shift[layer - 1, 0:1]
            z = h + (f_mine[at].astype(f32) + f_theirs[at].astype(f32)) + ob[layer - 1, 1:2]
            new, n, r = norm_forward(z, gain[layer - 1, 1:2], shift[layer - 1, 1:2])
            xr[at] = new.astype(bf16)
            normed[at] = n
            recip[at] = r
        for n in range(3):
            moves.send(vals[n], outs[n])

    wait_all(bias_waits)
    a_row, b_row = (jnp.sum(packed[n, 0:3].astype(f32), 0, keepdims=True) for n in range(2))
    a_row = jnp.where(core == 0, own_bias[...], a_row)
    qb = []
    for i in range(2):
        base = (2 * layer + i) * cols
        qb.append(jnp.concatenate([a_row[:, base : base + cols], b_row[:, base : base + cols]], 1))
    wait_all(weight_waits)
    rows = 256
    for t in range(3):
        for i in range(seq // rows):
            at = pl.ds(i * rows, rows)
            acc = dot_nt(xr[at], w[t])
            if t != 1:
                acc = acc + qb[t // 2]
            qkv[t, at] = acc.astype(bf16)
    moves.send(qkv, outs[-4])
    mask_wait.wait()
    pairs = qkv.shape[2] // 128
    tile = 128
    lane = lax.broadcasted_iota(jnp.int32, (tile, 128), 1)

    @pl.loop(0, seq // tile)
    def _(i):
        at = pl.ds(pl.multiple_of(i * tile, tile), tile)
        bias = mask[at]
        keep = jnp.zeros((tile, 128), f32)
        for g in range(pairs):
            cs = pl.ds(g * 128, 128)
            q2 = qkv[0, at, cs] * jnp.asarray(1.0 / math.sqrt(HEAD_DIM), bf16)
            k2 = qkv[1, :, cs]
            v2 = qkv[2, :, cs]
            acc = None
            for hh in range(2):
                qm = jnp.where(lane_half(tile, hh), q2, jnp.zeros_like(q2))
                s = dot_nt(qm, k2) + bias
                top = jnp.max(s, -1, keepdims=True)
                e = jnp.exp(s - top)
                d = jnp.sum(e, -1, keepdims=True)
                pr = (e * (1.0 / d)).astype(bf16)
                keep = jnp.where(lane == 2 * g + hh, top + jnp.log(d), keep)
                vm = jnp.where(lane_half(seq, hh), v2, jnp.zeros_like(v2))
                got = dot_nn(pr, vm)
                acc = got if acc is None else acc + got
            o[at, cs] = acc.astype(bf16)
        lse[at] = keep

    moves.send(o, outs[-2])
    for i in range(seq // rows):
        at = pl.ds(i * rows, rows)
        a_low[at] = dot_nn(o[at], w[3]).astype(bf16)
        moves.send(a_low.at[at], outs[-1].at[at])
    lse_t[...] = jnp.transpose(lse[...])[0:8]
    moves.send(lse_t, outs[-3])
    moves.finish()


def attn_fwd(layer, rows_in, mask, bias, own_qkv, own_out, a_refs, b_refs):
    first = layer == 0
    seq, width, cols = mask.shape[0], own_out.shape[2], own_out.shape[1]
    wide = SLOTS * cols
    outs = [shape((seq, width), bf16)]
    if not first:
        outs += [shape((seq, width), f32), shape((seq, 1), f32)]
    outs += [
        shape((3, seq, wide), bf16),
        shape((8, seq), f32),
        shape((seq, wide), bf16),
        shape((seq, width), bf16),
    ]
    moving = 2 if first else 3
    small = rows_in[moving:]
    got = pl.pallas_call(
        functools.partial(attn_fwd_kernel, layer),
        out_shape=outs,
        in_specs=[ANY] * moving + [VMEM] * (len(small) + 1) + [ANY] * 13,
        out_specs=[HBM] * len(outs),
        scratch_shapes=[pltpu.VMEM(v.shape, v.dtype) for v in rows_in[:moving]]
        + [pltpu.VMEM(v.shape, v.dtype) for v in outs]
        + [
            pltpu.VMEM((seq, seq), f32),
            pltpu.VMEM((4, wide, width), bf16),
            pltpu.VMEM((seq, 128), f32),
            pltpu.VMEM((2, BIAS_ROWS, width), bf16),
            pltpu.SemaphoreType.DMA((MOVES,)),
        ],
        compiler_params=params(56),
        cost_estimate=cost(10),
        name="attn_fwd",
    )(*rows_in, bias[0], mask, *bias[1:], own_qkv, own_out, *a_refs, *b_refs)
    if first:
        xr, qkv, lse_t, o, a_low = got
        return xr, None, None, qkv, lse_t, o, a_low
    return got


def ff_fwd_kernel(layer, state_in, a_mine, a_theirs, ob, gain, shift, ub, own_up, own_down, *refs):
    moved, outs = refs[:5], refs[5:11]
    state, am, at_, hr, normed, recip, g, gp, f_low, wu, wd, sems = refs[11:]
    seq = state.shape[0]
    moves = Moves(sems)
    rows = 256
    tiles = [pl.ds(i * rows, rows) for i in range(seq // rows)]
    ins = ((state_in, state), (a_mine, am), (a_theirs, at_))
    row_waits = [[moves.start(src.at[at], dst.at[at]) for src, dst in ins] for at in tiles]
    up, down, n_t = fetch_ff(moves, layer, own_up, own_down, moved, wu, wd)
    up_waits = [up(k) for k in range(n_t)]
    down_waits = [down(k) for k in range(n_t)]
    half = wu.shape[1] // n_t
    for i, at in enumerate(tiles):
        wait_all(row_waits[i])
        entered = state[at].astype(f32)
        if layer:
            entered = entered * gain[layer - 1, 1:2] + shift[layer - 1, 1:2]
        z = entered + (am[at].astype(f32) + at_[at].astype(f32)) + ob[layer, 0:1]
        new, n, r = norm_forward(z, gain[layer, 0:1], shift[layer, 0:1])
        hr[at] = new.astype(bf16)
        normed[at] = n
        recip[at] = r
        for val, out in zip((hr, normed, recip), outs):
            moves.send(val.at[at], out.at[at])
    bias = jnp.concatenate([ub[k : k + 1] for k in range(ub.shape[0])], 1)
    for c in range(wu.shape[1] // CHUNK):
        cs = pl.ds(c * CHUNK, CHUNK)
        chunk_waits(up_waits, c, half)
        u = dot_nn(hr[...], wu[:, cs]) + bias[:, c * CHUNK : (c + 1) * CHUNK]
        phi = 0.5 * (1.0 + lax.erf(u * math.sqrt(0.5)))
        g[:, cs] = (u * phi).astype(bf16)
        gp[:, cs] = (phi + u * (jnp.exp(-0.5 * u * u) * (1.0 / math.sqrt(2 * math.pi)))).astype(bf16)
        moves.send(gp.at[:, cs], outs[4].at[:, cs])
    moves.send(g, outs[3])
    for copies in down_waits:
        wait_all(copies)
    for c in range(wd.shape[1] // CHUNK):
        cs = pl.ds(c * CHUNK, CHUNK)
        f_low[:, cs] = dot_nn(g[...], wd[:, cs]).astype(bf16)
        moves.send(f_low.at[:, cs], outs[5].at[:, cs])
    moves.finish()


def ff_fwd(layer, state, a_mine, a_theirs, norms, ub, own_up, own_down, moved):
    seq, width = state.shape
    n_t, half = ub.shape
    outs = [
        shape((seq, width), bf16),
        shape((seq, width), f32),
        shape((seq, 1), f32),
        shape((seq, n_t * half), bf16),
        shape((seq, n_t * half), bf16),
        shape((seq, width), bf16),
    ]
    return pl.pallas_call(
        functools.partial(ff_fwd_kernel, layer),
        out_shape=outs,
        in_specs=[ANY] * 3 + [VMEM] * 4 + [ANY] * 7,
        out_specs=[HBM] * len(outs),
        scratch_shapes=[pltpu.VMEM(v.shape, v.dtype) for v in (state, a_mine, a_theirs)]
        + [pltpu.VMEM(v.shape, v.dtype) for v in outs]
        + [
            pltpu.VMEM((width, n_t * half), bf16),
            pltpu.VMEM((n_t * half, width), bf16),
            pltpu.SemaphoreType.DMA((MOVES,)),
        ],
        compiler_params=params(56),
        cost_estimate=cost(8),
        name="ff_fwd",
    )(state, a_mine, a_theirs, *norms, ub, own_up, own_down, *moved)


def ff_bwd_kernel(last, layer, *refs):
    rows_in, refs = refs[:5], refs[5:]
    ob, gain, shift, gp_in, own_up, own_down = refs[:6]
    moved, refs = refs[6:11], refs[11:]
    n_out = 7 if last else 6
    outs, refs = refs[:n_out], refs[n_out:]
    bufs, gp, refs = refs[:5], refs[5], refs[6:]
    vals, refs = refs[:n_out], refs[n_out:]
    wu, wd, sems = refs
    dz2, dzr2, du, dh_low, small, ub_sum = vals[-6:]
    core, _, _ = here()
    seq = dz2.shape[0]
    moves = Moves(sems)
    rows = 256
    tiles = [pl.ds(i * rows, rows) for i in range(seq // rows)]
    if last:
        row_waits = [[moves.start(src.at[at], dst.at[at]) for src, dst in zip(rows_in[:3], bufs)] for at in tiles]
        cot_waits = [moves.start(src, dst) for src, dst in zip(rows_in[3:], bufs[3:])]
    else:
        row_waits = [[moves.start(src.at[at], dst.at[at]) for src, dst in zip(rows_in, bufs)] for at in tiles]
    up, down, n_t = fetch_ff(moves, layer, own_up, own_down, moved, wu, wd)
    half = wu.shape[1] // n_t
    down_waits, gp_waits = [], []
    for k in range(n_t):
        down_waits.append(down(k))
        for c in range(gp.shape[1] // CHUNK):
            if k * half <= c * CHUNK < (k + 1) * half:
                cs = pl.ds(c * CHUNK, CHUNK)
                gp_waits.append(moves.start(gp_in.at[:, cs], gp.at[:, cs]))
    up_waits = [up(k) for k in range(n_t)]
    small[...] = jnp.zeros_like(small)
    for i, at in enumerate(tiles):
        wait_all(row_waits[i])
        if last:
            h_in, f_mine, f_theirs, c_mine, c_theirs = bufs
            h = h_in[at] * gain[layer, 0:1] + shift[layer, 0:1]
            z = h + (f_mine[at].astype(f32) + f_theirs[at].astype(f32)) + ob[layer, 1:2]
            new, n, r = norm_forward(z, gain[layer, 1:2], shift[layer, 1:2])
            vals[0][at] = new.astype(bf16)
            if i == 0:
                wait_all(cot_waits)
            dy = jnp.where(core == i, c_mine[...], c_theirs[...]).astype(f32)
        else:
            dz_in, x_mine, x_theirs, normed, recip = bufs
            dy = dz_in[at] + (x_mine[at].astype(f32) + x_theirs[at].astype(f32))
            n, r = normed[at], recip[at]
        dz = norm_backward(dy, n, r, gain[layer, 1:2])
        dz2[at] = dz
        low = dz.astype(bf16)
        dzr2[at] = low
        if last:
            moves.send(vals[0].at[at], outs[0].at[at])
        moves.send(dz2.at[at], outs[-6].at[at])
        moves.send(dzr2.at[at], outs[-5].at[at])
        small[0:1] += jnp.sum(dy * n, 0, keepdims=True)
        small[1:2] += jnp.sum(dy, 0, keepdims=True)
        small[2:3] += jnp.sum(dz, 0, keepdims=True)
    for c in range(wd.shape[0] // CHUNK):
        cs = pl.ds(c * CHUNK, CHUNK)
        chunk_waits(down_waits, c, half)
        gp_waits[c].wait()
        back = (dot_nt(dzr2[...], wd[cs]) * gp[:, cs].astype(f32)).astype(bf16)
        du[:, cs] = back
        ub_sum[:, cs] = jnp.sum(back.astype(f32), 0, keepdims=True)
        moves.send(du.at[:, cs], outs[-4].at[:, cs])
    moves.send(small, outs[-2])
    moves.send(ub_sum, outs[-1])
    for copies in up_waits:
        wait_all(copies)
    for c in range(wu.shape[0] // CHUNK):
        cs = pl.ds(c * CHUNK, CHUNK)
        dh_low[:, cs] = dot_nt(du[...], wu[cs]).astype(bf16)
        moves.send(dh_low.at[:, cs], outs[-3].at[:, cs])
    moves.finish()


def ff_bwd(layer, rows_in, norms, gp, own_up, own_down, moved, last):
    width = own_up.shape[1]
    seq, wide = gp.shape
    outs = [
        shape((seq, width), f32),
        shape((seq, width), bf16),
        shape((seq, wide), bf16),
        shape((seq, width), bf16),
        shape((8, width), f32),
        shape((1, wide), f32),
    ]
    if last:
        outs = [shape((seq, width), bf16)] + outs
    return pl.pallas_call(
        functools.partial(ff_bwd_kernel, last, layer),
        out_shape=outs,
        in_specs=[ANY] * 5 + [VMEM] * 3 + [ANY] * 8,
        out_specs=[HBM] * len(outs),
        scratch_shapes=[pltpu.VMEM(v.shape, v.dtype) for v in (*rows_in, gp)]
        + [pltpu.VMEM(v.shape, v.dtype) for v in outs]
        + [
            pltpu.VMEM((width, wide), bf16),
            pltpu.VMEM((wide, width), bf16),
            pltpu.SemaphoreType.DMA((MOVES,)),
        ],
        compiler_params=params(56),
        cost_estimate=cost(9),
        name="ff_bwd",
    )(*rows_in, *norms, gp, own_up, own_down, *moved)


SEND = ((2, 3), (1, 3))
NEXT = (1, 2)


def ff_dw_kernel(z_first, *refs):
    ins, outs = refs[:4], refs[4:-8]
    g, du, hr, dzr2, su, sd, in_sems, sems = refs[-8:]
    _, place, z = here()
    n_t, width, half = su.shape
    part, rows = width // 4, half // 4

    def target(s, j):
        send, nxt, keep = outs[3 * s : 3 * s + 3]
        if j in SEND[s]:
            return send.at[SEND[s].index(j)]
        return nxt if j == NEXT[s] else keep

    def quarter(k):
        return lax.rem(z + n_t - k, n_t)

    copies = []

    def start(src, dst):
        copies.append(pltpu.make_async_copy(src, dst, sems.at[len(copies)]))
        copies[-1].start()

    moves = Moves(in_sems)
    pair = 2 * half
    hr_wait = moves.start(ins[2], hr)
    du_waits = [moves.start(ins[1].at[:, pl.ds(m * pair, pair)], du.at[:, pl.ds(m * pair, pair)]) for m in range(n_t // 2)]
    dzr2_wait = moves.start(ins[3], dzr2)
    g_waits = [moves.start(ins[0].at[:, pl.ds(m * pair, pair)], g.at[:, pl.ds(m * pair, pair)]) for m in range(n_t // 2)]
    hr_wait.wait()
    for m in range(n_t // 2):
        du_waits[m].wait()
        for c in range(width // CHUNK):
            at = pl.ds(c * CHUNK, CHUNK)
            got = dot_tn(hr[:, at], du[:, m * pair : (m + 1) * pair]).astype(bf16)
            for k in (2 * m, 2 * m + 1):
                su[k, at] = got[:, (k - 2 * m) * half : (k - 2 * m + 1) * half]
        if z_first:
            for k in (2 * m, 2 * m + 1):
                for p in range(4):
                    start(su.at[k, pl.ds(p * part, part)], outs[0].at[quarter(k), p, 0])
    if not z_first:
        for j in range(4):
            at = pl.ds(pl.multiple_of((j ^ place) * part, part), part)
            start(su.at[:, at], target(0, j))
    dzr2_wait.wait()
    for m in range(n_t // 2):
        g_waits[m].wait()
        for c in range(pair // CHUNK):
            at = pl.ds(m * pair + c * CHUNK, CHUNK)
            sd[at] = dot_tn(g[:, at], dzr2[...]).astype(bf16)
        if z_first:
            for k in (2 * m, 2 * m + 1):
                for p in range(4):
                    for n in range(2):
                        start(
                            sd.at[pl.ds(k * half + p * rows, rows), pl.ds(n * half, half)],
                            outs[0].at[quarter(k), p, 1, pl.ds(n * rows, rows)],
                        )
    if not z_first:
        for j in range(4):
            for k in range(n_t):
                at = pl.ds(pl.multiple_of(k * half + (j ^ place) * rows, rows), rows)
                for n in range(2):
                    start(sd.at[at, pl.ds(n * half, half)], target(1, j).at[k, pl.ds(n * rows, rows)])
    for c in copies:
        c.wait()


def ff_dw(g, du, hr, dzr2, z_first):
    width = hr.shape[1]
    half = width // 2
    n_t = g.shape[1] // half
    one = (n_t, width // 4, half)
    if z_first:
        outs = [shape((n_t, 4, 2, width // 4, half), bf16)]
    else:
        outs = [shape((2,) + one, bf16), shape(one, bf16), shape(one, bf16)] * 2
    return pl.pallas_call(
        functools.partial(ff_dw_kernel, z_first),
        out_shape=outs,
        in_specs=[ANY] * 4,
        out_specs=[HBM] * len(outs),
        scratch_shapes=[pltpu.VMEM(v.shape, v.dtype) for v in (g, du, hr, dzr2)]
        + [
            pltpu.VMEM((n_t, width, half), bf16),
            pltpu.VMEM((n_t * half, width), bf16),
            pltpu.SemaphoreType.DMA((2 + 2 * n_t,)),
            pltpu.SemaphoreType.DMA((12 * n_t,)),
        ],
        compiler_params=params(56),
        cost_estimate=cost(5),
        name="ff_dw",
    )(g, du, hr, dzr2)


def attn_bwd_kernel(layer, *refs):
    rows_in, refs = refs[:4], refs[4:]
    recip, gain, qkv_in, lse_t, o, mask_in, own_qkv, own_out = refs[:8]
    a_refs, b_refs, refs = refs[8:12], refs[12:16], refs[16:]
    outs, refs = refs[:5], refs[5:]
    bufs, refs = refs[:4], refs[4:]
    dz1, dzr1, d4, dx_low, small, qkv, mask, w, do, sems = refs
    dz2, h_mine, h_theirs, normed = bufs
    seq, width = dz1.shape
    moves = Moves(sems)
    half = seq // 2
    row_waits = []
    for i in range(2):
        at = pl.ds(i * half, half)
        row_waits.append([moves.start(src.at[at], dst.at[at]) for src, dst in zip(rows_in, bufs)])
    weight_waits = fetch_attn(moves, layer, own_qkv, own_out, a_refs, b_refs, w)
    qkv_wait = moves.start(qkv_in, qkv)
    mask_wait = moves.start(mask_in, mask)
    o_wait = moves.start(o, d4.at[3])
    small[...] = jnp.zeros_like(small)
    for i in range(seq // 128):
        if i * 128 % half == 0:
            wait_all(row_waits[i * 128 // half])
        at = pl.ds(i * 128, 128)
        dh = dz2[at] + (h_mine[at].astype(f32) + h_theirs[at].astype(f32))
        n = normed[at]
        dz = norm_backward(dh, n, recip[at], gain[layer, 0:1])
        dz1[at] = dz
        dzr1[at] = dz.astype(bf16)
        small[0:1] += jnp.sum(dh * n, 0, keepdims=True)
        small[1:2] += jnp.sum(dh, 0, keepdims=True)
        small[2:3] += jnp.sum(dz, 0, keepdims=True)
    moves.send(dz1, outs[0])
    moves.send(dzr1, outs[1])
    wait_all(weight_waits)
    rows = 256
    for i in range(seq // rows):
        at = pl.ds(i * rows, rows)
        do[at] = dot_nt(dzr1[at], w[3]).astype(bf16)
    qkv_wait.wait()
    mask_wait.wait()
    pairs = qkv.shape[2] // 128
    tile = 256
    scale = 1.0 / math.sqrt(HEAD_DIM)
    for g in range(pairs):
        cs = pl.ds(g * 128, 128)
        k2 = qkv[1, :, cs] * jnp.asarray(scale, bf16)
        v2 = qkv[2, :, cs]
        dv = dk = None
        for i in range(seq // tile):
            at = pl.ds(i * tile, tile)
            q2 = qkv[0, at, cs]
            do2 = do[at, cs]
            bias = mask[:, at]
            dq = None
            for hh in range(2):
                all_half = lane_half(seq, hh)
                tile_half = lane_half(tile, hh)
                km = jnp.where(all_half, k2, jnp.zeros_like(k2))
                vm = jnp.where(all_half, v2, jnp.zeros_like(v2))
                qm = jnp.where(tile_half, q2, jnp.zeros_like(q2))
                dom = jnp.where(tile_half, do2, jnp.zeros_like(do2))
                head = 2 * g + hh
                s = dot_nt(km, q2) + bias
                pr = jnp.exp(s - lse_t[head : head + 1, at])
                dp = dot_nt(vm, do2)
                delta = jnp.sum(pr * dp, 0, keepdims=True)
                ds = (pr * (dp - delta)).astype(bf16)
                got_v = dot_nn(pr.astype(bf16), dom)
                got_k = dot_nn(ds, qm)
                got_q = dot_nn(jnp.transpose(km), ds)
                dv = got_v if dv is None else dv + got_v
                dk = got_k if dk is None else dk + got_k
                dq = got_q if dq is None else dq + got_q
            dqr = jnp.transpose(dq)
            d4[0, at, cs] = dqr.astype(bf16)
        d4[1, :, cs] = (dk * scale).astype(bf16)
        d4[2, :, cs] = dv.astype(bf16)
    o_wait.wait()
    moves.send(d4, outs[2])
    wide = d4.shape[2]
    small[3:4, 0:wide] = jnp.sum(d4[0].astype(f32), 0, keepdims=True)
    small[3:4, wide : 2 * wide] = jnp.sum(d4[2].astype(f32), 0, keepdims=True)
    for i in range(seq // rows):
        at = pl.ds(i * rows, rows)
        acc = dot_nn(d4[0, at], w[0]) + dot_nn(d4[1, at], w[1]) + dot_nn(d4[2, at], w[2])
        dx_low[at] = acc.astype(bf16)
        moves.send(dx_low.at[at], outs[3].at[at])
    moves.send(small, outs[4])
    moves.finish()


def attn_bwd(layer, dz2, h_mine, h_theirs, normed, recip, gain, qkv, lse_t, o, mask, own_qkv, own_out, a_refs, b_refs):
    seq, width = dz2.shape
    wide = qkv.shape[2]
    outs = [
        shape((seq, width), f32),
        shape((seq, width), bf16),
        shape((4, seq, wide), bf16),
        shape((seq, width), bf16),
        shape((8, width), f32),
    ]
    rows_in = (dz2, h_mine, h_theirs, normed)
    return pl.pallas_call(
        functools.partial(attn_bwd_kernel, layer),
        out_shape=outs,
        in_specs=[ANY] * 4 + [VMEM] * 2 + [ANY, VMEM] + [ANY] * 12,
        out_specs=[HBM] * 5,
        scratch_shapes=[pltpu.VMEM(v.shape, v.dtype) for v in (*rows_in, *outs, qkv, mask)]
        + [
            pltpu.VMEM((4, wide, width), bf16),
            pltpu.VMEM((seq, wide), bf16),
            pltpu.SemaphoreType.DMA((MOVES,)),
        ],
        compiler_params=params(56),
        cost_estimate=cost(12),
        name="attn_bwd",
    )(*rows_in, recip, gain, qkv, lse_t, o, mask, own_qkv, own_out, *a_refs, *b_refs)


def attn_dw_kernel(*refs):
    ins, outs = refs[:3], refs[3:5]
    d4, right, full, sems = refs[5:]
    core, place, _ = here()
    cols = d4.shape[2] // SLOTS
    count, half = outs[0].shape[3:]
    moves = Moves(sems)
    waits = [moves.start(ins[1], right.at[0]), moves.start(ins[2], right.at[1])]
    d4_waits = [moves.start(ins[0].at[j ^ place], d4.at[j ^ place]) for j in range(4)]
    wait_all(waits)
    for j in range(4):
        t = j ^ place
        d4_waits[j].wait()
        full[j] = dot_tn(d4[t], right[t // 3]).astype(bf16)
        for s in range(SLOTS):
            for out, c in zip(outs, (core, 1 - core)):
                at = pl.ds(pl.multiple_of(s * cols + c * count, count), count)
                for n in range(2):
                    moves.send(full.at[j, at, pl.ds(n * half, half)], out.at[s, j, n])
    moves.finish()


def attn_dw(d4, xr, dzr1):
    wide, width = d4.shape[2], xr.shape[1]
    out = shape((SLOTS, 4, 2, wide // 4, width // 2), bf16)
    return pl.pallas_call(
        attn_dw_kernel,
        out_shape=[out, out],
        in_specs=[ANY] * 3,
        out_specs=[HBM] * 2,
        scratch_shapes=[
            pltpu.VMEM(d4.shape, bf16),
            pltpu.VMEM((2,) + xr.shape, bf16),
            pltpu.VMEM((4, wide, width), bf16),
            pltpu.SemaphoreType.DMA((MOVES,)),
        ],
        compiler_params=params(56),
        cost_estimate=cost(3.5),
        name="attn_dw",
    )(d4, xr, dzr1)


def arrange_kernel(mine, theirs, *outs):
    first = here()[0] == 0
    for ref, same in ((mine, first), (theirs, jnp.logical_not(first))):
        for s in range(SLOTS):
            k = jnp.where(same, s, 3 - s)
            for n in range(2):
                send, nxt, keep = outs[3 * n : 3 * n + 3]
                for j in range(4):
                    val = ref[s, j, n]
                    if j in SEND[n]:
                        send[SEND[n].index(j), k] = val
                    elif j == NEXT[n]:
                        nxt[k] = val
                    else:
                        keep[k] = val


def low_sum(*parts):
    total = parts[0].astype(f32)
    for v in parts[1:]:
        total = total + v.astype(f32)
    return total.astype(bf16)


def small_call(kernel, outs, us, name, *ins):
    n, m = len(ins), len(outs)

    def body(*refs):
        bufs, sems = refs[n + m : -1], refs[-1]
        copies = [pltpu.make_async_copy(src, dst, sems.at[i]) for i, (src, dst) in enumerate(zip(refs[:n], bufs))]
        for c in copies:
            c.start()
        for c in copies:
            c.wait()
        kernel(*bufs, *refs[n : n + m])

    return pl.pallas_call(
        body,
        out_shape=outs,
        in_specs=[ANY] * n,
        out_specs=[VMEM] * m,
        scratch_shapes=[pltpu.VMEM(v.shape, v.dtype) for v in ins] + [pltpu.SemaphoreType.DMA((n,))],
        compiler_params=params(16),
        cost_estimate=cost(us * 0.01),
        name=name,
    )(*ins)


def second_kernel(nxt_a, got_a, nxt_b, got_b, out_a, out_b):
    out_a[...] = low_sum(nxt_a[...], got_a[1])
    out_b[...] = low_sum(nxt_b[...], got_b[1])


def third_kernel(*refs):
    out = refs[-1]
    n_t = out.shape[0]
    z = here()[2]
    row = 0
    for c in range(len(refs) // 6):
        ins = refs[6 * c : 6 * c + 6]
        rows = ins[0].shape[1]
        for n in range(2):
            keep, got, more = ins[3 * n : 3 * n + 3]
            for k in range(n_t):
                q = lax.rem(z + n_t - k, n_t)
                out[q, n, row : row + rows] = low_sum(keep[k], got[0, k], more[k])
        row += rows


def merge_kernel(keep_a, got_a, more_a, keep_b, got_b, more_b, attn, out):
    rows = keep_a.shape[1]
    out[0, :rows] = low_sum(keep_a[0], got_a[0, 0], more_a[0])
    out[1, :rows] = low_sum(keep_b[0], got_b[0, 0], more_b[0])
    out[:, rows:] = attn[...]


def split_kernel(every, *outs):
    _, place, _ = here()
    for s in range(SLOTS):
        send, nxt, keep = outs[3 * s : 3 * s + 3]
        for j in range(4):
            val = every[j ^ place, s]
            if j in SEND[s]:
                send[SEND[s].index(j), 0] = val
            elif j == NEXT[s]:
                nxt[0] = val
            else:
                keep[0] = val


def pick_kernel(every, out, ub):
    n_t, rows = every.shape[0], out.shape[2]
    z = here()[2]
    for k in range(n_t):
        q = lax.rem(z + n_t - k, n_t)
        ub[k : k + 1] = jnp.sum(every[q, 2 * rows : 2 * rows + 3].astype(f32), 0, keepdims=True)
        if k:
            for n in range(2):
                out[n, k - 1] = every[q, n * rows : (n + 1) * rows]


def pack_kernel(*refs):
    out = refs[-1]
    layers = (len(refs) - 1) // 3
    small1, small2, ub = refs[:layers], refs[layers : 2 * layers], refs[2 * layers : 3 * layers]
    core, _, z = here()
    half = out.shape[1] // 2
    n_t = ub[0].shape[1] // half
    cols = half // 2
    once = jnp.where(core == 0, 1.0, 0.0).astype(f32)
    for l in range(layers):
        out[6 * l : 6 * l + 3] = small1[l][0:3] * once
        out[6 * l + 3 : 6 * l + 6] = small2[l][0:3] * once
    none = jnp.zeros((1, half), f32)
    for l in range(layers):
        for q in range(n_t):
            row = none
            for k in range(n_t):
                row = jnp.where(lax.rem(z + n_t - k, n_t) == q, ub[l][:, k * half : (k + 1) * half], row)
            left = jnp.where(core == 0, row, none)
            out[6 * layers + n_t * l + q : 6 * layers + n_t * l + q + 1] = jnp.concatenate([left, row - left], 1)
    slot_k = (jnp.where(core == 0, 0, 3), jnp.where(core == 0, 1, 2))
    none = jnp.zeros((1, cols), f32)
    for q in range(n_t):
        parts = []
        for l in range(layers):
            for i in range(2):
                row = none
                for s in range(SLOTS):
                    at = i * half + s * cols
                    here_q = lax.rem(z + n_t - slot_k[s], n_t) == q
                    row = jnp.where(here_q, small1[l][3:4, at : at + cols], row)
                parts.append(row)
        at = (6 + n_t) * layers + q
        out[at : at + 1] = jnp.concatenate(parts, 1)


def unpack_kernel(flat, gain, shift, bias, up, qv):
    layers, _, cols = qv.shape
    n_t = (flat.shape[0] - 6 * layers) // (layers + 1)
    z = here()[2]

    def own(first):
        row = flat[first : first + 1]
        for q in range(1, n_t):
            row = jnp.where(z == q, flat[first + q : first + q + 1], row)
        return row

    row = own((6 + n_t) * layers)
    for l in range(layers):
        for n in range(2):
            at = 6 * l + 3 * n
            gain[l, n : n + 1] = flat[at : at + 1]
            shift[l, n : n + 1] = flat[at + 1 : at + 2]
            bias[l, n : n + 1] = flat[at + 2 : at + 3]
            qv[l, n : n + 1] = row[:, (2 * l + n) * cols : (2 * l + n + 1) * cols]
        up[l : l + 1] = own(6 * layers + n_t * l)


def out_kernel(layer, n_alias, *refs):
    mine, theirs = refs[:4], refs[4:8]
    up, down, qkv, out, wide, sems = refs[8 + n_alias :]
    core, place, _ = here()
    part, half, cols = up.shape[1] // 4, up.shape[2] // 2, out.shape[1]
    rows, count = half // 4, cols // 2
    copies = []

    def start(src, dst):
        copies.append(pltpu.make_async_copy(src, dst, sems.at[len(copies)]))
        copies[-1].start()

    for n, (pieces, c) in enumerate(((mine, core), (theirs, 1 - core))):
        off = pl.multiple_of(c * half, half)
        for j, ref in enumerate(pieces):
            p = j ^ place
            buf = wide.at[n, j]
            buf[...] = ref[...].astype(f32)
            start(buf.at[0, pl.ds(0, part)], up.at[layer, pl.ds(pl.multiple_of(p * part, part), part), pl.ds(off, half)])
            for m in range(2):
                lanes = pl.ds(m * half, half)
                at = pl.ds(pl.multiple_of(c * half + p * rows, rows), rows)
                start(buf.at[1, pl.ds(m * rows, rows)], down.at[layer, at, lanes])
                src, sem = buf.at[m, pl.ds(part, count)], sems.at[len(copies)]
                at = pl.ds(pl.multiple_of(c * count, count), count)
                to_qkv = pltpu.make_async_copy(src, qkv.at[layer, jnp.minimum(p, 2), at, lanes], sem)
                to_out = pltpu.make_async_copy(src, out.at[layer, at, lanes], sem)

                @pl.when(p < 3)
                def _(to_qkv=to_qkv):
                    to_qkv.start()

                @pl.when(p == 3)
                def _(to_out=to_out):
                    to_out.start()

                copies.append(to_out)
    for c in copies:
        c.wait()


def outputs(layer, dims, mine, theirs, before):
    before = list(before or [])
    n = len(mine) + len(theirs)
    return pl.pallas_call(
        functools.partial(out_kernel, layer, len(before)),
        out_shape=[shape(d, f32) for d in dims],
        in_specs=[VMEM] * n + [HBM] * len(before),
        out_specs=[HBM] * len(dims),
        scratch_shapes=[
            pltpu.VMEM((2, 4) + mine[0].shape, f32),
            pltpu.SemaphoreType.DMA((5 * n,)),
        ],
        input_output_aliases={n + i: i for i in range(len(before))},
        compiler_params=params(24),
        cost_estimate=cost(4),
        name="gradients_out",
    )(*mine, *theirs, *before)


def after(v, *others):
    return lax.optimization_barrier((v, *others))[0]


def local(
    block_input,
    w_qkv,
    qv_bias,
    w_out,
    out_bias,
    w_up,
    up_bias,
    w_down,
    norm_gain,
    norm_shift,
    segment_ids,
    slot_counts,
    cotangent,
):
    layers, width, _, cols = w_qkv.shape
    hidden = w_up.shape[2]
    seq = segment_ids.shape[1]
    n_dp, n_t = lax.axis_size("dp"), lax.axis_size("tensor")
    dp, z = lax.axis_index("dp"), lax.axis_index("tensor")
    core, place = dp & 1, (dp >> 1) & 3
    first = core == 0
    part, half = hidden // 4, hidden // 2
    norms_in = (out_bias, norm_gain, norm_shift)

    def send(v, axis, pairs, name):
        with jax.named_scope(name):
            return lax.ppermute(v, axis, pairs)

    def flip(v, bits, name, odd=False):
        return send(v, "dp", [(i, i ^ bits) for i in range(n_dp) if not odd or i & 1], name)

    def across(v, name):
        return flip(v, 1, name)

    def shift(v, by, name):
        pairs = []
        for i in range(n_dp):
            move = by[i & 1]
            if move:
                pairs += [(i * n_t + k, i * n_t + (k + move) % n_t) for k in range(n_t)]
        return send(v, ("dp", "tensor"), pairs, name)

    def swap(v, name):
        pairs = []
        for i in range(n_dp):
            for k in range(n_t):
                if (i & 1) != (k & 1):
                    pairs.append((i * n_t + k, (i ^ 1) * n_t + (k ^ 1)))
        moved = send(v, ("dp", "tensor"), pairs, name)
        return jnp.where(core == (z & 1), v, moved)

    own_qkv = jnp.transpose(w_qkv, (0, 2, 3, 1))
    own_bias = qv_bias.reshape(1, -1)

    def attn_over_z(piece, l):
        return shift(piece, (1, 2), f"attn{l}_z_b"), shift(piece, (0, 3), f"attn{l}_z_a")

    def attn_over_xy(b, a, l, *late):
        name = f"attn{l}_"
        bx = flip(b, 2, name + "b_x")
        by = flip(b, 4, name + "b_y")
        ay = flip(a, 4, name + "a_y", True)
        ax = flip(a, 2, name + "a_x", True)
        bd = flip(after(bx, *late), 4, name + "b_xy")
        ad = flip(after(ay, *late), 2, name + "a_yx", True)
        return (a, ax, ay, ad), (b, bx, by, bd)

    def ff_over_xy(own, l):
        x, y = flip(own, 2, f"ff{l}_x"), flip(own, 4, f"ff{l}_y")
        return own, x, y, flip(x[0], 4, f"ff{l}_xy"), flip(y[1], 2, f"ff{l}_yx")

    x_mine = swap(block_input, "x_swap")
    attn_piece, ff_piece, packed = prepare(own_qkv, w_out, w_up, w_down, up_bias, own_bias, segment_ids, slot_counts)
    mask, mask_t = masks(packed, across(packed, "seg"))
    x_theirs = across(x_mine, "x_across")

    def ff_over_z(l, *late):
        with jax.named_scope(f"ff{l}_z"):
            return lax.all_gather(after(ff_piece[l], *late), "tensor", axis=0)

    def take(every, l, *late):
        outs = [shape((2, n_t - 1, part, half), bf16), shape((n_t, half), f32)]
        own, ub = small_call(pick_kernel, outs, 1.5, "pick_quarters", after(every, *late))
        return ff_over_xy(own, l), ub

    attn0_z = attn_over_z(attn_piece[0], 0)
    ff0_z = ff_over_z(0, x_mine)
    attn0 = attn_over_xy(after(attn0_z[0], mask, x_mine), after(attn0_z[1], mask, x_mine), 0, x_theirs)
    attn1_z = attn_over_z(after(attn_piece[1], *attn0[0], *attn0[1]), 1)
    ff1_z = ff_over_z(1, *attn1_z)
    ff0, ub0 = take(ff0_z, 0, *attn0[0], *attn0[1])
    attn1 = attn_over_xy(*attn1_z, 1)
    attn_w, ff_z = [attn0, attn1], [ff0_z, ff1_z]
    bias = (own_bias,) + attn0_z[::-1]

    rows_in = (after(x_mine, ff0[0]), x_theirs)
    saved = []
    ff_w, ubs = [ff0], [ub0]
    for l in range(layers):
        xr, n2, r2, qkv, lse_t, o, a_low = attn_fwd(l, rows_in, mask, bias, own_qkv, w_out, *attn_w[l])
        state = n2 if l else xr
        if l:
            saved[l - 1] += (n2, r2)
        else:
            ff1, ub1 = take(ff1_z, 1, *ff0)
            ff_w.append(ff1)
            ubs.append(ub1)
            state = after(state, ff1[0], *attn1[0], *attn1[1])
        hr, n1, r1, g, gp, f_low = ff_fwd(
            l, state, a_low, across(a_low, f"a{l}"), norms_in, ubs[l], w_up, w_down, ff_w[l]
        )
        saved.append((xr, qkv, lse_t, o, hr, n1, r1, g, gp))
        rows_in = (after(n1, ff1[1], ff1[2]), f_low, across(f_low, f"f{l}")) + norms_in

    class Sums:
        def __init__(self, name):
            self.name = name

        def first(self, pieces):
            self.pieces = pieces
            self.got = (flip(pieces[0], 4, self.name + "_1a"), flip(pieces[3], 2, self.name + "_1b"))
            return self

        def second(self, *late):
            p, got = self.pieces, self.got
            nxt = after(p[1], *late)
            outs = [shape(nxt.shape, bf16)] * 2
            self.sec = small_call(second_kernel, outs, 1.2, "add_second", nxt, got[0], p[4], got[1])
            self.more = (flip(self.sec[0], 2, self.name + "_2a"), flip(self.sec[1], 4, self.name + "_2b"))
            return self

        def parts(self):
            p, got, more = self.pieces, self.got, self.more
            return [p[2], got[0], more[0], p[5], got[1], more[1]]

    def over_z(every):
        with jax.named_scope("sums_z"):
            return lax.psum_scatter(every, "tensor", scatter_dimension=0)

    def third(chunks, *late):
        ins = [v for c in chunks for v in c.parts()]
        rows = sum(c.pieces[2].shape[1] for c in chunks)
        outs = [shape((n_t, 2, rows, half), bf16)]
        (every,) = small_call(third_kernel, outs, 1.5, "add_third", after(ins[0], *late), *ins[1:])
        return every, over_z(every)

    def attn_first(name, mine, theirs):
        one = (n_t, cols // 2, half)
        outs = [shape((2,) + one, bf16), shape(one, bf16), shape(one, bf16)] * 2
        return Sums(name).first(small_call(arrange_kernel, outs, 1.5, "arrange", mine, theirs))

    def split(total, *late):
        one = (1, part, half)
        outs = [shape((2,) + one, bf16), shape(one, bf16), shape(one, bf16)] * 2
        return Sums("gf1").first(small_call(split_kernel, outs, 1.5, "split_pieces", after(total, *late)))

    def spread(total, name):
        bits = 8
        while bits < n_dp:
            total = low_sum(total, flip(total, bits, name + "_rest"))
            bits *= 2
        mine = [total] + [flip(total, bits, f"{name}_c{bits}") for bits in (2, 4, 6)]
        return mine, [across(v, f"{name}_cc{n}") for n, v in enumerate(mine)]

    def finish(l, mine, theirs, before, *late):
        dims = [(layers, width, hidden), (layers, hidden, width), (layers, 3, cols, width), (layers, cols, width)]
        return outputs(l, dims, [after(mine[0], *late)] + mine[1:], theirs, before)

    a1 = None
    smalls = []
    for l in reversed(range(layers)):
        last = l == layers - 1
        xr, qkv, lse_t, o, hr, n1, r1, g, gp = saved[l][:9]
        if last:
            c_mine = swap(cotangent, "cot_swap")
            ff_rows = rows_in[:3] + (c_mine, across(c_mine, "cot_across"))
        else:
            ff_rows = (dz1, dx_low, across(dx_low, f"dx{l}")) + saved[l][9:]
        got = ff_bwd(l, ff_rows, norms_in, gp, w_up, w_down, ff_w[l], last)
        if last:
            out_half = lax.dynamic_slice_in_dim(got[0], core * (seq // 2), seq // 2, 0)
            got = got[1:]
        dz2, dzr2, du, dh_low, small2, ub_sum = got
        if a1:
            a1.second(dzr2)
            dzr2 = after(dzr2, *a1.sec)
        ff_pieces = ff_dw(g, du, hr, dzr2, last)
        if last:
            f1_total = over_z(ff_pieces[0])
        else:
            first_out = [after(ff_pieces[0], *a1.more), *ff_pieces[1:3], after(ff_pieces[3], *a1.more), *ff_pieces[4:]]
            f0 = Sums("gf0").first(first_out)
        dh_theirs = across(dh_low, f"dh{l}")
        dz2 = after(dz2, ff_pieces[0])
        if a1:
            dz2 = after(dz2, *a1.more)
        dz1, dzr1, d4, dx_low, small1 = attn_bwd(
            l, dz2, dh_low, dh_theirs, n1, r1, norm_gain, qkv, lse_t, o, mask_t, own_qkv, w_out, *attn_w[l]
        )
        at_pieces = attn_dw(d4, xr, dzr1)
        at_theirs = across(at_pieces[1], f"ga{l}_core")
        if last:
            a1 = attn_first("ga1", at_pieces[0], at_theirs)
            dz1 = after(dz1, a1.pieces[0])
        smalls.append((small1, small2, ub_sum))
    smalls = smalls[::-1]

    dx = dz1 + (dx_low.astype(f32) + across(dx_low, "dx_last").astype(f32))
    input_grad = swap(lax.dynamic_slice_in_dim(dx, core * (seq // 2), seq // 2, 0), "grad_swap")

    def more_flat(flat, axis, bits, *late):
        n = lax.axis_size(axis)
        return flat + send(after(flat, *late), axis, [(i, i ^ bits) for i in range(n)], f"flat_{axis}{bits}")

    n_rows = (6 + n_t) * layers + n_t
    (flat,) = small_call(
        pack_kernel,
        [shape((n_rows, width), f32)],
        1.5,
        "pack_small",
        *[g[0] for g in smalls],
        *[g[1] for g in smalls],
        *[g[2] for g in smalls],
    )
    f0.second(at_pieces[0], dx)
    mixed = swap(after(out_half, *f0.sec), "mixed_swap")
    a0 = attn_first("ga0", after(at_pieces[0], *f0.sec), at_theirs)
    a1_every, a1_total = third([a1], a0.pieces[0])
    flat = more_flat(flat, "dp", 1, a1_every)
    a0.second(flat)
    flat = more_flat(flat, "dp", 2, *a0.sec)
    l0_every, l0_total = third([f0, a0], flat, input_grad, mixed)
    f1 = split(f1_total, l0_every)
    flat = more_flat(flat, "dp", 4, f1.pieces[0])
    bits = 8
    while bits < n_dp:
        flat = more_flat(flat, "dp", bits)
        bits *= 2
    f1.second(flat)
    flat = more_flat(flat, "tensor", 1, *f1.sec)
    ins = f1.parts()
    ins[0] = after(ins[0], flat)
    (l1_total,) = small_call(merge_kernel, [shape((2, part + cols // 2, half), bf16)], 1.5, "merge", *ins, a1_total)
    flat = more_flat(flat, "tensor", 2, l1_total)
    l1 = spread(l1_total, "l1")
    l0 = spread(after(l0_total, *l1[0]), "l0")
    grads = finish(1, *l1, None, l0_total, flat)
    grads = finish(0, *l0, grads)
    grad_gain, grad_shift, grad_out_bias, grad_up_bias, grad_qv_bias = small_call(
        unpack_kernel,
        [shape((layers, 2, width), f32)] * 3 + [shape((layers, hidden), f32), shape((layers, 2, cols), f32)],
        1.5,
        "unpack_small",
        flat,
    )
    return (
        mixed,
        input_grad,
        jnp.transpose(grads[2], (0, 3, 1, 2)),
        grad_qv_bias,
        grads[3],
        grad_out_bias,
        grads[0],
        grad_up_bias,
        grads[1],
        grad_gain,
        grad_shift,
    )


def solution(mesh):
    placed = (
        P(("dp", "tensor"), None),
        P(None, None, None, "tensor"),
        P(None, None, "tensor"),
        P(None, "tensor", None),
        P(),
        P(None, None, "tensor"),
        P(None, "tensor"),
        P(None, "tensor", None),
        P(),
        P(),
        P("dp", None),
        P("dp"),
        P(("dp", "tensor"), None),
    )
    return jax.shard_map(
        local,
        mesh=mesh,
        in_specs=placed,
        out_specs=(
            P(("dp", "tensor"), None),
            P(("dp", "tensor"), None),
            P(None, None, None, "tensor"),
            P(None, None, "tensor"),
            P(None, "tensor", None),
            P(),
            P(None, None, "tensor"),
            P(None, "tensor"),
            P(None, "tensor", None),
            P(),
            P(),
        ),
        check_vma=False,
    )
```

time: 667 us -> 435 us (0.65)
  Pallas kernels: 0 us -> 143 us
  other arithmetic: 118 us -> 5.88 us
  matrix products: 86 us -> 0 us
  local copies, waits for them, and re-layouts: 108 us -> 28.3 us
  starting transfers between devices: 144 us -> 96.5 us
  waiting for transfers between devices: 178 us -> 141 us
  blocking collectives: 21.7 us -> 0 us
  between operations: 4.1 us -> 15.2 us
    pallas_call x0 -> x30, Pallas kernels: none -> 143 us  [the longest x2 28.9 us: attn_bwd(): pl.pallas_call(functools.partial(attn_bwd_kernel, layer), out_shape=outs,...]
    dot_general x38 -> x0, matrix products: 86 us -> none  [the longest x8 31.3 us: dot_nt(): lax.dot_general(left, right, (((1,), (1,)), ((), ())), preferred_element_...]
    ppermute x101 -> x76, starting transfers between devices: 144 us -> 96.3 us  [send(): return lax.ppermute(v, axis, pairs)]
    ppermute x101 -> x76, waiting for transfers between devices: 178 us -> 140 us  [send(): return lax.ppermute(v, axis, pairs)]
    select_n x24 -> x0, other arithmetic: 26.6 us -> none  [the longest x10 16.8 us: in_core_order(): jnp.where(first, jnp.concatenate([mine, theirs], axis), jnp.concatenate([...]
    gather x17 -> x0, local copies, waits for them, and re-layouts: 25.8 us -> none  [the longest x2 5.99 us: local(): both = jnp.take(both, order, axis=1)]
    slice x43 -> x0, local copies, waits for them, and re-layouts: 23.4 us -> none  [the longest x2 4.48 us: reduce_pieces(): b = add_low(b[:, 0::2], rb)]
    convert_element_type x25 -> x0, other arithmetic: 22.9 us -> none  [the longest x16 13.3 us: add_low(): return (a.astype(f32) + b.astype(f32)).astype(bf16)]
  transfers between devices with their start and end apart: 101 -> 81, of which waited for: 40 -> 29; matrix products, arithmetic and copies ran while one was open for 42% -> 2% of each run, Pallas kernels for 0% -> 25%
where the time goes in v3:
time: 435 us; the launch traced here: 429 us
  Pallas kernels  143 us (33%)
  waiting for transfers between devices  141 us (32%)
  starting transfers between devices  96.5 us (22%)
  local copies, waits for them, and re-layouts  28.3 us (7%)
  between operations  15.2 us (3%)
  other arithmetic  5.88 us (1%)
    ppermute x76, waiting for transfers between devices, send(): return lax.ppermute(v, axis, pairs)  140 us
    ppermute x76, starting transfers between devices, send(): return lax.ppermute(v, axis, pairs)  96.3 us
    pallas_call x2, Pallas kernels, attn_bwd(): pl.pallas_call(functools.partial(attn_bwd_kernel, layer), out_shape=outs,...  28.9 us
    pallas_call x2, Pallas kernels, attn_fwd(): pl.pallas_call(functools.partial(attn_fwd_kernel, layer), out_shape=outs,...  25.3 us
    unnamed x166, local copies, waits for them, and re-layouts  24.4 us
    pallas_call x2, Pallas kernels, ff_bwd(): pl.pallas_call(functools.partial(ff_bwd_kernel, last, layer), out_shape=o...  21.6 us
    pallas_call x2, Pallas kernels, ff_fwd(): pl.pallas_call(functools.partial(ff_fwd_kernel, layer), out_shape=outs, i...  18.8 us
    pallas_call x2, Pallas kernels, ff_dw(): pl.pallas_call(functools.partial(ff_dw_kernel, z_first), out_shape=outs,...  13.6 us
  transfers between devices with their start and end apart: 81, of which 29 were waited for; matrix products, arithmetic and copies ran while one was open for 2% of the time, Pallas kernels for 25%

profile of v3, /device:TPU:0, one launch (start us, length us, event | category | flops | bytes accessed | tf_op | source)
XLA Modules:
  0.0 429.4 jit_solution(5415093761895058464)
XLA Ops:
  9.3 3.2 prepare.1
  13.3 7.1 %collective-permute-start.7 = (bf16[208,768]{1,0:T(8,128)(2,1)}, bf16[208,768]{1,0:T(8,128)(2,1)S(1)}, u32[]{:S(2)}, u32[]{:S(2)}) collective-permute-start(bf16[208,768]{1,0:T(8,128)(2,1)} %get-tuple-element.157), channel_id=1, source_target_pairs={{0,1},{1,2},{2,3},{3,0},{4,6},{5,7},{6,4},{7,5},{8,9},{9,10},{10,1... | collective-permute-start | bytes 958472 | tf_op jit(solution)/shard_map/attn0_z_b/ppermute | solution.py:1109
  20.4 1.9 collective-permute-start.2
  27.2 3.3 collective-permute-done.7.refs_5_.refs_12_.refs_9_.refs_16_
  32.7 1.6 collective-permute-start.9
  35.0 2.5 collective-permute-done.8.refs_13_.refs_17_
  40.1 4.4 %collective-permute-done.10.refs_15_.refs_19_ = bf16[208,768]{1,0:T(8,128)(2,1)S(1)} collective-permute-done((bf16[208,768]{1,0:T(8,128)(2,1)S(1)}, bf16[208,768]{1,0:T(8,128)(2,1)S(1)}, u32[]{:S(2)}, u32[]{:S(2)}) %collective-permute-start.10) | collective-permute-done | bytes 319520 | tf_op jit(solution)/shard_map/attn0_b_xy/ppermute | solution.py:1109
  45.9 9.8 %collective-permute-start.11 = (bf16[192,768]{1,0:T(8,128)(2,1)S(1)}, bf16[192,768]{1,0:T(8,128)(2,1)}, u32[]{:S(2)}, u32[]{:S(2)}) collective-permute-start(bf16[192,768]{1,0:T(8,128)(2,1)S(1)} %copy-done.82), channel_id=1, source_target_pairs={{0,1},{1,2},{2,3},{3,0},{4,6},{5,7},{6,4},{7,5},{8,9},{9,10},{10,1... | collective-permute-start | bytes 884744 | tf_op jit(solution)/shard_map/attn1_z_b/ppermute | solution.py:1109
  55.7 4.2 collective-permute-done.11.refs_16_
  66.0 12.3 %attn_fwd.2 = (bf16[512,768]{1,0:T(8,128)(2,1)}, bf16[3,512,384]{2,1,0:T(8,128)(2,1)}, f32[8,512]{1,0:T(8,128)}, bf16[512,384]{1,0:T(8,128)(2,1)}, bf16[512,768]{1,0:T(8,128)(2,1)}) custom-call(bf16[256,768]{1,0:T(8,128)(2,1)} %copy-done.52, bf16[256,768]{1,0:T(8,128)(2,1)} %copy-done.72, f32[1,768]{1,0:T(1,128)} %reshape.25.qv_bias.refs_2_.refs_6_, ...), custom_call_target="tpu_custom_call" | custom-call | flops 11000000512 | bytes 36000000 | tf_op jit(solution)/shard_map/attn_fwd/pallas_call | solution.py:394
  78.3 15.0 %collective-permute-start.23 = (bf16[512,768]{1,0:T(8,128)(2,1)}, bf16[512,768]{1,0:T(8,128)(2,1)S(1)}, u32[]{:S(2)}, u32[]{:S(2)}) collective-permute-start(bf16[512,768]{1,0:T(8,128)(2,1)} %get-tuple-element.175.a_mine), channel_id=1, source_target_pairs={{0,4},{4,0},{8,12},{12,8},{16,20},{20,16},{24,28},{28,24},{1,5},{5... | collective-permute-start | bytes 2359304 | tf_op jit(solution)/shard_map/a0/ppermute | solution.py:1109
  99.2 12.7 %collective-permute-done.20.refs_17_ = bf16[192,768]{1,0:T(8,128)(2,1)} collective-permute-done((bf16[192,768]{1,0:T(8,128)(2,1)}, bf16[192,768]{1,0:T(8,128)(2,1)}, u32[]{:S(2)}, u32[]{:S(2)}) %collective-permute-start.20) | collective-permute-done | bytes 294944 | tf_op jit(solution)/shard_map/attn1_b_x/ppermute | solution.py:1109
  118.8 3.2 collective-permute-done.21.refs_18_
  122.9 5.4 %collective-permute-done.22.refs_19_ = bf16[192,768]{1,0:T(8,128)(2,1)} collective-permute-done((bf16[192,768]{1,0:T(8,128)(2,1)}, bf16[192,768]{1,0:T(8,128)(2,1)}, u32[]{:S(2)}, u32[]{:S(2)}) %collective-permute-start.22) | collective-permute-done | bytes 294944 | tf_op jit(solution)/shard_map/attn1_b_xy/ppermute | solution.py:1109
  129.3 9.3 %ff_fwd.2 = (bf16[512,768]{1,0:T(8,128)(2,1)}, f32[512,768]{1,0:T(8,128)}, f32[512,1]{1,0:T(8,128)}, bf16[512,1536]{1,0:T(8,128)(2,1)}, bf16[512,1536]{1,0:T(8,128)(2,1)}, /*index=5*/bf16[512,768]{1,0:T(8,128)(2,1)}) custom-call(bf16[512,768]{1,0:T(8,128)(2,1)} %get-tuple-element.174.state_in.refs_1_, bf16[512,768]{1,0:T(8,128)(2,1)} %get-tuple-element.175.a_mine, ...), custom_call_target="tpu_custom_call" | custom-call | flops 8800000000 | bytes 28800000 | tf_op jit(solution)/shard_map/ff_fwd/pallas_call | solution.py:473
  138.7 8.2 %collective-permute-done.25.refs_2_.refs_13_ = bf16[2,3,192,384]{3,2,1,0:T(8,128)(2,1)S(1)} collective-permute-done((bf16[2,3,192,384]{3,2,1,0:T(8,128)(2,1)S(1)}, bf16[2,3,192,384]{3,2,1,0:T(8,128)(2,1)S(1)}, u32[]{:S(2)}, u32[]{:S(2)}) %collective-permute-start.25) | collective-permute-done | bytes 884768 | tf_op jit(solution)/shard_map/ff1_y/ppermute | solution.py:1109
  147.8 13.0 %attn_fwd.3 = (bf16[512,768]{1,0:T(8,128)(2,1)}, f32[512,768]{1,0:T(8,128)}, f32[512,1]{1,0:T(8,128)}, bf16[3,512,384]{2,1,0:T(8,128)(2,1)}, f32[8,512]{1,0:T(8,...) custom-call(f32[512,768]{1,0:T(8,128)} %get-tuple-element.178.refs_0_.refs_3_, ...), custom_call_target="tpu_custom_call" | custom-call | flops 11000000512 | bytes 36000000 | tf_op jit(solution)/shard_map/attn_fwd/pallas_call | solution.py:394
  164.3 9.3 %collective-permute-done.29.refs_4_.refs_15_ = bf16[3,192,384]{2,1,0:T(8,128)(2,1)S(1)} collective-permute-done((bf16[3,192,384]{2,1,0:T(8,128)(2,1)S(1)}, bf16[3,192,384]{2,1,0:T(8,128)(2,1)S(1)}, u32[]{:S(2)}, u32[]{:S(2)}) %collective-permute-start.29) | collective-permute-done | bytes 442400 | tf_op jit(solution)/shard_map/ff1_yx/ppermute | solution.py:1109
  175.4 9.5 %ff_fwd.3 = (bf16[512,768]{1,0:T(8,128)(2,1)}, f32[512,768]{1,0:T(8,128)}, f32[512,1]{1,0:T(8,128)}, bf16[512,1536]{1,0:T(8,128)(2,1)}, bf16[512,1536]{1,0:T(8,128)(2,1)}, /*index=5*/bf16[512,768]{1,0:T(8,128)(2,1)}) custom-call(f32[512,768]{1,0:T(8,128)} %get-tuple-element.180.state_in.refs_3_, bf16[512,768]{1,0:T(8,128)(2,1)} %get-tuple-element.181.a_mine, ...), custom_call_target="tpu_custom_call" | custom-call | flops 8800000000 | bytes 28800000 | tf_op jit(solution)/shard_map/ff_fwd/pallas_call | solution.py:473
  185.6 2.2 collective-permute-done.32.refs_4_
  188.8 11.0 %ff_bwd.2 = (bf16[512,768]{1,0:T(8,128)(2,1)}, f32[512,768]{1,0:T(8,128)}, bf16[512,768]{1,0:T(8,128)(2,1)}, bf16[512,1536]{1,0:T(8,128)(2,1)}, bf16[512,768]{1,...) custom-call(f32[512,768]{1,0:T(8,128)} %get-tuple-element.184.refs_0_.refs_3_, ...), custom_call_target="tpu_custom_call" | custom-call | flops 9900000256 | bytes 32400000 | tf_op jit(solution)/shard_map/ff_bwd/pallas_call | solution.py:580
  199.8 6.6 %ff_dw.2 = bf16[4,4,2,192,384]{4,3,2,1,0:T(8,128)(2,1)} custom-call(bf16[512,1536]{1,0:T(8,128)(2,1)} %get-tuple-element.190.refs_0_, bf16[512,1536]{1,0:T(8,128)(2,1)} %get-tuple-element.191.refs_1_, bf16[512,768]{1,0:T(8,128)(2,1)} %get-tuple-element.192.refs_2_, bf16[512,768]{1,0:T(8,128)(2,1)} %get-tuple-element.193.refs_3_), custom_call_target="tpu_custom_call" | custom-call | flops 5500000256 | bytes 18000000 | tf_op jit(solution)/shard_map/ff_dw/pallas_call | solution.py:679
  207.7 2.2 collective-permute-done.33.refs_2_
  210.7 15.0 %attn_bwd.2 = (f32[512,768]{1,0:T(8,128)}, bf16[512,768]{1,0:T(8,128)(2,1)}, bf16[4,512,384]{2,1,0:T(8,128)(2,1)}, bf16[512,768]{1,0:T(8,128)(2,1)}, f32[8,768]{1,0:T(8,128)}) custom-call(f32[512,768]{1,0:T(8,128)} %get-tuple-element.194.refs_0_, bf16[512,768]{1,0:T(8,128)(2,1)} %get-tuple-element.195.refs_1_, bf16[512,768]{1,0:T(8,128)(2,1)} %copy-done.66, ...), custom_call_target="tpu_custom_call" | custom-call | flops 13200000000 | bytes 43200000 | tf_op jit(solution)/shard_map/attn_bwd/pallas_call | solution.py:800
  225.8 5.5 %attn_dw.2 = (bf16[2,4,2,96,384]{4,3,2,1,0:T(8,128)(2,1)}, bf16[2,4,2,96,384]{4,3,2,1,0:T(8,128)(2,1)}) custom-call(bf16[4,512,384]{2,1,0:T(8,128)(2,1)} %get-tuple-element.202.refs_0_, bf16[512,768]{1,0:T(8,128)(2,1)} %get-tuple-element.203.refs_1_, bf16[512,768]{1,0:T(8,128)(2,1)} %get-tuple-element.204.refs_2_), custom_call_target="tpu_custom_call" | custom-call | flops 3849999872 | bytes 12600000 | tf_op jit(solution)/shard_map/attn_dw/pallas_call | solution.py:842
  232.0 3.4 collective-permute-done.34.refs_1_
  241.6 10.7 %ff_bwd.3 = (f32[512,768]{1,0:T(8,128)}, bf16[512,768]{1,0:T(8,128)(2,1)}, bf16[512,1536]{1,0:T(8,128)(2,1)}, bf16[512,768]{1,0:T(8,128)(2,1)}, f32[8,768]{1,0:T(8,128)}, /*index=5*/f32[1,1536]{1,0:T(1,128)}) custom-call(f32[512,768]{1,0:T(8,128)} %get-tuple-element.208.refs_0_, bf16[512,768]{1,0:T(8,128)(2,1)} %get-tuple-element.209.refs_1_, ...), custom_call_target="tpu_custom_call" | custom-call | flops 9900000256 | bytes 32400000 | tf_op jit(solution)/shard_map/ff_bwd/pallas_call | solution.py:580
  252.3 2.7 collective-permute-done.37.refs_3_.refs_4_
  258.0 6.9 %ff_dw.3 = (bf16[2,4,192,384]{3,2,1,0:T(8,128)(2,1)}, bf16[4,192,384]{2,1,0:T(8,128)(2,1)}, bf16[4,192,384]{2,1,0:T(8,128)(2,1)}, bf16[2,4,192,384]{3,2,1,0:T(8,...) custom-call(bf16[512,1536]{1,0:T(8,128)(2,1)} %get-tuple-element.188.refs_0_, ...), custom_call_target="tpu_custom_call" | custom-call | flops 5500000256 | bytes 18000000 | tf_op jit(solution)/shard_map/ff_dw/pallas_call | solution.py:679
  268.1 13.8 %attn_bwd.3 = (f32[512,768]{1,0:T(8,128)}, bf16[512,768]{1,0:T(8,128)(2,1)}, bf16[4,512,384]{2,1,0:T(8,128)(2,1)}, bf16[512,768]{1,0:T(8,128)(2,1)}, f32[8,768]{1,0:T(8,128)}) custom-call(f32[512,768]{1,0:T(8,128)} %get-tuple-element.226.refs_0_, bf16[512,768]{1,0:T(8,128)(2,1)} %get-tuple-element.227.refs_1_, bf16[512,768]{1,0:T(8,128)(2,1)} %copy-done.60, ...), custom_call_target="tpu_custom_call" | custom-call | flops 13200000000 | bytes 43200000 | tf_op jit(solution)/shard_map/attn_bwd/pallas_call | solution.py:800
  282.0 5.6 %attn_dw.3 = (bf16[2,4,2,96,384]{4,3,2,1,0:T(8,128)(2,1)}, bf16[2,4,2,96,384]{4,3,2,1,0:T(8,128)(2,1)}) custom-call(bf16[4,512,384]{2,1,0:T(8,128)(2,1)} %get-tuple-element.232.refs_0_, bf16[512,768]{1,0:T(8,128)(2,1)} %get-tuple-element.174.state_in.refs_1_, bf16[512,768]{1,0:T(8,128)(2,1)} %get-tuple-element.233.refs_2_), custom_call_target="tpu_custom_call" | custom-call | flops 3849999872 | bytes 12600000 | tf_op jit(solution)/shard_map/attn_dw/pallas_call | solution.py:842
  288.1 3.8 collective-permute-done.41
  291.9 3.4 add_add_fusion
  298.1 1.7 arrange.3
  310.5 4.4 %collective-permute-start.47 = (f32[24,768]{1,0:T(8,128)S(1)}, f32[24,768]{1,0:T(8,128)S(1)}, u32[]{:S(2)}, u32[]{:S(2)}) collective-permute-start(f32[24,768]{1,0:T(8,128)S(1)} %pack_small.1), channel_id=1, source_target_pairs={{0,4},{4,0},{8,12},{12,8},{16,20},{20,16},{24,28},{28,24},{1,5},{5... | collective-permute-start | bytes 221192 | tf_op jit(solution)/shard_map/flat_dp1/ppermute | solution.py:1109
  316.6 2.7 collective-permute-done.49.refs_3_.refs_10_
  325.9 13.0 %collective-permute-done.50 = f32[24,768]{1,0:T(8,128)S(1)} collective-permute-done((f32[24,768]{1,0:T(8,128)S(1)}, f32[24,768]{1,0:T(8,128)S(1)}, u32[]{:S(2)}, u32[]{:S(2)}) %collective-permute-start.50) | collective-permute-done | bytes 73760 | tf_op jit(solution)/shard_map/flat_dp2/ppermute | solution.py:1109
  339.5 3.4 add_third.3
  347.5 9.3 %collective-permute-done.55 = f32[24,768]{1,0:T(8,128)S(1)} collective-permute-done((f32[24,768]{1,0:T(8,128)S(1)}, f32[24,768]{1,0:T(8,128)S(1)}, u32[]{:S(2)}, u32[]{:S(2)}) %collective-permute-start.55) | collective-permute-done | bytes 73760 | tf_op jit(solution)/shard_map/flat_dp4/ppermute | solution.py:1109
  360.3 7.5 %collective-permute-done.58 = f32[24,768]{1,0:T(8,128)S(1)} collective-permute-done((f32[24,768]{1,0:T(8,128)S(1)}, f32[24,768]{1,0:T(8,128)S(1)}, u32[]{:S(2)}, u32[]{:S(2)}) %collective-permute-start.58) | collective-permute-done | bytes 73760 | tf_op jit(solution)/shard_map/flat_tensor1/ppermute | solution.py:1109
  371.0 1.8 collective-permute-start.62
  373.6 10.5 %collective-permute-done.63.refs_3_ = bf16[2,288,384]{2,1,0:T(8,128)(2,1)S(1)} collective-permute-done((bf16[2,288,384]{2,1,0:T(8,128)(2,1)S(1)}, bf16[2,288,384]{2,1,0:T(8,128)(2,1)S(1)}, u32[]{:S(2)}, u32[]{:S(2)}) %collective-permute-start.63) | collective-permute-done | bytes 442400 | tf_op jit(solution)/shard_map/l1_c6/ppermute | solution.py:1109
  385.3 6.4 %collective-permute-done.62.refs_2_ = bf16[2,288,384]{2,1,0:T(8,128)(2,1)S(1)} collective-permute-done((bf16[2,288,384]{2,1,0:T(8,128)(2,1)S(1)}, bf16[2,288,384]{2,1,0:T(8,128)(2,1)S(1)}, u32[]{:S(2)}, u32[]{:S(2)}) %collective-permute-start.62) | collective-permute-done | bytes 442400 | tf_op jit(solution)/shard_map/l1_c4/ppermute | solution.py:1109
  393.5 1.6 collective-permute-start.64
  395.6 10.1 %collective-permute-done.66.refs_3_ = bf16[2,288,384]{2,1,0:T(8,128)(2,1)S(1)} collective-permute-done((bf16[2,288,384]{2,1,0:T(8,128)(2,1)}, bf16[2,288,384]{2,1,0:T(8,128)(2,1)S(1)}, u32[]{:S(2)}, u32[]{:S(2)}) %collective-permute-start.66) | collective-permute-done | bytes 442400 | tf_op jit(solution)/shard_map/l0_c6/ppermute | solution.py:1109
  405.8 9.0 %collective-permute-done.65.refs_2_ = bf16[2,288,384]{2,1,0:T(8,128)(2,1)S(1)} collective-permute-done((bf16[2,288,384]{2,1,0:T(8,128)(2,1)}, bf16[2,288,384]{2,1,0:T(8,128)(2,1)S(1)}, u32[]{:S(2)}, u32[]{:S(2)}) %collective-permute-start.65) | collective-permute-done | bytes 442400 | tf_op jit(solution)/shard_map/l0_c4/ppermute | solution.py:1109
  416.1 3.3 gradients_out.2
  419.4 3.3 gradients_out.3
  (332 shorter events, 97.8 us)
Async XLA Ops:
  7.2 53.4 %all-gather.5.cloned.1.call-start = ((), (), s32[]{:S(2)}) async-start(), calls=%async_computation.6 | async-start | bytes 1536000 | tf_op jit(solution)/shard_map/ff0_z/all_gather | solution.py:1161
  12.6 103.0 %all-gather.7.cloned.1.call-start = ((), (), s32[]{:S(2)}) async-start(), calls=%async_computation.7 | async-start | bytes 1536000 | tf_op jit(solution)/shard_map/ff1_z/all_gather | solution.py:1161
  12.6 13.9 %collective-permute-start.1 = (bf16[208,768]{1,0:T(8,128)(2,1)}, bf16[208,768]{1,0:T(8,128)(2,1)S(1)}, u32[]{:S(2)}, u32[]{:S(2)}) collective-permute-start(bf16[208,768]{1,0:T(8,128)(2,1)} %get-tuple-element.157), channel_id=1, source_target_pairs={{4,7},{5,4},{6,5},{7,6},{12,15},{13,12},{14,13},{15,14},{20,23},{2... | collective-permute-start | bytes 958472 | tf_op jit(solution)/shard_map/attn0_z_a/ppermute | solution.py:1109
  13.3 17.2 %collective-permute-start.7 = (bf16[208,768]{1,0:T(8,128)(2,1)}, bf16[208,768]{1,0:T(8,128)(2,1)S(1)}, u32[]{:S(2)}, u32[]{:S(2)}) collective-permute-start(bf16[208,768]{1,0:T(8,128)(2,1)} %get-tuple-element.157), channel_id=1, source_target_pairs={{0,1},{1,2},{2,3},{3,0},{4,6},{5,7},{6,4},{7,5},{8,9},{9,10},{10,1... | collective-permute-start | bytes 958472 | tf_op jit(solution)/shard_map/attn0_z_b/ppermute | solution.py:1109
  22.4 11.9 %collective-permute-start.5 = (bf16[256,768]{1,0:T(8,128)(2,1)S(1)}, bf16[256,768]{1,0:T(8,128)(2,1)S(1)}, u32[]{:S(2)}, u32[]{:S(2)}) collective-permute-start(bf16[256,768]{1,0:T(8,128)(2,1)S(1)} %broadcast_select_fusion.3.refs_0_), channel_id=1, source_target_pairs={{0,4},{4,0},{8,12},{12,8},{16,20},{20,16},{24,28},{28,24},{1,5},{5... | collective-permute-start | bytes 1179656 | tf_op jit(solution)/shard_map/x_across/ppermute | solution.py:1109
  45.9 14.0 %collective-permute-start.11 = (bf16[192,768]{1,0:T(8,128)(2,1)S(1)}, bf16[192,768]{1,0:T(8,128)(2,1)}, u32[]{:S(2)}, u32[]{:S(2)}) collective-permute-start(bf16[192,768]{1,0:T(8,128)(2,1)S(1)} %copy-done.82), channel_id=1, source_target_pairs={{0,1},{1,2},{2,3},{3,0},{4,6},{5,7},{6,4},{7,5},{8,9},{9,10},{10,1... | collective-permute-start | bytes 884744 | tf_op jit(solution)/shard_map/attn1_z_b/ppermute | solution.py:1109
  59.9 283.1 %reduce-scatter.6.cloned.1.call-start = ((), (), s32[]{:S(2)}) async-start(), calls=%async_computation.4 | async-start | bytes 5898240 | tf_op jit(solution)/shard_map/sums_z/reduce_scatter | solution.py:1220
  62.9 30.3 %collective-permute-start.14 = (bf16[2,3,192,384]{3,2,1,0:T(8,128)(2,1)S(1)}, bf16[2,3,192,384]{3,2,1,0:T(8,128)(2,1)S(1)}, u32[]{:S(2)}, u32[]{:S(2)}) collective-permute-start(bf16[2,3,192,384]{3,2,1,0:T(8,128)(2,1)S(1)} %get-tuple-element.165.refs_0_.refs_11_), channel_id=1, source_target_pairs={{0,16},{4,20},{8,24},{12,28},{16,0},{20,4},{24,8},{28,12},{1,17},{... | collective-permute-start | bytes 2654216 | tf_op jit(solution)/shard_map/ff0_y/ppermute | solution.py:1109
  64.4 29.8 %collective-permute-start.13 = (bf16[2,3,192,384]{3,2,1,0:T(8,128)(2,1)S(1)}, bf16[2,3,192,384]{3,2,1,0:T(8,128)(2,1)S(1)}, u32[]{:S(2)}, u32[]{:S(2)}) collective-permute-start(bf16[2,3,192,384]{3,2,1,0:T(8,128)(2,1)S(1)} %get-tuple-element.165.refs_0_.refs_11_), channel_id=1, source_target_pairs={{0,8},{4,12},{8,0},{12,4},{16,24},{20,28},{24,16},{28,20},{1,9},{5... | collective-permute-start | bytes 2654216 | tf_op jit(solution)/shard_map/ff0_x/ppermute | solution.py:1109
  78.3 50.1 %collective-permute-start.23 = (bf16[512,768]{1,0:T(8,128)(2,1)}, bf16[512,768]{1,0:T(8,128)(2,1)S(1)}, u32[]{:S(2)}, u32[]{:S(2)}) collective-permute-start(bf16[512,768]{1,0:T(8,128)(2,1)} %get-tuple-element.175.a_mine), channel_id=1, source_target_pairs={{0,4},{4,0},{8,12},{12,8},{16,20},{20,16},{24,28},{28,24},{1,5},{5... | collective-permute-start | bytes 2359304 | tf_op jit(solution)/shard_map/a0/ppermute | solution.py:1109
  93.3 19.6 %collective-permute-start.16 = (bf16[3,192,384]{2,1,0:T(8,128)(2,1)S(1)}, bf16[3,192,384]{2,1,0:T(8,128)(2,1)S(1)}, u32[]{:S(2)}, u32[]{:S(2)}) collective-permute-start(bf16[3,192,384]{2,1,0:T(8,128)(2,1)S(1)} %slice_bitcast_fusion.2), channel_id=1, source_target_pairs={{0,8},{4,12},{8,0},{12,4},{16,24},{20,28},{24,16},{28,20},{1,9},{5... | collective-permute-start | bytes 1327112 | tf_op jit(solution)/shard_map/ff0_yx/ppermute | solution.py:1109
  94.3 20.1 %collective-permute-start.15 = (bf16[3,192,384]{2,1,0:T(8,128)(2,1)S(1)}, bf16[3,192,384]{2,1,0:T(8,128)(2,1)S(1)}, u32[]{:S(2)}, u32[]{:S(2)}) collective-permute-start(bf16[3,192,384]{2,1,0:T(8,128)(2,1)S(1)} %slice_bitcast_fusion.3), channel_id=1, source_target_pairs={{0,16},{4,20},{8,24},{12,28},{16,0},{20,4},{24,8},{28,12},{1,17},{... | collective-permute-start | bytes 1327112 | tf_op jit(solution)/shard_map/ff0_xy/ppermute | solution.py:1109
  97.0 15.0 %collective-permute-start.20 = (bf16[192,768]{1,0:T(8,128)(2,1)}, bf16[192,768]{1,0:T(8,128)(2,1)}, u32[]{:S(2)}, u32[]{:S(2)}) collective-permute-start(bf16[192,768]{1,0:T(8,128)(2,1)} %collective-permute-done.11.refs_16_), channel_id=1, source_target_pairs={{0,8},{4,12},{8,0},{12,4},{16,24},{20,28},{24,16},{28,20},{1,9},{5... | collective-permute-start | bytes 884744 | tf_op jit(solution)/shard_map/attn1_b_x/ppermute | solution.py:1109
  97.9 20.0 %collective-permute-start.17 = (bf16[192,768]{1,0:T(8,128)(2,1)}, bf16[192,768]{1,0:T(8,128)(2,1)}, u32[]{:S(2)}, u32[]{:S(2)}) collective-permute-start(bf16[192,768]{1,0:T(8,128)(2,1)} %collective-permute-done.12.refs_12_), channel_id=1, source_target_pairs={{4,12},{12,4},{20,28},{28,20},{5,13},{13,5},{21,29},{29,21},{6,14}... | collective-permute-start | bytes 884744 | tf_op jit(solution)/shard_map/attn1_a_x/ppermute | solution.py:1109
  114.4 13.9 %collective-permute-start.22 = (bf16[192,768]{1,0:T(8,128)(2,1)}, bf16[192,768]{1,0:T(8,128)(2,1)}, u32[]{:S(2)}, u32[]{:S(2)}) collective-permute-start(bf16[192,768]{1,0:T(8,128)(2,1)} %collective-permute-done.20.refs_17_), channel_id=1, source_target_pairs={{0,16},{4,20},{8,24},{12,28},{16,0},{20,4},{24,8},{28,12},{1,17},{... | collective-permute-start | bytes 884744 | tf_op jit(solution)/shard_map/attn1_b_xy/ppermute | solution.py:1109
  117.9 29.0 %collective-permute-start.25 = (bf16[2,3,192,384]{3,2,1,0:T(8,128)(2,1)S(1)}, bf16[2,3,192,384]{3,2,1,0:T(8,128)(2,1)S(1)}, u32[]{:S(2)}, u32[]{:S(2)}) collective-permute-start(bf16[2,3,192,384]{3,2,1,0:T(8,128)(2,1)S(1)} %get-tuple-element.173.refs_0_.refs_11_), channel_id=1, source_target_pairs={{0,16},{4,20},{8,24},{12,28},{16,0},{20,4},{24,8},{28,12},{1,17},{... | collective-permute-start | bytes 2654216 | tf_op jit(solution)/shard_map/ff1_y/ppermute | solution.py:1109
  122.0 24.8 %collective-permute-start.24 = (bf16[2,3,192,384]{3,2,1,0:T(8,128)(2,1)S(1)}, bf16[2,3,192,384]{3,2,1,0:T(8,128)(2,1)S(1)}, u32[]{:S(2)}, u32[]{:S(2)}) collective-permute-start(bf16[2,3,192,384]{3,2,1,0:T(8,128)(2,1)S(1)} %get-tuple-element.173.refs_0_.refs_11_), channel_id=1, source_target_pairs={{0,8},{4,12},{8,0},{12,4},{16,24},{20,28},{24,16},{28,20},{1,9},{5... | collective-permute-start | bytes 2654216 | tf_op jit(solution)/shard_map/ff1_x/ppermute | solution.py:1109
  160.8 13.5 %collective-permute-start.27 = (bf16[512,768]{1,0:T(8,128)(2,1)}, bf16[512,768]{1,0:T(8,128)(2,1)S(1)}, u32[]{:S(2)}, u32[]{:S(2)}) collective-permute-start(bf16[512,768]{1,0:T(8,128)(2,1)} %get-tuple-element.181.a_mine), channel_id=1, source_target_pairs={{0,4},{4,0},{8,12},{12,8},{16,20},{20,16},{24,28},{28,24},{1,5},{5... | collective-permute-start | bytes 2359304 | tf_op jit(solution)/shard_map/a1/ppermute | solution.py:1109
  161.0 12.6 %collective-permute-start.29 = (bf16[3,192,384]{2,1,0:T(8,128)(2,1)S(1)}, bf16[3,192,384]{2,1,0:T(8,128)(2,1)S(1)}, u32[]{:S(2)}, u32[]{:S(2)}) collective-permute-start(bf16[3,192,384]{2,1,0:T(8,128)(2,1)S(1)} %slice_bitcast_fusion), channel_id=1, source_target_pairs={{0,8},{4,12},{8,0},{12,4},{16,24},{20,28},{24,16},{28,20},{1,9},{5... | collective-permute-start | bytes 1327112 | tf_op jit(solution)/shard_map/ff1_yx/ppermute | solution.py:1109
  162.0 12.3 %collective-permute-start.28 = (bf16[3,192,384]{2,1,0:T(8,128)(2,1)S(1)}, bf16[3,192,384]{2,1,0:T(8,128)(2,1)S(1)}, u32[]{:S(2)}, u32[]{:S(2)}) collective-permute-start(bf16[3,192,384]{2,1,0:T(8,128)(2,1)S(1)} %slice_bitcast_fusion.1), channel_id=1, source_target_pairs={{0,16},{4,20},{8,24},{12,28},{16,0},{20,4},{24,8},{28,12},{1,17},{... | collective-permute-start | bytes 1327112 | tf_op jit(solution)/shard_map/ff1_xy/ppermute | solution.py:1109
  163.2 21.7 %collective-permute-start.31 = (bf16[256,768]{1,0:T(8,128)(2,1)S(1)}, bf16[256,768]{1,0:T(8,128)(2,1)S(1)}, u32[]{:S(2)}, u32[]{:S(2)}) collective-permute-start(bf16[256,768]{1,0:T(8,128)(2,1)S(1)} %copy-done.51), channel_id=1, source_target_pairs={{1,4},{3,6},{4,1},{6,3},{9,12},{11,14},{12,9},{14,11},{17,20},{19,... | collective-permute-start | bytes 1179656 | tf_op jit(solution)/shard_map/cot_swap/ppermute | solution.py:1109
  206.4 161.4 %reduce-scatter.8.cloned.1.call-start = ((), (), s32[]{:S(2)}) async-start(), calls=%async_computation.5 | async-start | bytes 737280 | tf_op jit(solution)/shard_map/sums_z/reduce_scatter | solution.py:1220
  238.9 16.2 %collective-permute-start.36 = (bf16[2,4,96,384]{3,2,1,0:T(8,128)(2,1)S(1)}, bf16[2,4,96,384]{3,2,1,0:T(8,128)(2,1)S(1)}, u32[]{:S(2)}, u32[]{:S(2)}) collective-permute-start(bf16[2,4,96,384]{3,2,1,0:T(8,128)(2,1)S(1)} %get-tuple-element.207), channel_id=1, source_target_pairs={{0,16},{4,20},{8,24},{12,28},{16,0},{20,4},{24,8},{28,12},{1,17},{... | collective-permute-start | bytes 1769480 | tf_op jit(solution)/shard_map/ga1_1a/ppermute | solution.py:1109
  239.9 15.1 %collective-permute-start.37 = (bf16[2,4,96,384]{3,2,1,0:T(8,128)(2,1)S(1)}, bf16[2,4,96,384]{3,2,1,0:T(8,128)(2,1)S(1)}, u32[]{:S(2)}, u32[]{:S(2)}) collective-permute-start(bf16[2,4,96,384]{3,2,1,0:T(8,128)(2,1)S(1)} %get-tuple-element.218), channel_id=1, source_target_pairs={{0,8},{4,12},{8,0},{12,4},{16,24},{20,28},{24,16},{28,20},{1,9},{5... | collective-permute-start | bytes 1769480 | tf_op jit(solution)/shard_map/ga1_1b/ppermute | solution.py:1109
  252.3 15.0 %collective-permute-start.40 = (bf16[512,768]{1,0:T(8,128)(2,1)}, bf16[512,768]{1,0:T(8,128)(2,1)S(1)}, u32[]{:S(2)}, u32[]{:S(2)}) collective-permute-start(bf16[512,768]{1,0:T(8,128)(2,1)} %get-tuple-element.227.refs_1_), channel_id=1, source_target_pairs={{0,4},{4,0},{8,12},{12,8},{16,20},{20,16},{24,28},{28,24},{1,5},{5... | collective-permute-start | bytes 2359304 | tf_op jit(solution)/shard_map/dh0/ppermute | solution.py:1109
  265.0 30.3 %collective-permute-start.42 = (bf16[2,4,192,384]{3,2,1,0:T(8,128)(2,1)}, bf16[2,4,192,384]{3,2,1,0:T(8,128)(2,1)S(1)}, u32[]{:S(2)}, u32[]{:S(2)}) collective-permute-start(bf16[2,4,192,384]{3,2,1,0:T(8,128)(2,1)} %get-tuple-element.238), channel_id=1, source_target_pairs={{0,16},{4,20},{8,24},{12,28},{16,0},{20,4},{24,8},{28,12},{1,17},{... | collective-permute-start | bytes 3538952 | tf_op jit(solution)/shard_map/gf0_1a/ppermute | solution.py:1109
  265.8 29.5 %collective-permute-start.43 = (bf16[2,4,192,384]{3,2,1,0:T(8,128)(2,1)}, bf16[2,4,192,384]{3,2,1,0:T(8,128)(2,1)S(1)}, u32[]{:S(2)}, u32[]{:S(2)}) collective-permute-start(bf16[2,4,192,384]{3,2,1,0:T(8,128)(2,1)} %get-tuple-element.241), channel_id=1, source_target_pairs={{0,8},{4,12},{8,0},{12,4},{16,24},{20,28},{24,16},{28,20},{1,9},{5... | collective-permute-start | bytes 3538952 | tf_op jit(solution)/shard_map/gf0_1b/ppermute | solution.py:1109
  302.7 17.5 %collective-permute-start.48 = (bf16[2,4,96,384]{3,2,1,0:T(8,128)(2,1)}, bf16[2,4,96,384]{3,2,1,0:T(8,128)(2,1)S(1)}, u32[]{:S(2)}, u32[]{:S(2)}) collective-permute-start(bf16[2,4,96,384]{3,2,1,0:T(8,128)(2,1)} %get-tuple-element.255), channel_id=1, source_target_pairs={{0,16},{4,20},{8,24},{12,28},{16,0},{20,4},{24,8},{28,12},{1,17},{... | collective-permute-start | bytes 1769480 | tf_op jit(solution)/shard_map/ga0_1a/ppermute | solution.py:1109
  303.8 15.5 %collective-permute-start.49 = (bf16[2,4,96,384]{3,2,1,0:T(8,128)(2,1)}, bf16[2,4,96,384]{3,2,1,0:T(8,128)(2,1)S(1)}, u32[]{:S(2)}, u32[]{:S(2)}) collective-permute-start(bf16[2,4,96,384]{3,2,1,0:T(8,128)(2,1)} %get-tuple-element.262), channel_id=1, source_target_pairs={{0,8},{4,12},{8,0},{12,4},{16,24},{20,28},{24,16},{28,20},{1,9},{5... | collective-permute-start | bytes 1769480 | tf_op jit(solution)/shard_map/ga0_1b/ppermute | solution.py:1109
  306.1 79.1 %reduce-scatter.4.cloned.1.call-start = ((), (), s32[]{:S(2)}) async-start(), calls=%async_computation.3 | async-start | bytes 2211840 | tf_op jit(solution)/shard_map/sums_z/reduce_scatter | solution.py:1220
  307.6 15.9 %collective-permute-start.45 = (f32[256,768]{1,0:T(8,128)S(1)}, f32[256,768]{1,0:T(8,128)S(1)}, u32[]{:S(2)}, u32[]{:S(2)}) collective-permute-start(f32[256,768]{1,0:T(8,128)S(1)} %constant_dynamic-slice_fusion), channel_id=1, source_target_pairs={{1,4},{3,6},{4,1},{6,3},{9,12},{11,14},{12,9},{14,11},{17,20},{19,... | collective-permute-start | bytes 2359304 | tf_op jit(solution)/shard_map/grad_swap/ppermute | solution.py:1109
  309.3 11.9 %collective-permute-start.44 = (bf16[256,768]{1,0:T(8,128)(2,1)S(1)}, bf16[256,768]{1,0:T(8,128)(2,1)S(1)}, u32[]{:S(2)}, u32[]{:S(2)}) collective-permute-start(bf16[256,768]{1,0:T(8,128)(2,1)S(1)} %constant_dynamic-slice_fusion.1), channel_id=1, source_target_pairs={{1,4},{3,6},{4,1},{6,3},{9,12},{11,14},{12,9},{14,11},{17,20},{19,... | collective-permute-start | bytes 1179656 | tf_op jit(solution)/shard_map/mixed_swap/ppermute | solution.py:1109
  315.8 23.6 %collective-permute-start.51 = (bf16[4,192,384]{2,1,0:T(8,128)(2,1)S(1)}, bf16[4,192,384]{2,1,0:T(8,128)(2,1)S(1)}, u32[]{:S(2)}, u32[]{:S(2)}) collective-permute-start(bf16[4,192,384]{2,1,0:T(8,128)(2,1)S(1)} %copy-done.43), channel_id=1, source_target_pairs={{0,8},{4,12},{8,0},{12,4},{16,24},{20,28},{24,16},{28,20},{1,9},{5... | collective-permute-start | bytes 1769480 | tf_op jit(solution)/shard_map/gf0_2a/ppermute | solution.py:1109
  319.3 20.2 %collective-permute-start.52 = (bf16[4,192,384]{2,1,0:T(8,128)(2,1)S(1)}, bf16[4,192,384]{2,1,0:T(8,128)(2,1)S(1)}, u32[]{:S(2)}, u32[]{:S(2)}) collective-permute-start(bf16[4,192,384]{2,1,0:T(8,128)(2,1)S(1)} %copy-done.41), channel_id=1, source_target_pairs={{0,16},{4,20},{8,24},{12,28},{16,0},{20,4},{24,8},{28,12},{1,17},{... | collective-permute-start | bytes 1769480 | tf_op jit(solution)/shard_map/gf0_2b/ppermute | solution.py:1109
  320.8 18.7 %collective-permute-start.53 = (bf16[4,96,384]{2,1,0:T(8,128)(2,1)S(1)}, bf16[4,96,384]{2,1,0:T(8,128)(2,1)S(1)}, u32[]{:S(2)}, u32[]{:S(2)}) collective-permute-start(bf16[4,96,384]{2,1,0:T(8,128)(2,1)S(1)} %get-tuple-element.263), channel_id=1, source_target_pairs={{0,8},{4,12},{8,0},{12,4},{16,24},{20,28},{24,16},{28,20},{1,9},{5... | collective-permute-start | bytes 884744 | tf_op jit(solution)/shard_map/ga0_2a/ppermute | solution.py:1109
  321.3 18.2 %collective-permute-start.54 = (bf16[4,96,384]{2,1,0:T(8,128)(2,1)S(1)}, bf16[4,96,384]{2,1,0:T(8,128)(2,1)S(1)}, u32[]{:S(2)}, u32[]{:S(2)}) collective-permute-start(bf16[4,96,384]{2,1,0:T(8,128)(2,1)S(1)} %get-tuple-element.264), channel_id=1, source_target_pairs={{0,16},{4,20},{8,24},{12,28},{16,0},{20,4},{24,8},{28,12},{1,17},{... | collective-permute-start | bytes 884744 | tf_op jit(solution)/shard_map/ga0_2b/ppermute | solution.py:1109
  323.5 15.3 %collective-permute-start.50 = (f32[24,768]{1,0:T(8,128)S(1)}, f32[24,768]{1,0:T(8,128)S(1)}, u32[]{:S(2)}, u32[]{:S(2)}) collective-permute-start(f32[24,768]{1,0:T(8,128)S(1)} %add.34), channel_id=1, source_target_pairs={{0,8},{4,12},{8,0},{12,4},{16,24},{20,28},{24,16},{28,20},{1,9},{5... | collective-permute-start | bytes 221192 | tf_op jit(solution)/shard_map/flat_dp2/ppermute | solution.py:1109
  344.7 12.2 %collective-permute-start.57 = (bf16[2,1,192,384]{3,2,1,0:T(8,128)(2,1)S(1)}, bf16[2,1,192,384]{3,2,1,0:T(8,128)(2,1)S(1)}, u32[]{:S(2)}, u32[]{:S(2)}) collective-permute-start(bf16[2,1,192,384]{3,2,1,0:T(8,128)(2,1)S(1)} %get-tuple-element.277), channel_id=1, source_target_pairs={{0,8},{4,12},{8,0},{12,4},{16,24},{20,28},{24,16},{28,20},{1,9},{5... | collective-permute-start | bytes 884744 | tf_op jit(solution)/shard_map/gf1_1b/ppermute | solution.py:1109
  370.0 14.0 %collective-permute-start.63 = (bf16[2,288,384]{2,1,0:T(8,128)(2,1)S(1)}, bf16[2,288,384]{2,1,0:T(8,128)(2,1)S(1)}, u32[]{:S(2)}, u32[]{:S(2)}) collective-permute-start(bf16[2,288,384]{2,1,0:T(8,128)(2,1)S(1)} %merge.1.refs_0_), channel_id=1, source_target_pairs={{0,24},{4,28},{8,16},{12,20},{16,8},{20,12},{24,0},{28,4},{1,25},{... | collective-permute-start | bytes 1327112 | tf_op jit(solution)/shard_map/l1_c6/ppermute | solution.py:1109
  371.0 20.6 %collective-permute-start.62 = (bf16[2,288,384]{2,1,0:T(8,128)(2,1)S(1)}, bf16[2,288,384]{2,1,0:T(8,128)(2,1)S(1)}, u32[]{:S(2)}, u32[]{:S(2)}) collective-permute-start(bf16[2,288,384]{2,1,0:T(8,128)(2,1)S(1)} %merge.1.refs_0_), channel_id=1, source_target_pairs={{0,16},{4,20},{8,24},{12,28},{16,0},{20,4},{24,8},{28,12},{1,17},{... | collective-permute-start | bytes 1327112 | tf_op jit(solution)/shard_map/l1_c4/ppermute | solution.py:1109
  372.8 18.8 %collective-permute-start.61 = (bf16[2,288,384]{2,1,0:T(8,128)(2,1)S(1)}, bf16[2,288,384]{2,1,0:T(8,128)(2,1)S(1)}, u32[]{:S(2)}, u32[]{:S(2)}) collective-permute-start(bf16[2,288,384]{2,1,0:T(8,128)(2,1)S(1)} %merge.1.refs_0_), channel_id=1, source_target_pairs={{0,8},{4,12},{8,0},{12,4},{16,24},{20,28},{24,16},{28,20},{1,9},{5... | collective-permute-start | bytes 1327112 | tf_op jit(solution)/shard_map/l1_c2/ppermute | solution.py:1109
  373.6 19.9 %collective-permute-start.72 = (bf16[2,288,384]{2,1,0:T(8,128)(2,1)S(1)}, bf16[2,288,384]{2,1,0:T(8,128)(2,1)S(1)}, u32[]{:S(2)}, u32[]{:S(2)}) collective-permute-start(bf16[2,288,384]{2,1,0:T(8,128)(2,1)S(1)} %merge.1.refs_0_), channel_id=1, source_target_pairs={{0,4},{4,0},{8,12},{12,8},{16,20},{20,16},{24,28},{28,24},{1,5},{5... | collective-permute-start | bytes 1327112 | tf_op jit(solution)/shard_map/l1_cc0/ppermute | solution.py:1109
  391.6 14.1 %collective-permute-start.66 = (bf16[2,288,384]{2,1,0:T(8,128)(2,1)}, bf16[2,288,384]{2,1,0:T(8,128)(2,1)S(1)}, u32[]{:S(2)}, u32[]{:S(2)}) collective-permute-start(bf16[2,288,384]{2,1,0:T(8,128)(2,1)} %bitcast.18), channel_id=1, source_target_pairs={{0,24},{4,28},{8,16},{12,20},{16,8},{20,12},{24,0},{28,4},{1,25},{... | collective-permute-start | bytes 1327112 | tf_op jit(solution)/shard_map/l0_c6/ppermute | solution.py:1109
  392.8 22.0 %collective-permute-start.65 = (bf16[2,288,384]{2,1,0:T(8,128)(2,1)}, bf16[2,288,384]{2,1,0:T(8,128)(2,1)S(1)}, u32[]{:S(2)}, u32[]{:S(2)}) collective-permute-start(bf16[2,288,384]{2,1,0:T(8,128)(2,1)} %bitcast.19), channel_id=1, source_target_pairs={{0,16},{4,20},{8,24},{12,28},{16,0},{20,4},{24,8},{28,12},{1,17},{... | collective-permute-start | bytes 1327112 | tf_op jit(solution)/shard_map/l0_c4/ppermute | solution.py:1109
  393.5 21.3 %collective-permute-start.64 = (bf16[2,288,384]{2,1,0:T(8,128)(2,1)}, bf16[2,288,384]{2,1,0:T(8,128)(2,1)S(1)}, u32[]{:S(2)}, u32[]{:S(2)}) collective-permute-start(bf16[2,288,384]{2,1,0:T(8,128)(2,1)} %bitcast.20), channel_id=1, source_target_pairs={{0,8},{4,12},{8,0},{12,4},{16,24},{20,28},{24,16},{28,20},{1,9},{5... | collective-permute-start | bytes 1327112 | tf_op jit(solution)/shard_map/l0_c2/ppermute | solution.py:1109
  395.1 20.9 %collective-permute-start.73 = (bf16[2,288,384]{2,1,0:T(8,128)(2,1)S(1)}, bf16[2,288,384]{2,1,0:T(8,128)(2,1)S(1)}, u32[]{:S(2)}, u32[]{:S(2)}) collective-permute-start(bf16[2,288,384]{2,1,0:T(8,128)(2,1)S(1)} %collective-permute-done.61.refs_1_), channel_id=1, source_target_pairs={{0,4},{4,0},{8,12},{12,8},{16,20},{20,16},{24,28},{28,24},{1,5},{5... | collective-permute-start | bytes 1327112 | tf_op jit(solution)/shard_map/l1_cc1/ppermute | solution.py:1109
  395.1 24.2 %collective-permute-start.67 = (bf16[2,288,384]{2,1,0:T(8,128)(2,1)}, bf16[2,288,384]{2,1,0:T(8,128)(2,1)S(1)}, u32[]{:S(2)}, u32[]{:S(2)}) collective-permute-start(bf16[2,288,384]{2,1,0:T(8,128)(2,1)} %bitcast.21), channel_id=1, source_target_pairs={{0,4},{4,0},{8,12},{12,8},{16,20},{20,16},{24,28},{28,24},{1,5},{5... | collective-permute-start | bytes 1327112 | tf_op jit(solution)/shard_map/l0_cc0/ppermute | solution.py:1109
  405.7 13.6 %collective-permute-start.70 = (bf16[2,288,384]{2,1,0:T(8,128)(2,1)S(1)}, bf16[2,288,384]{2,1,0:T(8,128)(2,1)S(1)}, u32[]{:S(2)}, u32[]{:S(2)}) collective-permute-start(bf16[2,288,384]{2,1,0:T(8,128)(2,1)S(1)} %collective-permute-done.66.refs_3_), channel_id=1, source_target_pairs={{0,4},{4,0},{8,12},{12,8},{16,20},{20,16},{24,28},{28,24},{1,5},{5... | collective-permute-start | bytes 1327112 | tf_op jit(solution)/shard_map/l0_cc3/ppermute | solution.py:1109
  (116 other events, 983.8 us)
Sparse Core Ops, SparseCore 0:
  12.7 47.8 all-gather.4
  62.7 46.2 all-gather.6
  206.6 86.1 reduce-scatter.5
  306.3 24.7 reduce-scatter.7
  343.1 42.0 reduce-scatter.3
